TPU v7x, 256 devices: a whole 4x4x8 slice. The times are simulated.
256 devices in a mesh: row: 8 (over z), col: 32 (over y, x, core).
Axes of the slice: x: 4, y: 4, z: 8, core: 2. Of those that a mesh axis runs over, the one named last changes fastest.
Arguments:
- left_blocks: bfloat16 [8, 32, 32, 128, 128], P('row', 'col'), may hold values from -6 to 6
- left_cols: int32 [8, 32, 32], P(None, 'col'), may hold values from 0 to 63, as said below
- reach_blocks: bfloat16 [64, 32, 128, 128], P('row', 'col'), may hold values from -0.125 to 0.125
- reach_cols: int32 [64, 32], P('row'), may hold values from 0 to 63, all different within a row
Outputs:
- product: bfloat16 [8, 32, 32, 128, 128], P('row', 'col')
Inputs may be any that keep to these rules, and one draw needn't show every extreme that they name: `left_cols`: within each slab row the 32 block columns are distinct; at most 8 of them lie in one panel of 8 block columns (panel q holds columns q * 8 to (q + 1) * 8 - 1), and every row has exactly 8 in some panel. `reach_cols`: within each reached block row the 32 block columns are distinct.
All inputs are finite; a program needn't handle non-finite values.
Results may differ from a plain program's by a relative error of at most 0.017.
Values may be sent and summed in bfloat16 or wider, within the bound.
No kernel may reach another device: no remote copies, remote signals or barrier semaphores. Data moves between devices by JAX's collectives and lax.ppermute only.
A program may use at most 192 MiB of HBM per device.

v0:
```python
import jax
import jax.numpy as jnp
from jax import lax
from jax.sharding import PartitionSpec as P

CAP = 8


def passed_along(block, axis, distance):
    devices = range(lax.axis_size(axis))
    route = [((i - distance) % len(devices), i) for i in devices]
    return lax.ppermute(block, axis, route)


def pick_panel(cols_rows, panel, pan_rows):
    slots = cols_rows.shape[1]
    inside = cols_rows // pan_rows == panel
    order_key = jnp.where(inside, 0, slots) + jnp.arange(slots, dtype=jnp.int32)[None, :]
    picked = lax.top_k(-order_key, CAP)[1]
    return (picked, jnp.take_along_axis(inside, picked, axis=1))


def slab_terms(selected, contract_col, usable, targets, panel_blocks, panel_cols, row_base):
    pan_rows = panel_cols.shape[0]
    slots = targets.shape[0]
    local_row = jnp.clip(contract_col - row_base, 0, pan_rows - 1)
    reach_row = panel_cols[local_row]
    matches = reach_row[:, None, :] == targets[None, :, None]
    present = jnp.any(matches, axis=2) & usable[:, None]
    slot_pick = jnp.sum(
        jnp.where(matches, jnp.arange(slots, dtype=jnp.int32)[None, None, :], 0), axis=2
    )
    chosen = panel_blocks[local_row[:, None], slot_pick]
    chosen = jnp.where(present[:, :, None, None], chosen, jnp.zeros((), chosen.dtype))
    return jnp.einsum("cxy,csyz->sxz", selected, chosen, preferred_element_type=jnp.float32)


def panel_rows_terms(blocks_sel, cols_rows, picked, usable, panel_blocks, panel_cols, row_base):
    contract_col = jnp.take_along_axis(cols_rows, picked, axis=1)

    def single(bundle):
        return slab_terms(
            bundle[0], bundle[1], bundle[2], bundle[3], panel_blocks, panel_cols, row_base
        )

    return lax.map(single, (blocks_sel, contract_col, usable, cols_rows))


def local(left_blocks, left_cols, reach_blocks, reach_cols):
    panels = lax.axis_size("row")
    my_panel = lax.axis_index("row")
    pan_rows = reach_blocks.shape[0]
    row_base = my_panel * pan_rows
    panel_blocks = lax.all_gather(reach_blocks, "col", axis=1, tiled=True)
    own_rows = left_blocks[0]
    portions = []
    current = own_rows
    for step_no in range(panels):
        source = (my_panel - step_no) % panels
        cols_src = lax.dynamic_index_in_dim(left_cols, source, 0, keepdims=False)
        picked, usable = pick_panel(cols_src, my_panel, pan_rows)
        selected = jnp.take_along_axis(current, picked[:, :, None, None], axis=1)
        portion = panel_rows_terms(
            selected, cols_src, picked, usable, panel_blocks, reach_cols, row_base
        )
        portions.append(portion.astype(jnp.bfloat16))
        if step_no + 1 < panels:
            current = passed_along(current, "row", 1)
    stacked = jnp.stack(portions, axis=0)
    order_idx = (my_panel - jnp.arange(panels, dtype=jnp.int32)) % panels
    partial_value = jnp.take(stacked, order_idx, axis=0)
    summed = lax.psum_scatter(
        partial_value.astype(jnp.float32).astype(jnp.bfloat16),
        "row",
        scatter_dimension=0,
        tiled=True,
    )
    return summed


def solution(mesh):
    in_specs = (
        P("row", "col", None, None, None),
        P(None, "col", None),
        P("row", "col", None, None),
        P("row", None),
    )
    out_specs = P("row", "col", None, None, None)
    return jax.shard_map(local, mesh=mesh, in_specs=in_specs, out_specs=out_specs, check_vma=False)
```

profile of v0, /device:TPU:1, one launch (start us, length us, event | category | flops | bytes accessed | tf_op | source)
XLA Modules:
  0.0 562.2 jit_solution(9242621731706960163)
XLA Ops:
  7.3 2.5 collective-permute-start
  11.0 0.8 top_k.69
  13.7 0.8 top_k.76
  17.9 0.8 top_k.79
  21.2 0.8 top_k.82
  24.8 0.8 top_k.89
  28.1 0.8 top_k.92
  41.7 1.7 collective-permute-start.1
  43.7 25.2 %collective-permute-done.1 = bf16[1,32,128,128]{3,2,1,0:T(8,128)(2,1)S(1)} collective-permute-done((bf16[1,32,128,128]{3,2,1,0:T(8,128)(2,1)S(1)}, bf16[1,32,128,128]{3,2,1,0:T(8,128)(2,1)S(1)}, u32[]{:S(2)}, u32[]{:S(2)}) %collective-permute-start.1) | collective-permute-done | bytes 1048608 | tf_op jit(solution)/shard_map/ppermute | solution.py:12
  69.5 24.1 %collective-permute-done.2 = bf16[1,32,128,128]{3,2,1,0:T(8,128)(2,1)S(1)} collective-permute-done((bf16[1,32,128,128]{3,2,1,0:T(8,128)(2,1)S(1)}, bf16[1,32,128,128]{3,2,1,0:T(8,128)(2,1)S(1)}, u32[]{:S(2)}, u32[]{:S(2)}) %collective-permute-start.2) | collective-permute-done | bytes 1048608 | tf_op jit(solution)/shard_map/ppermute | solution.py:12
  94.2 23.2 %collective-permute-done.3 = bf16[1,32,128,128]{3,2,1,0:T(8,128)(2,1)S(1)} collective-permute-done((bf16[1,32,128,128]{3,2,1,0:T(8,128)(2,1)S(1)}, bf16[1,32,128,128]{3,2,1,0:T(8,128)(2,1)S(1)}, u32[]{:S(2)}, u32[]{:S(2)}) %collective-permute-start.3) | collective-permute-done | bytes 1048608 | tf_op jit(solution)/shard_map/ppermute | solution.py:12
  118.0 22.3 %collective-permute-done.4 = bf16[1,32,128,128]{3,2,1,0:T(8,128)(2,1)S(1)} collective-permute-done((bf16[1,32,128,128]{3,2,1,0:T(8,128)(2,1)S(1)}, bf16[1,32,128,128]{3,2,1,0:T(8,128)(2,1)S(1)}, u32[]{:S(2)}, u32[]{:S(2)}) %collective-permute-start.4) | collective-permute-done | bytes 1048608 | tf_op jit(solution)/shard_map/ppermute | solution.py:12
  140.9 21.5 %collective-permute-done.5 = bf16[1,32,128,128]{3,2,1,0:T(8,128)(2,1)} collective-permute-done((bf16[1,32,128,128]{3,2,1,0:T(8,128)(2,1)S(1)}, bf16[1,32,128,128]{3,2,1,0:T(8,128)(2,1)}, u32[]{:S(2)}, u32[]{:S(2)}) %collective-permute-start.5) | collective-permute-done | bytes 1048608 | tf_op jit(solution)/shard_map/ppermute | solution.py:12
  164.1 1.8 gather_fusion.19
  167.2 1.8 gather_fusion.28
  169.0 1.8 gather_fusion.31
  170.8 1.8 gather_fusion.34
  172.7 1.8 gather_fusion.37
  174.5 9.5 %collective-permute-done.6 = bf16[1,32,128,128]{3,2,1,0:T(8,128)(2,1)} collective-permute-done((bf16[1,32,128,128]{3,2,1,0:T(8,128)(2,1)}, bf16[1,32,128,128]{3,2,1,0:T(8,128)(2,1)}, u32[]{:S(2)}, u32[]{:S(2)}) %collective-permute-start.6) | collective-permute-done | bytes 1048608 | tf_op jit(solution)/shard_map/ppermute | solution.py:12
  184.0 1.8 gather_fusion.40
  185.9 13.5 %gather_fusion.1 = bf16[256,128,128]{2,1,0:T(8,128)(2,1)} fusion(bf16[8,32,128,128]{3,2,1,0:T(8,128)(2,1)} %all-gather.2.cloned.1.call-done, s32[256]{0:T(256)S(1)} %reshape.2159), kind=kCustom, calls=%fused_computation.25 | custom fusion | bytes 16779264 | tf_op jit(solution)/shard_map/while/body/eval_jaxpr/gather | solution.py:33
  199.3 11.9 %copy.135 = bf16[8,32,128,128]{2,3,0,1:T(8,128)(2,1)} copy(bf16[8,32,128,128]{3,2,1,0:T(8,128)(2,1)} %bitcast.408) | data formatting | bytes 16777216 | tf_op jit(solution)/shard_map/while/body/eval_jaxpr/gather | solution.py:33
  211.3 12.7 %gather_fusion.3 = bf16[256,128,128]{2,1,0:T(8,128)(2,1)} fusion(bf16[8,32,128,128]{3,2,1,0:T(8,128)(2,1)} %all-gather.2.cloned.1.call-done, s32[256]{0:T(256)S(1)} %reshape.2173), kind=kCustom, calls=%fused_computation.27 | custom fusion | bytes 16779264 | tf_op jit(solution)/shard_map/while/body/eval_jaxpr/gather | solution.py:33
  224.0 12.0 %copy.143 = bf16[8,32,128,128]{2,3,0,1:T(8,128)(2,1)} copy(bf16[8,32,128,128]{3,2,1,0:T(8,128)(2,1)} %bitcast.409) | data formatting | bytes 16777216 | tf_op jit(solution)/shard_map/while/body/eval_jaxpr/gather | solution.py:33
  235.9 13.4 %gather_fusion.5 = bf16[256,128,128]{2,1,0:T(8,128)(2,1)} fusion(bf16[8,32,128,128]{3,2,1,0:T(8,128)(2,1)} %all-gather.2.cloned.1.call-done, s32[256]{0:T(256)S(1)} %reshape.2187), kind=kCustom, calls=%fused_computation.29 | custom fusion | bytes 16779264 | tf_op jit(solution)/shard_map/while/body/eval_jaxpr/gather | solution.py:33
  249.4 11.9 %copy.151 = bf16[8,32,128,128]{2,3,0,1:T(8,128)(2,1)} copy(bf16[8,32,128,128]{3,2,1,0:T(8,128)(2,1)} %bitcast.410) | data formatting | bytes 16777216 | tf_op jit(solution)/shard_map/while/body/eval_jaxpr/gather | solution.py:33
  261.3 24.7 %gather_fusion.7 = bf16[256,128,128]{2,1,0:T(8,128)(2,1)} fusion(bf16[8,32,128,128]{3,2,1,0:T(8,128)(2,1)} %all-gather.2.cloned.1.call-done, s32[256]{0:T(256)S(1)} %reshape.2201), kind=kCustom, calls=%fused_computation.31 | custom fusion | bytes 16779264 | tf_op jit(solution)/shard_map/while/body/eval_jaxpr/gather | solution.py:33
  286.0 12.0 %copy.159 = bf16[8,32,128,128]{2,3,0,1:T(8,128)(2,1)} copy(bf16[8,32,128,128]{3,2,1,0:T(8,128)(2,1)} %bitcast.411) | data formatting | bytes 16777216 | tf_op jit(solution)/shard_map/while/body/eval_jaxpr/gather | solution.py:33
  298.0 13.4 %gather_fusion.9 = bf16[256,128,128]{2,1,0:T(8,128)(2,1)} fusion(bf16[8,32,128,128]{3,2,1,0:T(8,128)(2,1)} %all-gather.2.cloned.1.call-done, s32[256]{0:T(256)S(1)} %reshape.2215), kind=kCustom, calls=%fused_computation.33 | custom fusion | bytes 16779264 | tf_op jit(solution)/shard_map/while/body/eval_jaxpr/gather | solution.py:33
  311.4 12.0 %copy.167 = bf16[8,32,128,128]{2,3,0,1:T(8,128)(2,1)} copy(bf16[8,32,128,128]{3,2,1,0:T(8,128)(2,1)} %bitcast.412) | data formatting | bytes 16777216 | tf_op jit(solution)/shard_map/while/body/eval_jaxpr/gather | solution.py:33
  323.4 13.0 %gather_fusion.11 = bf16[256,128,128]{2,1,0:T(8,128)(2,1)} fusion(bf16[8,32,128,128]{3,2,1,0:T(8,128)(2,1)} %all-gather.2.cloned.1.call-done, s32[256]{0:T(256)S(1)} %reshape.2229), kind=kCustom, calls=%fused_computation.35 | custom fusion | bytes 16779264 | tf_op jit(solution)/shard_map/while/body/eval_jaxpr/gather | solution.py:33
  336.4 12.0 %copy.175 = bf16[8,32,128,128]{2,3,0,1:T(8,128)(2,1)} copy(bf16[8,32,128,128]{3,2,1,0:T(8,128)(2,1)} %bitcast.413) | data formatting | bytes 16777216 | tf_op jit(solution)/shard_map/while/body/eval_jaxpr/gather | solution.py:33
  348.4 13.4 %gather_fusion.13 = bf16[256,128,128]{2,1,0:T(8,128)(2,1)} fusion(bf16[8,32,128,128]{3,2,1,0:T(8,128)(2,1)} %all-gather.2.cloned.1.call-done, s32[256]{0:T(256)S(1)} %reshape.2243), kind=kCustom, calls=%fused_computation.37 | custom fusion | bytes 16779264 | tf_op jit(solution)/shard_map/while/body/eval_jaxpr/gather | solution.py:33
  361.8 12.0 %copy.183 = bf16[8,32,128,128]{2,3,0,1:T(8,128)(2,1)} copy(bf16[8,32,128,128]{3,2,1,0:T(8,128)(2,1)} %bitcast.414) | data formatting | bytes 16777216 | tf_op jit(solution)/shard_map/while/body/eval_jaxpr/gather | solution.py:33
  373.8 13.4 %gather_fusion.15 = bf16[256,128,128]{2,1,0:T(8,128)(2,1)} fusion(bf16[8,32,128,128]{3,2,1,0:T(8,128)(2,1)} %all-gather.2.cloned.1.call-done, s32[256]{0:T(256)S(1)} %reshape.2257), kind=kCustom, calls=%fused_computation.39 | custom fusion | bytes 16779264 | tf_op jit(solution)/shard_map/while/body/eval_jaxpr/gather | solution.py:33
  387.2 12.2 %copy.191 = bf16[8,32,128,128]{2,3,0,1:T(8,128)(2,1)} copy(bf16[8,32,128,128]{3,2,1,0:T(8,128)(2,1)} %bitcast.407) | data formatting | bytes 16777216 | tf_op jit(solution)/shard_map/while/body/eval_jaxpr/gather | solution.py:33
  399.4 6.8 %fusion.51 = bf16[8,1,32,128,128]{3,4,2,1,0:T(8,128)(2,1)} fusion(bf16[8,32,128,128]{2,3,0,1:T(8,128)(2,1)} %copy.135, pred[8,32]{0,1:T(8,128)(4,1)S(1)} %copy.134, bf16[8,128,128]{2,1,0:T(8,128)(2,1)S(1)} %gather_fusion.19, pred[8]{0:T(512)(128)(4,1)S(1)} %and_bitcast_fusion.7), kind=kOutput, calls=%fused_computation.83 | convolution fusion | flops 1078591488 | bytes 9699592 | tf_op jit(solution)/shard_map/while/body/eval_jaxpr/cxy,csyz->sxz/dot_general | solution.py:35
  406.2 7.0 %fusion.57 = bf16[8,1,32,128,128]{3,4,2,1,0:T(8,128)(2,1)} fusion(bf16[8,1,32,128,128]{3,4,2,1,0:T(8,128)(2,1)} %fusion.51, bf16[8,32,128,128]{2,3,0,1:T(8,128)(2,1)} %copy.143, pred[8,32]{0,1:T(8,128)(4,1)S(1)} %copy.142, bf16[8,128,128]{2,1,0:T(8,128)(2,1)S(1)} %gather_fusion.22, pred[8]{0:T(512)(128)(4,1)S(1)} %and_bitcast_fusion.6), kind=kOutput, calls=%fused_computation.85 | convolution fusion | flops 1078591488 | bytes 9699592 | tf_op jit(solution)/shard_map/while/body/eval_jaxpr/cxy,csyz->sxz/dot_general | solution.py:35
  413.2 7.0 %fusion.63 = bf16[8,1,32,128,128]{3,4,2,1,0:T(8,128)(2,1)} fusion(bf16[8,1,32,128,128]{3,4,2,1,0:T(8,128)(2,1)} %fusion.57, bf16[8,32,128,128]{2,3,0,1:T(8,128)(2,1)} %copy.151, pred[8,32]{0,1:T(8,128)(4,1)S(1)} %copy.150, bf16[8,128,128]{2,1,0:T(8,128)(2,1)S(1)} %gather_fusion.25, pred[8]{0:T(512)(128)(4,1)S(1)} %and_bitcast_fusion.5), kind=kOutput, calls=%fused_computation.87 | convolution fusion | flops 1078591488 | bytes 9699592 | tf_op jit(solution)/shard_map/while/body/eval_jaxpr/cxy,csyz->sxz/dot_general | solution.py:35
  420.2 3.5 fusion.69
  423.7 3.5 fusion.75
  427.3 3.5 fusion.81
  430.8 3.8 fusion.87
  434.6 3.5 fusion.93
  438.1 8.1 %gather_fusion.16 = bf16[8,32,128,128]{2,3,1,0:T(8,128)(2,1)} fusion(bf16[8,32,128,128]{2,3,1,0:T(8,128)(2,1)} %bitcast.145, s32[1024]{0:T(1024)S(1)} %pad_clamp_fusion), kind=kCustom, calls=%fused_computation.40 | custom fusion | bytes 16777248 | tf_op jit(solution)/shard_map/jit(_take)/gather | solution.py:71
  446.2 7.5 %bitcast_select_fusion = bf16[8,1,32,128,128]{3,4,2,0,1:T(8,128)(2,1)} fusion(bf16[8,32,128,128]{2,3,1,0:T(8,128)(2,1)} %gather_fusion.16, pred[8]{0:T(512)(128)(4,1)S(1)} %compare_and_fusion.8), kind=kLoop, calls=%fused_computation.41 | loop fusion | flops 4194304 | bytes 16777224 | tf_op jit(solution)/shard_map/jit(_take)/select_n | solution.py:71
  453.7 98.9 %reduce-scatter.2.cloned.1.call-done = bf16[1,1,32,128,128]{3,4,2,0,1:T(8,128)(2,1)} async-done(((bf16[8,1,32,128,128]{3,4,2,0,1:T(8,128)(2,1)}), bf16[1,1,32,128,128]{3,4,2,0,1:T(8,128)(2,1)}) %reduce-scatter.2.cloned.1.call-update) | async-done | bytes 1048592 | tf_op jit(solution)/shard_map/reduce_scatter | solution.py:72
  552.6 2.3 copy.192
  (250 shorter events, 32.8 us)
Async XLA Ops:
  6.5 9.9 %copy-start = (s32[8,32]{1,0:T(8,128)S(1)}, s32[8,32]{1,0:T(8,128)}, u32[]{:S(2)}) copy-start(s32[8,32]{1,0:T(8,128)} %param.13) | copy-start | bytes 3076
  6.5 179.3 %all-gather.2.cloned.1.call-start = ((), (), s32[]{:S(2)}) async-start(), calls=%async_computation.1 | async-start | bytes 8650752 | tf_op jit(solution)/shard_map/all_gather | solution.py:54
  7.3 545.4 %reduce-scatter.2.cloned.1.call-start = ((), (), s32[]{:S(2)}) async-start(), calls=%async_computation.2 | async-start | bytes 9437184 | tf_op jit(solution)/shard_map/reduce_scatter | solution.py:72
  7.3 34.4 %collective-permute-start = (bf16[1,32,128,128]{3,2,1,0:T(8,128)(2,1)}, bf16[1,32,128,128]{3,2,1,0:T(8,128)(2,1)S(1)}, u32[]{:S(2)}, u32[]{:S(2)}) collective-permute-start(bf16[1,32,128,128]{3,2,1,0:T(8,128)(2,1)} %bitcast.425), channel_id=1, source_target_pairs={{224,0},{0,32},{32,64},{64,96},{96,128},{128,160},{160,192},{192,2... | collective-permute-start | bytes 3145736 | tf_op jit(solution)/shard_map/ppermute | solution.py:12
  41.7 27.2 %collective-permute-start.1 = (bf16[1,32,128,128]{3,2,1,0:T(8,128)(2,1)S(1)}, bf16[1,32,128,128]{3,2,1,0:T(8,128)(2,1)S(1)}, u32[]{:S(2)}, u32[]{:S(2)}) collective-permute-start(bf16[1,32,128,128]{3,2,1,0:T(8,128)(2,1)S(1)} %collective-permute-done), channel_id=1, source_target_pairs={{224,0},{0,32},{32,64},{64,96},{96,128},{128,160},{160,192},{192,2... | collective-permute-start | bytes 3145736 | tf_op jit(solution)/shard_map/ppermute | solution.py:12
  68.9 24.7 %collective-permute-start.2 = (bf16[1,32,128,128]{3,2,1,0:T(8,128)(2,1)S(1)}, bf16[1,32,128,128]{3,2,1,0:T(8,128)(2,1)S(1)}, u32[]{:S(2)}, u32[]{:S(2)}) collective-permute-start(bf16[1,32,128,128]{3,2,1,0:T(8,128)(2,1)S(1)} %collective-permute-done.1), channel_id=1, source_target_pairs={{224,0},{0,32},{32,64},{64,96},{96,128},{128,160},{160,192},{192,2... | collective-permute-start | bytes 3145736 | tf_op jit(solution)/shard_map/ppermute | solution.py:12
  93.6 70.5 %copy-start.2 = (bf16[1,32,128,128]{3,2,1,0:T(8,128)(2,1)}, bf16[1,32,128,128]{3,2,1,0:T(8,128)(2,1)S(1)}, u32[]{:S(2)}) copy-start(bf16[1,32,128,128]{3,2,1,0:T(8,128)(2,1)S(1)} %collective-permute-done.2) | copy-start | bytes 3145732
  93.6 23.8 %collective-permute-start.3 = (bf16[1,32,128,128]{3,2,1,0:T(8,128)(2,1)S(1)}, bf16[1,32,128,128]{3,2,1,0:T(8,128)(2,1)S(1)}, u32[]{:S(2)}, u32[]{:S(2)}) collective-permute-start(bf16[1,32,128,128]{3,2,1,0:T(8,128)(2,1)S(1)} %collective-permute-done.2), channel_id=1, source_target_pairs={{224,0},{0,32},{32,64},{64,96},{96,128},{128,160},{160,192},{192,2... | collective-permute-start | bytes 3145736 | tf_op jit(solution)/shard_map/ppermute | solution.py:12
  117.4 45.2 %copy-start.3 = (bf16[1,32,128,128]{3,2,1,0:T(8,128)(2,1)}, bf16[1,32,128,128]{3,2,1,0:T(8,128)(2,1)S(1)}, u32[]{:S(2)}) copy-start(bf16[1,32,128,128]{3,2,1,0:T(8,128)(2,1)S(1)} %collective-permute-done.3) | copy-start | bytes 3145732
  117.4 22.9 %collective-permute-start.4 = (bf16[1,32,128,128]{3,2,1,0:T(8,128)(2,1)S(1)}, bf16[1,32,128,128]{3,2,1,0:T(8,128)(2,1)S(1)}, u32[]{:S(2)}, u32[]{:S(2)}) collective-permute-start(bf16[1,32,128,128]{3,2,1,0:T(8,128)(2,1)S(1)} %collective-permute-done.3), channel_id=1, source_target_pairs={{224,0},{0,32},{32,64},{64,96},{96,128},{128,160},{160,192},{192,2... | collective-permute-start | bytes 3145736 | tf_op jit(solution)/shard_map/ppermute | solution.py:12
  140.3 22.3 %copy-start.4 = (bf16[1,32,128,128]{3,2,1,0:T(8,128)(2,1)}, bf16[1,32,128,128]{3,2,1,0:T(8,128)(2,1)S(1)}, u32[]{:S(2)}) copy-start(bf16[1,32,128,128]{3,2,1,0:T(8,128)(2,1)S(1)} %collective-permute-done.4) | copy-start | bytes 3145732
  140.3 22.1 %collective-permute-start.5 = (bf16[1,32,128,128]{3,2,1,0:T(8,128)(2,1)S(1)}, bf16[1,32,128,128]{3,2,1,0:T(8,128)(2,1)}, u32[]{:S(2)}, u32[]{:S(2)}) collective-permute-start(bf16[1,32,128,128]{3,2,1,0:T(8,128)(2,1)S(1)} %collective-permute-done.4), channel_id=1, source_target_pairs={{224,0},{0,32},{32,64},{64,96},{96,128},{128,160},{160,192},{192,2... | collective-permute-start | bytes 3145736 | tf_op jit(solution)/shard_map/ppermute | solution.py:12
  162.4 21.6 %collective-permute-start.6 = (bf16[1,32,128,128]{3,2,1,0:T(8,128)(2,1)}, bf16[1,32,128,128]{3,2,1,0:T(8,128)(2,1)}, u32[]{:S(2)}, u32[]{:S(2)}) collective-permute-start(bf16[1,32,128,128]{3,2,1,0:T(8,128)(2,1)} %collective-permute-done.5), channel_id=1, source_target_pairs={{224,0},{0,32},{32,64},{64,96},{96,128},{128,160},{160,192},{192,2... | collective-permute-start | bytes 3145736 | tf_op jit(solution)/shard_map/ppermute | solution.py:12
  406.2 14.0 %slice-start.8 = ((s8[8388608]{0:T(1024)(128)(4,1)}), s8[4194304]{0:T(1024)(128)(4,1)S(1)}, s32[]{:S(2)}) async-start(s8[8388608]{0:T(1024)(128)(4,1)} %bitcast.423), calls=%async_computation.11 | async-start | bytes 8388608
  413.2 7.0 %slice-start.9 = ((s8[8388608]{0:T(1024)(128)(4,1)}), s8[4194304]{0:T(1024)(128)(4,1)S(1)}, s32[]{:S(2)}) async-start(s8[8388608]{0:T(1024)(128)(4,1)} %bitcast.423), calls=%async_computation.12 | async-start | bytes 8388608
  413.2 10.5 %slice-start.6 = ((s8[8388608]{0:T(1024)(128)(4,1)}), s8[4194304]{0:T(1024)(128)(4,1)S(1)}, s32[]{:S(2)}) async-start(s8[8388608]{0:T(1024)(128)(4,1)} %bitcast.421), calls=%async_computation.9 | async-start | bytes 8388608
  420.2 3.5 slice-start.7
  420.2 7.1 %slice-start.4 = ((s8[8388608]{0:T(1024)(128)(4,1)}), s8[4194304]{0:T(1024)(128)(4,1)S(1)}, s32[]{:S(2)}) async-start(s8[8388608]{0:T(1024)(128)(4,1)} %bitcast.419), calls=%async_computation.7 | async-start | bytes 8388608
  423.7 3.5 slice-start.5
  423.7 7.1 %slice-start.2 = ((s8[8388608]{0:T(1024)(128)(4,1)}), s8[4194304]{0:T(1024)(128)(4,1)S(1)}, s32[]{:S(2)}) async-start(s8[8388608]{0:T(1024)(128)(4,1)} %bitcast.417), calls=%async_computation.5 | async-start | bytes 8388608
  427.3 3.5 slice-start.3
  427.3 7.3 %slice-start = ((s8[8388608]{0:T(1024)(128)(4,1)}), s8[4194304]{0:T(1024)(128)(4,1)S(1)}, s32[]{:S(2)}) async-start(s8[8388608]{0:T(1024)(128)(4,1)} %bitcast.415), calls=%async_computation.3 | async-start | bytes 8388608
  430.8 3.8 slice-start.1
  446.2 108.7 %copy-start.1 = (s32[8,32]{1,0:T(8,128)S(1)}, s32[8,32]{1,0:T(8,128)}, u32[]{:S(2)}) copy-start(s32[8,32]{1,0:T(8,128)} %param.13) | copy-start | bytes 3076
Sparse Core Ops, SparseCore 0:
  10.0 62.1 all-gather.1
  453.8 98.7 reduce-scatter.1
where the time goes:
time: 573 us; the launch traced here: 562 us
  local copies, waits for them, and re-layouts  255 us (45%)
  waiting for transfers between devices  226 us (39%)
  matrix products  38.6 us (7%)
  other arithmetic  23.6 us (4%)
  between operations  14.6 us (3%)
    gather x16, local copies, waits for them, and re-layouts, slab_terms(): chosen = panel_blocks[local_row[:, None], slot_pick]  213 us
    ppermute x7, waiting for transfers between devices, passed_along(): return lax.ppermute(block, axis, route)  126 us
    reduce_scatter x1, waiting for transfers between devices, local(): lax.psum_scatter(partial_value.astype(jnp.float32).astype(jnp.bfloat16),...  98.9 us
    dot_general x8, matrix products, slab_terms(): jnp.einsum('cxy,csyz->sxz', selected, chosen, preferred_element_type=jnp....  38.6 us
    gather x8, local copies, waits for them, and re-layouts, local(): selected = jnp.take_along_axis(current, picked[:, :, None, None], axis=1)  12.1 us
  transfers between devices with their start and end apart: 9, of which 7 were waited for; matrix products, arithmetic and copies ran while one was open for 8% of the time, Pallas kernels for 0%

commit v1 on v0

v1 whole, which is shorter than its diff:
```python
import functools

import jax
import jax.numpy as jnp
from jax import lax
from jax.experimental import pallas as pl
from jax.experimental.pallas import tpu as pltpu
from jax.sharding import PartitionSpec as P

BLK = 128
NZ, NY, NX, NC = 8, 4, 4, 2
KEPT = 32
HALF = 4
SEL = 8
SET = 128
ZERO = 2 * SET
AXES = ("row", "col")
OFFSETS = (2, 1, -1, 0)


def send(block, target):
    pairs = []
    for z in range(NZ):
        for y in range(NY):
            for x in range(NX):
                for c in range(NC):
                    tz, ty, tx, tc = target(z, y, x, c)
                    tz, ty, tx = tz % NZ, ty % NY, tx % NX
                    src = ((z * NY + y) * NX + x) * NC + c
                    dst = ((tz * NY + ty) * NX + tx) * NC + tc
                    pairs.append((src, dst))
    return lax.ppermute(block, AXES, pairs)


def swap(block):
    return send(block, lambda z, y, x, c: (z, y, x, 1 - c))


def along_z(block, distance):
    return send(block, lambda z, y, x, c: (z + distance * (1 - 2 * c), y, x, c))


def in_plane(block, distance, flip):
    def target(z, y, x, c):
        if c ^ flip:
            return (z, y + distance, x, c)
        return (z, y, x + distance, c)

    return send(block, target)


def ring(block, flip):
    half = block.shape[0] // 2
    up = in_plane(block, 1, flip)
    down = in_plane(block, -1, flip)
    up2 = in_plane(up[:half], 1, flip)
    down2 = in_plane(down[half:], -1, flip)
    return (up, down, up2, down2)


def plane_gather(block, flip):
    first = jnp.concatenate((block,) + ring(block, flip), axis=0)
    return (first,) + ring(first, 1 - flip)


def products_kernel(n_rows, n_add, row_srcs, idx_ref, order_ref, count_ref, *refs):
    n_left = max(src for src, _ in row_srcs) + 1
    panel_refs = refs[:10]
    left_refs = refs[10:10 + n_left]
    add_refs = refs[10 + n_left:10 + n_left + n_add]
    out_ref, panel, lcat, panel_sem, left_sem = refs[10 + n_left + n_add:]
    copies = []
    at = 0
    for n, ref in enumerate(panel_refs):
        size = ref.shape[0]
        copies.append(pltpu.make_async_copy(ref, panel.at[pl.ds(at, size)], panel_sem.at[n]))
        at += size
    for copy in copies:
        copy.start()
    left_copies = []
    for r, (src, base) in enumerate(row_srcs):
        for t in range(SEL):
            which = order_ref[r * SEL + t]
            copy = pltpu.make_async_copy(
                left_refs[src].at[base + which],
                lcat.at[r, :, pl.ds(t * BLK, BLK)],
                left_sem.at[r, t],
            )
            copy.start()
            left_copies.append(copy)
    panel[ZERO] = jnp.zeros((BLK, BLK), panel.dtype)
    for copy in left_copies:
        copy.wait()
    for copy in copies:
        copy.wait()
    for r in range(n_rows):
        pairs_here = (count_ref[r] + 1) // 2
        for pairs in range(SEL // 2 + 1):

            @pl.when(pairs_here == pairs)
            def _(r=r, pairs=pairs):
                def step(sp, carry):
                    s0 = 2 * sp
                    s1 = s0 + 1
                    if pairs:
                        strips = []
                        for t in range(2 * pairs):
                            at0 = idx_ref[(r * SEL + t) * KEPT + s0]
                            at1 = idx_ref[(r * SEL + t) * KEPT + s1]
                            strips.append(jnp.concatenate([panel[at0], panel[at1]], axis=1))
                        rhs = jnp.concatenate(strips, axis=0)
                        total = jnp.dot(
                            lcat[r, :, : 2 * pairs * BLK], rhs, preferred_element_type=jnp.float32
                        )
                    else:
                        total = jnp.zeros((BLK, 2 * BLK), jnp.float32)
                    first = total[:, :BLK]
                    second = total[:, BLK:]
                    for add in add_refs:
                        first = first + add[r, s0].astype(jnp.float32)
                        second = second + add[r, s1].astype(jnp.float32)
                    out_ref[r, s0] = first.astype(out_ref.dtype)
                    out_ref[r, s1] = second.astype(out_ref.dtype)
                    return carry

                lax.fori_loop(0, KEPT // 2, step, 0)


def products(tables, rows, panel_parts, lefts, row_srcs, adds, dtype=jnp.bfloat16):
    idx, order, count = tables
    n = len(rows)
    pick = jnp.array(rows, dtype=jnp.int32)
    idx = idx[pick].reshape(-1)
    order = order[pick].reshape(-1)
    count = count[pick]
    smem = pl.BlockSpec(memory_space=pltpu.SMEM)
    hbm = pl.BlockSpec(memory_space=pl.ANY)
    vmem = pl.BlockSpec(memory_space=pltpu.VMEM)
    return pl.pallas_call(
        functools.partial(products_kernel, n, len(adds), row_srcs),
        out_shape=jax.ShapeDtypeStruct((n, KEPT, BLK, BLK), dtype),
        in_specs=[smem] * 3 + [hbm] * (len(panel_parts) + len(lefts)) + [vmem] * len(adds),
        out_specs=vmem,
        scratch_shapes=[
            pltpu.VMEM((ZERO + 1, BLK, BLK), jnp.bfloat16),
            pltpu.VMEM((n, BLK, SEL * BLK), jnp.bfloat16),
            pltpu.SemaphoreType.DMA((len(panel_parts),)),
            pltpu.SemaphoreType.DMA((n, SEL)),
        ],
        compiler_params=pltpu.CompilerParams(vmem_limit_bytes=40 * 1024 * 1024),
        cost_estimate=pl.CostEstimate(
            flops=n * KEPT * SEL * 2 * BLK**3, bytes_accessed=10 * 1024 * 1024, transcendentals=0
        ),
    )(idx, order, count, *panel_parts, *lefts, *adds)


def reached(z, c):
    j = jnp.arange(SEL, dtype=jnp.int32)
    panel = (z + NZ // 2 * (j // HALF)) % NZ
    return panel * (2 * HALF) + c * HALF + j % HALF


def local(left_blocks, left_cols, reach_blocks, reach_cols):
    z = lax.axis_index("row")
    col = lax.axis_index("col")
    c = col % NC
    x = col // NC % NX
    y = col // (NC * NX)
    sign = 1 - 2 * c

    blocks = reach_blocks[:, 0]
    own_half = lax.dynamic_slice_in_dim(blocks, HALF * c, HALF, 0)
    other_half = lax.dynamic_slice_in_dim(blocks, HALF * (1 - c), HALF, 0)
    near_set = jnp.concatenate([own_half, swap(other_half)], axis=0)
    far_set = send(near_set, lambda z, y, x, c: (z + NZ // 2, y, x, c))
    panel_parts = plane_gather(near_set, 0) + plane_gather(far_set, 1)

    own_left = left_blocks[0, 0]
    own_cols = lax.dynamic_index_in_dim(left_cols[:, 0], z, 0, keepdims=False)

    def chosen(offset):
        target = z + offset * sign + NZ
        names = jnp.concatenate([reached(target, c), reached(target, 1 - c)])
        at = jnp.argmax(names[:, None] == own_cols[None, :], axis=1).astype(jnp.int32)
        return own_left[at]

    arrived = []
    for offset in OFFSETS:
        picked = chosen(offset)
        arrived.append(along_z(picked, offset) if offset else picked)
    swapped = swap(jnp.concatenate([a[SEL:] for a in arrived], axis=0))

    cols_here = left_cols[:, 0]
    cols_there = swap(cols_here)
    steps = jnp.array(OFFSETS, dtype=jnp.int32)
    cols = jnp.concatenate(
        [cols_there[(z + steps * sign + NZ) % NZ], cols_here[(z - steps * sign + NZ) % NZ]], axis=0
    )
    far_cols = send(reach_cols, lambda z, y, x, c: (z + NZ // 2, y, x, c))
    kept = jnp.concatenate(
        [
            lax.dynamic_slice_in_dim(reach_cols, HALF * c, HALF, 0),
            lax.dynamic_slice_in_dim(far_cols, HALF * c, HALF, 0),
        ],
        axis=0,
    )
    slot = jnp.arange(KEPT, dtype=jnp.int32)

    def place(offset):
        offset = offset % 4
        return jnp.where(offset == 0, 0, jnp.where(offset == 3, 1, jnp.where(offset == 1, 2, 3)))

    dx = place(slot // NC % NX - x + NX)
    dy = place(slot // (NC * NX) - y + NY)
    other = jnp.where(slot % NC == c, 0, 1)
    along = jnp.where(c == 0, dx, dy)
    across = jnp.where(c == 0, dy, dx)
    j = jnp.arange(SEL, dtype=jnp.int32)
    near_place = across * 32 + along * 8 + other * HALF
    far_place = along * 32 + across * 8 + other * HALF + SET
    place_of = jnp.where(j[:, None] < HALF, near_place[None, :], far_place[None, :]) + j[:, None] % HALF
    present = jnp.any(reached(z, c)[None, :, None] == cols[:, None, :], axis=2)
    rank = jnp.cumsum(present.astype(jnp.int32), axis=1) - 1
    hit = present[:, None, :] & (rank[:, None, :] == j[None, :, None])
    order = jnp.sum(jnp.where(hit, j[None, None, :], 0), axis=2)
    same = kept[None, :, None, :] == cols[:, None, :, None]
    at = jnp.sum(jnp.where(same, place_of[None, :, None, :] - ZERO, 0), axis=3)
    idx = ZERO + jnp.sum(jnp.where(hit[:, :, :, None], at[:, None, :, :], 0), axis=2)
    count = jnp.sum(present.astype(jnp.int32), axis=1)
    tables = (idx, order, count)

    call = functools.partial(products, tables)
    far_l, near_l, leaf_l, own_l = arrived
    far_there = call((0,), panel_parts, (swapped,), ((0, 0),), ())
    far_here = call((4,), panel_parts, (far_l,), ((0, 0),), (swap(far_there),))
    far_got = along_z(far_here, -1)
    rest_there = call((1, 2, 3), panel_parts, (swapped,), ((0, 8), (0, 16), (0, 24)), ())
    rest_got = swap(rest_there)
    rest_here = call(
        (6, 7), panel_parts, (leaf_l, own_l), ((0, 0), (1, 0)), (rest_got[1:],)
    )
    leaf_got = along_z(rest_here[:1], 1)
    near_here = call((5,), panel_parts, (near_l,), ((0, 0),), (rest_got[:1], far_got))
    near_got = along_z(near_here, -1)
    total = (
        rest_here[1].astype(jnp.float32)
        + leaf_got[0].astype(jnp.float32)
        + near_got[0].astype(jnp.float32)
    )
    return total.astype(jnp.bfloat16)[None, None]


def solution(mesh):
    in_specs = (
        P("row", "col", None, None, None),
        P(None, "col", None),
        P("row", "col", None, None),
        P("row", None),
    )
    out_specs = P("row", "col", None, None, None)
    return jax.shard_map(local, mesh=mesh, in_specs=in_specs, out_specs=out_specs, check_vma=False)
```

time: 573 us -> 183 us (0.32); the launches traced: 562 us -> 182 us
  local copies, waits for them, and re-layouts: 255 us -> 33.9 us
  waiting for transfers between devices: 226 us -> 41.8 us
  Pallas kernels: 0 us -> 50.5 us
  starting transfers between devices: 4.55 us -> 45.8 us
  matrix products: 38.6 us -> 0 us
  between operations: 14.6 us -> 0.43 us
  other arithmetic: 23.6 us -> 9.56 us
    gather x65 -> x14, local copies, waits for them, and re-layouts: 250 us -> 10.9 us  [the longest x4 4.93 us: chosen(): return own_left[at]]
    reduce_scatter x1 -> x0, waiting for transfers between devices: 98.9 us -> none  [local(): lax.psum_scatter(partial_value.astype(jnp.float32).astype(jnp.bfloat16),...]
    ppermute x7 -> x29, waiting for transfers between devices: 126 us -> 41.8 us  [send(): return lax.ppermute(block, AXES, pairs)]
    pallas_call x0 -> x5, Pallas kernels: none -> 50.5 us  [products(): pl.pallas_call(functools.partial(products_kernel, n, len(adds), row_srcs)...]
    ppermute x7 -> x29, starting transfers between devices: 4.51 us -> 45.8 us  [send(): return lax.ppermute(block, AXES, pairs)]
    dot_general x8 -> x0, matrix products: 38.6 us -> none  [slab_terms(): jnp.einsum('cxy,csyz->sxz', selected, chosen, preferred_element_type=jnp....]
    slice x0 -> x16, local copies, waits for them, and re-layouts: none -> 11.7 us  [the longest x5 2.92 us: local(): swapped = swap(jnp.concatenate([a[SEL:] for a in arrived], axis=0))]
    select_n x18 -> x4, other arithmetic: 8.5 us -> 0.68 us  [the longest x1 0.67 us: local(): cols_there[(z + steps * sign + NZ) % NZ]]
  transfers between devices with their start and end apart: 9 -> 29, of which waited for: 7 -> 9; matrix products, arithmetic and copies ran while one was open for 8% -> 23% of each run, Pallas kernels for 0% -> 19%
where the time goes in v1:
time: 183 us; the launch traced here: 182 us
  Pallas kernels  50.5 us (28%)
  starting transfers between devices  45.8 us (25%)
  waiting for transfers between devices  41.8 us (23%)
  local copies, waits for them, and re-layouts  33.9 us (19%)
  other arithmetic  9.56 us (5%)
    pallas_call x5, Pallas kernels, products(): pl.pallas_call(functools.partial(products_kernel, n, len(adds), row_srcs)...  50.5 us
    ppermute x29, starting transfers between devices, send(): return lax.ppermute(block, AXES, pairs)  45.8 us
    ppermute x29, waiting for transfers between devices, send(): return lax.ppermute(block, AXES, pairs)  41.8 us
    unnamed x17, local copies, waits for them, and re-layouts  7.24 us
    gather x4, local copies, waits for them, and re-layouts, chosen(): return own_left[at]  4.93 us
  transfers between devices with their start and end apart: 29, of which 9 were waited for; matrix products, arithmetic and copies ran while one was open for 23% of the time, Pallas kernels for 19%

profile of v1, /device:TPU:1, one launch (start us, length us, event | category | flops | bytes accessed | tf_op | source)
XLA Modules:
  0.0 182.0 jit_solution(2688181341477147102)
XLA Ops:
  0.0 3.2 %collective-permute-start = (s32[8,32]{1,0:T(8,128)}, s32[8,32]{1,0:T(8,128)S(1)}, u32[]{:S(2)}, u32[]{:S(2)}) collective-permute-start(s32[8,32]{1,0:T(8,128)} %bitcast.21), channel_id=1, source_target_pairs={{0,1},{1,0},{2,3},{3,2},{4,5},{5,4},{6,7},{7,6},{8,9},{9,8},{10,11... | collective-permute-start | bytes 3080 | tf_op jit(solution)/shard_map/ppermute | solution.py:32
  3.2 5.2 %collective-permute-start.1 = (s32[8,32]{1,0:T(8,128)}, s32[8,32]{1,0:T(8,128)S(1)}, u32[]{:S(2)}, u32[]{:S(2)}) collective-permute-start(s32[8,32]{1,0:T(8,128)} %param.13), channel_id=1, source_target_pairs={{0,128},{1,129},{2,130},{3,131},{4,132},{5,133},{6,134},{7,135},{8... | collective-permute-start | bytes 3080 | tf_op jit(solution)/shard_map/ppermute | solution.py:32
  8.4 0.9 dynamic-slice_bitcast_fusion
  15.3 1.6 constant_dynamic-update-slice_fusion.5
  17.1 2.7 %collective-permute-start.4 = (bf16[8,128,128]{2,1,0:T(8,128)(2,1)S(1)}, bf16[8,128,128]{2,1,0:T(8,128)(2,1)S(1)}, u32[]{:S(2)}, u32[]{:S(2)}) collective-permute-start(bf16[8,128,128]{2,1,0:T(8,128)(2,1)S(1)} %pad_maximum_fusion.1), channel_id=1, source_target_pairs={{0,6},{1,25},{2,0},{3,27},{4,2},{5,29},{6,4},{7,31},{8,14},{9,1},{... | collective-permute-start | bytes 786440 | tf_op jit(solution)/shard_map/ppermute | solution.py:32
  20.5 1.2 gather_fusion.1
  22.4 1.5 gather_fusion.10
  23.9 1.4 gather_fusion.5
  25.3 1.4 gather_fusion.11
  28.0 2.8 %collective-permute-start.6 = (bf16[4,128,128]{2,1,0:T(8,128)(2,1)S(1)}, bf16[4,128,128]{2,1,0:T(8,128)(2,1)S(1)}, u32[]{:S(2)}, u32[]{:S(2)}) collective-permute-start(bf16[4,128,128]{2,1,0:T(8,128)(2,1)S(1)} %slice.161), channel_id=1, source_target_pairs={{0,6},{1,25},{2,0},{3,27},{4,2},{5,29},{6,4},{7,31},{8,14},{9,1},{... | collective-permute-start | bytes 393224 | tf_op jit(solution)/shard_map/ppermute | solution.py:32
  30.8 2.6 %collective-permute-start.13 = (bf16[8,128,128]{2,1,0:T(8,128)(2,1)S(1)}, bf16[8,128,128]{2,1,0:T(8,128)(2,1)S(1)}, u32[]{:S(2)}, u32[]{:S(2)}) collective-permute-start(bf16[8,128,128]{2,1,0:T(8,128)(2,1)S(1)} %collective-permute-done.11), channel_id=1, source_target_pairs={{0,24},{1,7},{2,26},{3,1},{4,28},{5,3},{6,30},{7,5},{8,0},{9,15},{... | collective-permute-start | bytes 786440 | tf_op jit(solution)/shard_map/ppermute | solution.py:32
  33.4 0.7 constant_dynamic-update-slice_fusion.10
  36.1 3.7 %collective-permute-start.22 = (bf16[16,128,128]{2,1,0:T(8,128)(2,1)}, bf16[16,128,128]{2,1,0:T(8,128)(2,1)}, u32[]{:S(2)}, u32[]{:S(2)}) collective-permute-start(bf16[16,128,128]{2,1,0:T(8,128)(2,1)} %gather_fusion.11), channel_id=1, source_target_pairs={{0,32},{1,225},{2,34},{3,227},{4,36},{5,229},{6,38},{7,231},{8,40}... | collective-permute-start | bytes 1572872 | tf_op jit(solution)/shard_map/ppermute | solution.py:32
  41.2 2.6 %collective-permute-start.15 = (bf16[4,128,128]{2,1,0:T(8,128)(2,1)S(1)}, bf16[4,128,128]{2,1,0:T(8,128)(2,1)S(1)}, u32[]{:S(2)}, u32[]{:S(2)}) collective-permute-start(bf16[4,128,128]{2,1,0:T(8,128)(2,1)S(1)} %slice.165), channel_id=1, source_target_pairs={{0,24},{1,7},{2,26},{3,1},{4,28},{5,3},{6,30},{7,5},{8,0},{9,15},{... | collective-permute-start | bytes 393224 | tf_op jit(solution)/shard_map/ppermute | solution.py:32
  43.9 0.7 constant_dynamic-update-slice_fusion.9
  45.4 3.9 %collective-permute-done.14 = bf16[4,128,128]{2,1,0:T(8,128)(2,1)S(1)} collective-permute-done((bf16[4,128,128]{2,1,0:T(8,128)(2,1)S(1)}, bf16[4,128,128]{2,1,0:T(8,128)(2,1)S(1)}, u32[]{:S(2)}, u32[]{:S(2)}) %collective-permute-start.14) | collective-permute-done | bytes 131104 | tf_op jit(solution)/shard_map/ppermute | solution.py:32
  49.3 1.4 collective-permute-start.21
  52.0 1.5 collective-permute-start.7
  53.5 2.8 %collective-permute-start.17 = (bf16[32,128,128]{2,1,0:T(8,128)(2,1)}, bf16[32,128,128]{2,1,0:T(8,128)(2,1)}, u32[]{:S(2)}, u32[]{:S(2)}) collective-permute-start(bf16[32,128,128]{2,1,0:T(8,128)(2,1)} %constant_dynamic-update-slice_fusion.6.refs_5_), channel_id=1, source_target_pairs={{0,6},{1,25},{2,0},{3,27},{4,2},{5,29},{6,4},{7,31},{8,14},{9,1},{... | collective-permute-start | bytes 3145736 | tf_op jit(solution)/shard_map/ppermute | solution.py:32
  56.8 1.0 slice.169
  57.8 1.0 slice.170
  58.8 5.9 %collective-permute-done.21.refs_10_ = bf16[16,128,128]{2,1,0:T(8,128)(2,1)} collective-permute-done((bf16[16,128,128]{2,1,0:T(8,128)(2,1)}, bf16[16,128,128]{2,1,0:T(8,128)(2,1)}, u32[]{:S(2)}, u32[]{:S(2)}) %collective-permute-start.21) | collective-permute-done | bytes 524320 | tf_op jit(solution)/shard_map/ppermute | solution.py:32
  64.7 1.0 slice.168
  65.6 1.1 pad_maximum_fusion
  66.8 6.0 %collective-permute-start.23 = (bf16[32,128,128]{2,1,0:T(8,128)(2,1)}, bf16[32,128,128]{2,1,0:T(8,128)(2,1)}, u32[]{:S(2)}, u32[]{:S(2)}) collective-permute-start(bf16[32,128,128]{2,1,0:T(8,128)(2,1)} %pad_maximum_fusion), channel_id=1, source_target_pairs={{0,1},{1,0},{2,3},{3,2},{4,5},{5,4},{6,7},{7,6},{8,9},{9,8},{10,11... | collective-permute-start | bytes 3145736 | tf_op jit(solution)/shard_map/ppermute | solution.py:32
  73.0 0.8 slice.163
  73.9 0.9 collective-permute-start.10
  74.8 0.8 slice.162
  76.2 2.8 %collective-permute-done.17.refs_7_ = bf16[32,128,128]{2,1,0:T(8,128)(2,1)} collective-permute-done((bf16[32,128,128]{2,1,0:T(8,128)(2,1)}, bf16[32,128,128]{2,1,0:T(8,128)(2,1)}, u32[]{:S(2)}, u32[]{:S(2)}) %collective-permute-start.17) | collective-permute-done | bytes 1048608 | tf_op jit(solution)/shard_map/ppermute | solution.py:32
  79.0 1.9 %slice.167 = bf16[16,128,128]{2,1,0:T(8,128)(2,1)} slice(bf16[32,128,128]{2,1,0:T(8,128)(2,1)} %collective-permute-done.17.refs_7_), slice={[16:32], [0:128], [0:128]} | slice | bytes 1048576 | tf_op jit(solution)/shard_map/slice | solution.py:57
  80.9 3.4 %collective-permute-start.19 = (bf16[16,128,128]{2,1,0:T(8,128)(2,1)}, bf16[16,128,128]{2,1,0:T(8,128)(2,1)}, u32[]{:S(2)}, u32[]{:S(2)}) collective-permute-start(bf16[16,128,128]{2,1,0:T(8,128)(2,1)} %slice.167), channel_id=1, source_target_pairs={{0,6},{1,25},{2,0},{3,27},{4,2},{5,29},{6,4},{7,31},{8,14},{9,1},{... | collective-permute-start | bytes 1572872 | tf_op jit(solution)/shard_map/ppermute | solution.py:32
  84.3 1.9 %slice.166 = bf16[16,128,128]{2,1,0:T(8,128)(2,1)} slice(bf16[32,128,128]{2,1,0:T(8,128)(2,1)} %collective-permute-done.16.refs_6_), slice={[0:16], [0:128], [0:128]} | slice | bytes 1048576 | tf_op jit(solution)/shard_map/slice | solution.py:56
  87.6 1.2 select_reduce_fusion
  89.7 5.8 %collective-permute-done.19.refs_9_ = bf16[16,128,128]{2,1,0:T(8,128)(2,1)} collective-permute-done((bf16[16,128,128]{2,1,0:T(8,128)(2,1)}, bf16[16,128,128]{2,1,0:T(8,128)(2,1)}, u32[]{:S(2)}, u32[]{:S(2)}) %collective-permute-start.19) | collective-permute-done | bytes 524320 | tf_op jit(solution)/shard_map/ppermute | solution.py:32
  95.5 4.6 %collective-permute-done.18.refs_8_ = bf16[16,128,128]{2,1,0:T(8,128)(2,1)} collective-permute-done((bf16[16,128,128]{2,1,0:T(8,128)(2,1)}, bf16[16,128,128]{2,1,0:T(8,128)(2,1)}, u32[]{:S(2)}, u32[]{:S(2)}) %collective-permute-start.18) | collective-permute-done | bytes 524320 | tf_op jit(solution)/shard_map/ppermute | solution.py:32
  100.1 15.1 %shard_map.100 = bf16[3,32,128,128]{3,2,1,0:T(8,128)(2,1)} custom-call(s32[768]{0:T(1024)S(1)} %reshape.306.idx_ref, s32[24]{0:T(128)S(1)} %reshape.307.order_ref, s32[3]{0:T(128)S(1)} %gather_fusion.9, bf16[32,128,128]{2,1,0:T(8,128)(2,1)} %constant_dynamic-update-slice_fusion.refs_0_, bf16[32,128,128]{2,1,0:T(8,128)(2,1)S(1)} %collective-permute-done.7.refs_1_, ...), custom_call_target="tpu_custom_call" | custom-call | flops 3221225472 | bytes 10485760 | tf_op jit(solution)/shard_map/pallas_call | solution.py:139
  115.1 1.7 collective-permute-start.24
  117.6 8.2 %shard_map.102 = bf16[1,32,128,128]{3,2,1,0:T(8,128)(2,1)} custom-call(s32[256]{0:T(256)S(1)} %reshape.312.idx_ref, s32[8]{0:T(128)S(1)} %get-tuple-element.117.order_ref, s32[1]{0:T(128)} %get-tuple-element.120.count_ref, bf16[32,128,128]{2,1,0:T(8,128)(2,1)} %constant_dynamic-update-slice_fusion.refs_0_, ...), custom_call_target="tpu_custom_call" | custom-call | flops 1073741824 | bytes 10485760 | tf_op jit(solution)/shard_map/pallas_call | solution.py:139
  126.0 2.9 %collective-permute-done.26.refs_11_ = bf16[1,32,128,128]{3,2,1,0:T(8,128)(2,1)} collective-permute-done((bf16[1,32,128,128]{3,2,1,0:T(8,128)(2,1)}, bf16[1,32,128,128]{3,2,1,0:T(8,128)(2,1)}, u32[]{:S(2)}, u32[]{:S(2)}) %collective-permute-start.26) | collective-permute-done | bytes 1048608 | tf_op jit(solution)/shard_map/ppermute | solution.py:32
  128.9 9.5 %shard_map.103 = bf16[1,32,128,128]{3,2,1,0:T(8,128)(2,1)} custom-call(s32[256]{0:T(256)S(1)} %reshape.310.idx_ref, s32[8]{0:T(128)S(1)} %get-tuple-element.118.order_ref, s32[1]{0:T(128)} %get-tuple-element.121.count_ref, bf16[32,128,128]{2,1,0:T(8,128)(2,1)} %constant_dynamic-update-slice_fusion.refs_0_, ...), custom_call_target="tpu_custom_call" | custom-call | flops 1073741824 | bytes 10485760 | tf_op jit(solution)/shard_map/pallas_call | solution.py:139
  140.7 1.9 %slice.172.refs_12_ = bf16[2,32,128,128]{3,2,1,0:T(8,128)(2,1)S(1)} slice(bf16[3,32,128,128]{3,2,1,0:T(8,128)(2,1)} %collective-permute-done.24), slice={[1:3], [0:32], [0:128], [0:128]} | slice | bytes 4194304 | tf_op jit(solution)/shard_map/slice | solution.py:240
  142.6 9.7 %shard_map.101 = bf16[2,32,128,128]{3,2,1,0:T(8,128)(2,1)S(1)} custom-call(s32[512]{0:T(512)S(1)} %reshape.304.idx_ref, s32[16]{0:T(128)S(1)} %reshape.305.order_ref, s32[2]{0:T(128)S(1)} %gather_fusion.4, bf16[32,128,128]{2,1,0:T(8,128)(2,1)} %constant_dynamic-update-slice_fusion.refs_0_, bf16[32,128,128]{2,1,0:T(8,128)(2,1)S(1)} %collective-permute-done.7.refs_1_, ...), custom_call_target="tpu_custom_call" | custom-call | flops 2147483648 | bytes 10485760 | tf_op jit(solution)/shard_map/pallas_call | solution.py:139
  152.4 3.5 %collective-permute-start.25 = (bf16[1,32,128,128]{3,2,1,0:T(8,128)(2,1)S(1)}, bf16[1,32,128,128]{3,2,1,0:T(8,128)(2,1)S(1)}, u32[]{:S(2)}, u32[]{:S(2)}) collective-permute-start(bf16[1,32,128,128]{3,2,1,0:T(8,128)(2,1)S(1)} %slice.174), channel_id=1, source_target_pairs={{0,32},{1,225},{2,34},{3,227},{4,36},{5,229},{6,38},{7,231},{8,40}... | collective-permute-start | bytes 3145736 | tf_op jit(solution)/shard_map/ppermute | solution.py:32
  155.9 1.3 slice.176.refs_11_
  157.2 8.1 %shard_map.104 = bf16[1,32,128,128]{3,2,1,0:T(8,128)(2,1)S(1)} custom-call(s32[256]{0:T(256)S(1)} %reshape.308.idx_ref, s32[8]{0:T(128)S(1)} %get-tuple-element.119.order_ref, s32[1]{0:T(128)} %get-tuple-element.122.count_ref, bf16[32,128,128]{2,1,0:T(8,128)(2,1)} %constant_dynamic-update-slice_fusion.refs_0_, ...), custom_call_target="tpu_custom_call" | custom-call | flops 1073741824 | bytes 10485760 | tf_op jit(solution)/shard_map/pallas_call | solution.py:139
  165.3 2.3 %collective-permute-done.25 = bf16[1,32,128,128]{3,2,1,0:T(8,128)(2,1)S(1)} collective-permute-done((bf16[1,32,128,128]{3,2,1,0:T(8,128)(2,1)S(1)}, bf16[1,32,128,128]{3,2,1,0:T(8,128)(2,1)S(1)}, u32[]{:S(2)}, u32[]{:S(2)}) %collective-permute-start.25) | collective-permute-done | bytes 1048608 | tf_op jit(solution)/shard_map/ppermute | solution.py:32
  167.6 13.0 %collective-permute-done.28 = bf16[1,32,128,128]{3,2,1,0:T(8,128)(2,1)S(1)} collective-permute-done((bf16[1,32,128,128]{3,2,1,0:T(8,128)(2,1)S(1)}, bf16[1,32,128,128]{3,2,1,0:T(8,128)(2,1)S(1)}, u32[]{:S(2)}, u32[]{:S(2)}) %collective-permute-start.28) | collective-permute-done | bytes 1048608 | tf_op jit(solution)/shard_map/ppermute | solution.py:32
  180.5 1.5 fusion
  (122 shorter events, 21.1 us)
Async XLA Ops:
  0.0 21.8 %copy-start = (bf16[1,1,32,128,128]{4,3,2,1,0:T(8,128)(2,1)S(1)}, bf16[1,1,32,128,128]{4,3,2,1,0:T(8,128)(2,1)}, u32[]{:S(2)}) copy-start(bf16[1,1,32,128,128]{4,3,2,1,0:T(8,128)(2,1)} %param.10) | copy-start | bytes 3145732
  0.0 26.7 %collective-permute-start = (s32[8,32]{1,0:T(8,128)}, s32[8,32]{1,0:T(8,128)S(1)}, u32[]{:S(2)}, u32[]{:S(2)}) collective-permute-start(s32[8,32]{1,0:T(8,128)} %bitcast.21), channel_id=1, source_target_pairs={{0,1},{1,0},{2,3},{3,2},{4,5},{5,4},{6,7},{7,6},{8,9},{9,8},{10,11... | collective-permute-start | bytes 3080 | tf_op jit(solution)/shard_map/ppermute | solution.py:32
  3.2 48.8 %collective-permute-start.1 = (s32[8,32]{1,0:T(8,128)}, s32[8,32]{1,0:T(8,128)S(1)}, u32[]{:S(2)}, u32[]{:S(2)}) collective-permute-start(s32[8,32]{1,0:T(8,128)} %param.13), channel_id=1, source_target_pairs={{0,128},{1,129},{2,130},{3,131},{4,132},{5,133},{6,134},{7,135},{8... | collective-permute-start | bytes 3080 | tf_op jit(solution)/shard_map/ppermute | solution.py:32
  9.3 7.5 %collective-permute-start.2 = (bf16[4,128,128]{2,1,0:T(8,128)(2,1)S(1)}, bf16[4,128,128]{2,1,0:T(8,128)(2,1)S(1)}, u32[]{:S(2)}, u32[]{:S(2)}) collective-permute-start(bf16[4,128,128]{2,1,0:T(8,128)(2,1)S(1)} %dynamic-slice_bitcast_fusion), channel_id=1, source_target_pairs={{0,1},{1,0},{2,3},{3,2},{4,5},{5,4},{6,7},{7,6},{8,9},{9,8},{10,11... | collective-permute-start | bytes 393224 | tf_op jit(solution)/shard_map/ppermute | solution.py:32
  16.9 13.9 %collective-permute-start.11 = (bf16[8,128,128]{2,1,0:T(8,128)(2,1)S(1)}, bf16[8,128,128]{2,1,0:T(8,128)(2,1)S(1)}, u32[]{:S(2)}, u32[]{:S(2)}) collective-permute-start(bf16[8,128,128]{2,1,0:T(8,128)(2,1)S(1)} %pad_maximum_fusion.1), channel_id=1, source_target_pairs={{0,128},{1,129},{2,130},{3,131},{4,132},{5,133},{6,134},{7,135},{8... | collective-permute-start | bytes 786440 | tf_op jit(solution)/shard_map/ppermute | solution.py:32
  17.1 10.9 %collective-permute-start.4 = (bf16[8,128,128]{2,1,0:T(8,128)(2,1)S(1)}, bf16[8,128,128]{2,1,0:T(8,128)(2,1)S(1)}, u32[]{:S(2)}, u32[]{:S(2)}) collective-permute-start(bf16[8,128,128]{2,1,0:T(8,128)(2,1)S(1)} %pad_maximum_fusion.1), channel_id=1, source_target_pairs={{0,6},{1,25},{2,0},{3,27},{4,2},{5,29},{6,4},{7,31},{8,14},{9,1},{... | collective-permute-start | bytes 786440 | tf_op jit(solution)/shard_map/ppermute | solution.py:32
  19.8 10.9 %collective-permute-start.3 = (bf16[8,128,128]{2,1,0:T(8,128)(2,1)S(1)}, bf16[8,128,128]{2,1,0:T(8,128)(2,1)S(1)}, u32[]{:S(2)}, u32[]{:S(2)}) collective-permute-start(bf16[8,128,128]{2,1,0:T(8,128)(2,1)S(1)} %pad_maximum_fusion.1), channel_id=1, source_target_pairs={{0,2},{1,9},{2,4},{3,11},{4,6},{5,13},{6,0},{7,15},{8,10},{9,17},{... | collective-permute-start | bytes 786440 | tf_op jit(solution)/shard_map/ppermute | solution.py:32
  22.4 5.5 %copy-start.1 = (bf16[16,128,128]{2,1,0:T(8,128)(2,1)}, bf16[16,128,128]{2,1,0:T(8,128)(2,1)S(1)}, u32[]{:S(2)}) copy-start(bf16[16,128,128]{2,1,0:T(8,128)(2,1)S(1)} %gather_fusion.6) | copy-start | bytes 1572868
  28.0 12.5 %collective-permute-start.6 = (bf16[4,128,128]{2,1,0:T(8,128)(2,1)S(1)}, bf16[4,128,128]{2,1,0:T(8,128)(2,1)S(1)}, u32[]{:S(2)}, u32[]{:S(2)}) collective-permute-start(bf16[4,128,128]{2,1,0:T(8,128)(2,1)S(1)} %slice.161), channel_id=1, source_target_pairs={{0,6},{1,25},{2,0},{3,27},{4,2},{5,29},{6,4},{7,31},{8,14},{9,1},{... | collective-permute-start | bytes 393224 | tf_op jit(solution)/shard_map/ppermute | solution.py:32
  30.7 5.4 %collective-permute-start.5 = (bf16[4,128,128]{2,1,0:T(8,128)(2,1)S(1)}, bf16[4,128,128]{2,1,0:T(8,128)(2,1)S(1)}, u32[]{:S(2)}, u32[]{:S(2)}) collective-permute-start(bf16[4,128,128]{2,1,0:T(8,128)(2,1)S(1)} %slice.160), channel_id=1, source_target_pairs={{0,2},{1,9},{2,4},{3,11},{4,6},{5,13},{6,0},{7,15},{8,10},{9,17},{... | collective-permute-start | bytes 393224 | tf_op jit(solution)/shard_map/ppermute | solution.py:32
  30.8 10.3 %collective-permute-start.13 = (bf16[8,128,128]{2,1,0:T(8,128)(2,1)S(1)}, bf16[8,128,128]{2,1,0:T(8,128)(2,1)S(1)}, u32[]{:S(2)}, u32[]{:S(2)}) collective-permute-start(bf16[8,128,128]{2,1,0:T(8,128)(2,1)S(1)} %collective-permute-done.11), channel_id=1, source_target_pairs={{0,24},{1,7},{2,26},{3,1},{4,28},{5,3},{6,30},{7,5},{8,0},{9,15},{... | collective-permute-start | bytes 786440 | tf_op jit(solution)/shard_map/ppermute | solution.py:32
  33.4 10.4 %collective-permute-start.12 = (bf16[8,128,128]{2,1,0:T(8,128)(2,1)S(1)}, bf16[8,128,128]{2,1,0:T(8,128)(2,1)S(1)}, u32[]{:S(2)}, u32[]{:S(2)}) collective-permute-start(bf16[8,128,128]{2,1,0:T(8,128)(2,1)S(1)} %collective-permute-done.11), channel_id=1, source_target_pairs={{0,8},{1,3},{2,10},{3,5},{4,12},{5,7},{6,14},{7,1},{8,16},{9,11},{... | collective-permute-start | bytes 786440 | tf_op jit(solution)/shard_map/ppermute | solution.py:32
  35.6 30.0 %slice-start = ((bf16[16,128,128]{2,1,0:T(8,128)(2,1)}), bf16[8,128,128]{2,1,0:T(8,128)(2,1)S(1)}, s32[]{:S(2)}) async-start(bf16[16,128,128]{2,1,0:T(8,128)(2,1)} %copy-done.1), calls=%async_computation | async-start | bytes 524288 | tf_op jit(solution)/shard_map/slice | solution.py:191
  36.1 17.4 %collective-permute-start.22 = (bf16[16,128,128]{2,1,0:T(8,128)(2,1)}, bf16[16,128,128]{2,1,0:T(8,128)(2,1)}, u32[]{:S(2)}, u32[]{:S(2)}) collective-permute-start(bf16[16,128,128]{2,1,0:T(8,128)(2,1)} %gather_fusion.11), channel_id=1, source_target_pairs={{0,32},{1,225},{2,34},{3,227},{4,36},{5,229},{6,38},{7,231},{8,40}... | collective-permute-start | bytes 1572872 | tf_op jit(solution)/shard_map/ppermute | solution.py:32
  40.5 15.9 %collective-permute-start.20 = (bf16[16,128,128]{2,1,0:T(8,128)(2,1)}, bf16[16,128,128]{2,1,0:T(8,128)(2,1)}, u32[]{:S(2)}, u32[]{:S(2)}) collective-permute-start(bf16[16,128,128]{2,1,0:T(8,128)(2,1)} %gather_fusion.5), channel_id=1, source_target_pairs={{0,224},{1,33},{2,226},{3,35},{4,228},{5,37},{6,230},{7,39},{8,232... | collective-permute-start | bytes 1572872 | tf_op jit(solution)/shard_map/ppermute | solution.py:32
  41.2 10.2 %collective-permute-start.15 = (bf16[4,128,128]{2,1,0:T(8,128)(2,1)S(1)}, bf16[4,128,128]{2,1,0:T(8,128)(2,1)S(1)}, u32[]{:S(2)}, u32[]{:S(2)}) collective-permute-start(bf16[4,128,128]{2,1,0:T(8,128)(2,1)S(1)} %slice.165), channel_id=1, source_target_pairs={{0,24},{1,7},{2,26},{3,1},{4,28},{5,3},{6,30},{7,5},{8,0},{9,15},{... | collective-permute-start | bytes 393224 | tf_op jit(solution)/shard_map/ppermute | solution.py:32
  43.8 5.5 %collective-permute-start.14 = (bf16[4,128,128]{2,1,0:T(8,128)(2,1)S(1)}, bf16[4,128,128]{2,1,0:T(8,128)(2,1)S(1)}, u32[]{:S(2)}, u32[]{:S(2)}) collective-permute-start(bf16[4,128,128]{2,1,0:T(8,128)(2,1)S(1)} %slice.164), channel_id=1, source_target_pairs={{0,8},{1,3},{2,10},{3,5},{4,12},{5,7},{6,14},{7,1},{8,16},{9,11},{... | collective-permute-start | bytes 393224 | tf_op jit(solution)/shard_map/ppermute | solution.py:32
  49.3 15.4 %collective-permute-start.21 = (bf16[16,128,128]{2,1,0:T(8,128)(2,1)}, bf16[16,128,128]{2,1,0:T(8,128)(2,1)}, u32[]{:S(2)}, u32[]{:S(2)}) collective-permute-start(bf16[16,128,128]{2,1,0:T(8,128)(2,1)} %gather_fusion.10), channel_id=1, source_target_pairs={{0,64},{1,193},{2,66},{3,195},{4,68},{5,197},{6,70},{7,199},{8,72}... | collective-permute-start | bytes 1572872 | tf_op jit(solution)/shard_map/ppermute | solution.py:32
  51.4 21.6 %collective-permute-start.8 = (bf16[32,128,128]{2,1,0:T(8,128)(2,1)}, bf16[32,128,128]{2,1,0:T(8,128)(2,1)S(1)}, u32[]{:S(2)}, u32[]{:S(2)}) collective-permute-start(bf16[32,128,128]{2,1,0:T(8,128)(2,1)} %constant_dynamic-update-slice_fusion.refs_0_), channel_id=1, source_target_pairs={{0,24},{1,7},{2,26},{3,1},{4,28},{5,3},{6,30},{7,5},{8,0},{9,15},{... | collective-permute-start | bytes 3145736 | tf_op jit(solution)/shard_map/ppermute | solution.py:32
  52.0 22.7 %collective-permute-start.7 = (bf16[32,128,128]{2,1,0:T(8,128)(2,1)}, bf16[32,128,128]{2,1,0:T(8,128)(2,1)S(1)}, u32[]{:S(2)}, u32[]{:S(2)}) collective-permute-start(bf16[32,128,128]{2,1,0:T(8,128)(2,1)} %constant_dynamic-update-slice_fusion.refs_0_), channel_id=1, source_target_pairs={{0,8},{1,3},{2,10},{3,5},{4,12},{5,7},{6,14},{7,1},{8,16},{9,11},{... | collective-permute-start | bytes 3145736 | tf_op jit(solution)/shard_map/ppermute | solution.py:32
  53.5 25.5 %collective-permute-start.17 = (bf16[32,128,128]{2,1,0:T(8,128)(2,1)}, bf16[32,128,128]{2,1,0:T(8,128)(2,1)}, u32[]{:S(2)}, u32[]{:S(2)}) collective-permute-start(bf16[32,128,128]{2,1,0:T(8,128)(2,1)} %constant_dynamic-update-slice_fusion.6.refs_5_), channel_id=1, source_target_pairs={{0,6},{1,25},{2,0},{3,27},{4,2},{5,29},{6,4},{7,31},{8,14},{9,1},{... | collective-permute-start | bytes 3145736 | tf_op jit(solution)/shard_map/ppermute | solution.py:32
  56.3 28.0 %collective-permute-start.16 = (bf16[32,128,128]{2,1,0:T(8,128)(2,1)}, bf16[32,128,128]{2,1,0:T(8,128)(2,1)}, u32[]{:S(2)}, u32[]{:S(2)}) collective-permute-start(bf16[32,128,128]{2,1,0:T(8,128)(2,1)} %constant_dynamic-update-slice_fusion.6.refs_5_), channel_id=1, source_target_pairs={{0,2},{1,9},{2,4},{3,11},{4,6},{5,13},{6,0},{7,15},{8,10},{9,17},{... | collective-permute-start | bytes 3145736 | tf_op jit(solution)/shard_map/ppermute | solution.py:32
  66.8 22.9 %collective-permute-start.23 = (bf16[32,128,128]{2,1,0:T(8,128)(2,1)}, bf16[32,128,128]{2,1,0:T(8,128)(2,1)}, u32[]{:S(2)}, u32[]{:S(2)}) collective-permute-start(bf16[32,128,128]{2,1,0:T(8,128)(2,1)} %pad_maximum_fusion), channel_id=1, source_target_pairs={{0,1},{1,0},{2,3},{3,2},{4,5},{5,4},{6,7},{7,6},{8,9},{9,8},{10,11... | collective-permute-start | bytes 3145736 | tf_op jit(solution)/shard_map/ppermute | solution.py:32
  73.9 15.8 %collective-permute-start.10 = (bf16[16,128,128]{2,1,0:T(8,128)(2,1)}, bf16[16,128,128]{2,1,0:T(8,128)(2,1)}, u32[]{:S(2)}, u32[]{:S(2)}) collective-permute-start(bf16[16,128,128]{2,1,0:T(8,128)(2,1)} %slice.163), channel_id=1, source_target_pairs={{0,24},{1,7},{2,26},{3,1},{4,28},{5,3},{6,30},{7,5},{8,0},{9,15},{... | collective-permute-start | bytes 1572872 | tf_op jit(solution)/shard_map/ppermute | solution.py:32
  75.6 14.1 %collective-permute-start.9 = (bf16[16,128,128]{2,1,0:T(8,128)(2,1)}, bf16[16,128,128]{2,1,0:T(8,128)(2,1)}, u32[]{:S(2)}, u32[]{:S(2)}) collective-permute-start(bf16[16,128,128]{2,1,0:T(8,128)(2,1)} %slice.162), channel_id=1, source_target_pairs={{0,8},{1,3},{2,10},{3,5},{4,12},{5,7},{6,14},{7,1},{8,16},{9,11},{... | collective-permute-start | bytes 1572872 | tf_op jit(solution)/shard_map/ppermute | solution.py:32
  80.9 14.6 %collective-permute-start.19 = (bf16[16,128,128]{2,1,0:T(8,128)(2,1)}, bf16[16,128,128]{2,1,0:T(8,128)(2,1)}, u32[]{:S(2)}, u32[]{:S(2)}) collective-permute-start(bf16[16,128,128]{2,1,0:T(8,128)(2,1)} %slice.167), channel_id=1, source_target_pairs={{0,6},{1,25},{2,0},{3,27},{4,2},{5,29},{6,4},{7,31},{8,14},{9,1},{... | collective-permute-start | bytes 1572872 | tf_op jit(solution)/shard_map/ppermute | solution.py:32
  86.2 13.9 %collective-permute-start.18 = (bf16[16,128,128]{2,1,0:T(8,128)(2,1)}, bf16[16,128,128]{2,1,0:T(8,128)(2,1)}, u32[]{:S(2)}, u32[]{:S(2)}) collective-permute-start(bf16[16,128,128]{2,1,0:T(8,128)(2,1)} %slice.166), channel_id=1, source_target_pairs={{0,2},{1,9},{2,4},{3,11},{4,6},{5,13},{6,0},{7,15},{8,10},{9,17},{... | collective-permute-start | bytes 1572872 | tf_op jit(solution)/shard_map/ppermute | solution.py:32
  115.1 25.6 %collective-permute-start.24 = (bf16[3,32,128,128]{3,2,1,0:T(8,128)(2,1)}, bf16[3,32,128,128]{3,2,1,0:T(8,128)(2,1)}, u32[]{:S(2)}, u32[]{:S(2)}) collective-permute-start(bf16[3,32,128,128]{3,2,1,0:T(8,128)(2,1)} %shard_map.100), channel_id=1, source_target_pairs={{0,1},{1,0},{2,3},{3,2},{4,5},{5,4},{6,7},{7,6},{8,9},{9,8},{10,11... | collective-permute-start | bytes 9437192 | tf_op jit(solution)/shard_map/ppermute | solution.py:32
  125.8 3.1 %collective-permute-start.26 = (bf16[1,32,128,128]{3,2,1,0:T(8,128)(2,1)}, bf16[1,32,128,128]{3,2,1,0:T(8,128)(2,1)}, u32[]{:S(2)}, u32[]{:S(2)}) collective-permute-start(bf16[1,32,128,128]{3,2,1,0:T(8,128)(2,1)} %shard_map.102), channel_id=1, source_target_pairs={{0,1},{1,0},{2,3},{3,2},{4,5},{5,4},{6,7},{7,6},{8,9},{9,8},{10,11... | collective-permute-start | bytes 3145736 | tf_op jit(solution)/shard_map/ppermute | solution.py:32
  128.9 9.8 %copy-start.3 = (s32[2]{0:T(128)S(1)}, s32[2]{0:T(128)}, u32[]{:S(2)}) copy-start(s32[2]{0:T(128)} %constant.493) | copy-start | bytes 28
  138.4 18.8 %collective-permute-start.27 = (bf16[1,32,128,128]{3,2,1,0:T(8,128)(2,1)}, bf16[1,32,128,128]{3,2,1,0:T(8,128)(2,1)}, u32[]{:S(2)}, u32[]{:S(2)}) collective-permute-start(bf16[1,32,128,128]{3,2,1,0:T(8,128)(2,1)} %shard_map.103), channel_id=1, source_target_pairs={{0,224},{1,33},{2,226},{3,35},{4,228},{5,37},{6,230},{7,39},{8,232... | collective-permute-start | bytes 3145736 | tf_op jit(solution)/shard_map/ppermute | solution.py:32
  140.7 1.9 %copy-start.2 = (bf16[16,128,128]{2,1,0:T(8,128)(2,1)S(1)}, bf16[16,128,128]{2,1,0:T(8,128)(2,1)}, u32[]{:S(2)}) copy-start(bf16[16,128,128]{2,1,0:T(8,128)(2,1)} %copy-done.1) | copy-start | bytes 1572868
  152.4 15.2 %collective-permute-start.25 = (bf16[1,32,128,128]{3,2,1,0:T(8,128)(2,1)S(1)}, bf16[1,32,128,128]{3,2,1,0:T(8,128)(2,1)S(1)}, u32[]{:S(2)}, u32[]{:S(2)}) collective-permute-start(bf16[1,32,128,128]{3,2,1,0:T(8,128)(2,1)S(1)} %slice.174), channel_id=1, source_target_pairs={{0,32},{1,225},{2,34},{3,227},{4,36},{5,229},{6,38},{7,231},{8,40}... | collective-permute-start | bytes 3145736 | tf_op jit(solution)/shard_map/ppermute | solution.py:32
  165.3 15.3 %collective-permute-start.28 = (bf16[1,32,128,128]{3,2,1,0:T(8,128)(2,1)S(1)}, bf16[1,32,128,128]{3,2,1,0:T(8,128)(2,1)S(1)}, u32[]{:S(2)}, u32[]{:S(2)}) collective-permute-start(bf16[1,32,128,128]{3,2,1,0:T(8,128)(2,1)S(1)} %shard_map.104), channel_id=1, source_target_pairs={{0,224},{1,33},{2,226},{3,35},{4,228},{5,37},{6,230},{7,39},{8,232... | collective-permute-start | bytes 3145736 | tf_op jit(solution)/shard_map/ppermute | solution.py:32

commit v2 on v0

v2 whole, which is shorter than its diff:
```python
import functools

import jax
import jax.numpy as jnp
from jax import lax
from jax.experimental import pallas as pl
from jax.experimental.pallas import tpu as pltpu
from jax.sharding import PartitionSpec as P

BLK = 128
NZ, NY, NX, NC = 8, 4, 4, 2
KEPT = 32
ROWS = 8
SEL = 16
SET = 256
AXES = ("row", "col")
OFFSETS = (2, 1, -1, 0)


def send(block, target):
    pairs = []
    for z in range(NZ):
        for y in range(NY):
            for x in range(NX):
                for c in range(NC):
                    tz, ty, tx, tc = target(z, y, x, c)
                    tz, ty, tx = tz % NZ, ty % NY, tx % NX
                    src = ((z * NY + y) * NX + x) * NC + c
                    dst = ((tz * NY + ty) * NX + tx) * NC + tc
                    pairs.append((src, dst))
    return lax.ppermute(block, AXES, pairs)


def swap(block):
    return send(block, lambda z, y, x, c: (z, y, x, 1 - c))


def along_z(block, distance):
    return send(block, lambda z, y, x, c: (z + distance * (1 - 2 * c), y, x, c))


def in_plane(block, distance, flip):
    def target(z, y, x, c):
        if c ^ flip:
            return (z, y + distance, x, c)
        return (z, y, x + distance, c)

    return send(block, target)


def pack_kernel(size, starts_ref, *refs):
    parts, out_ref = refs[:-1], refs[-1]
    for n, ref in enumerate(parts):
        for i in range(size):
            out_ref[n * size + i] = ref[starts_ref[n] + i]


def pack(parts, size, starts=None):
    if starts is None:
        starts = jnp.zeros((len(parts),), jnp.int32)
    total = size * len(parts)
    vmem = pl.BlockSpec(memory_space=pltpu.VMEM)
    return pl.pallas_call(
        functools.partial(pack_kernel, size),
        out_shape=jax.ShapeDtypeStruct((total, BLK, BLK), jnp.bfloat16),
        in_specs=[pl.BlockSpec(memory_space=pltpu.SMEM)] + [vmem] * len(parts),
        out_specs=vmem,
        compiler_params=pltpu.CompilerParams(vmem_limit_bytes=8 * 1024 * 1024),
        cost_estimate=pl.CostEstimate(
            flops=0, bytes_accessed=4 * total * BLK * BLK, transcendentals=0
        ),
        name="pack",
    )(starts, *parts)


def pick_kernel(at_ref, blocks_ref, *outs):
    for n, out in enumerate(outs):
        for i in range(SEL):
            out[i] = blocks_ref[at_ref[n * SEL + i]]


def pick(blocks, at):
    n = len(OFFSETS)
    vmem = pl.BlockSpec(memory_space=pltpu.VMEM)
    return pl.pallas_call(
        pick_kernel,
        out_shape=[jax.ShapeDtypeStruct((SEL, BLK, BLK), jnp.bfloat16)] * n,
        in_specs=[pl.BlockSpec(memory_space=pltpu.SMEM), vmem],
        out_specs=[vmem] * n,
        compiler_params=pltpu.CompilerParams(vmem_limit_bytes=8 * 1024 * 1024),
        cost_estimate=pl.CostEstimate(
            flops=0, bytes_accessed=4 * n * SEL * BLK * BLK, transcendentals=0
        ),
        name="pick",
    )(at, blocks)


def products_kernel(n_panel, n_left, base, n_add, idx_ref, order_ref, count_ref, *refs):
    panel_refs, refs = refs[:n_panel], refs[n_panel:]
    left_refs, refs = refs[:n_left], refs[n_left:]
    add_ref = refs[0] if n_add else None
    out_ref, panel, lefts, panel_sem, left_sem = refs[n_add:]
    copies = []
    at = 0
    for n, ref in enumerate(panel_refs):
        size = ref.shape[0]
        copies.append(pltpu.make_async_copy(ref, panel.at[pl.ds(at, size)], panel_sem.at[n]))
        at += size
    for r, ref in enumerate(left_refs):
        copies.append(
            pltpu.make_async_copy(ref.at[pl.ds(base, ROWS)], lefts.at[r], left_sem.at[r])
        )
    for copy in copies:
        copy.start()
    panel[SET] = jnp.zeros((BLK, BLK), panel.dtype)
    for copy in copies:
        copy.wait()

    def row(r, carry):
        pairs_here = (count_ref[r] + 1) // 2
        for pairs in range(ROWS // 2 + 1):

            @pl.when(pairs_here == pairs)
            def _(pairs=pairs):
                def step(sp, inner):
                    s0 = 2 * sp
                    if pairs:
                        strips = []
                        for t in range(2 * pairs):
                            spot = (r * ROWS + t) * KEPT + s0
                            strips.append(
                                jnp.concatenate(
                                    [panel[idx_ref[spot]], panel[idx_ref[spot + 1]]], axis=1
                                )
                            )
                        lhs = jnp.concatenate(
                            [lefts[r, order_ref[r * ROWS + t]] for t in range(2 * pairs)], axis=1
                        )
                        total = jnp.dot(
                            lhs,
                            jnp.concatenate(strips, axis=0),
                            preferred_element_type=jnp.float32,
                        )
                    else:
                        total = jnp.zeros((BLK, 2 * BLK), jnp.float32)
                    both = [total[:, :BLK], total[:, BLK:]]
                    for k in range(2):
                        if n_add:
                            both[k] = both[k] + add_ref[r, s0 + k].astype(jnp.float32)
                        out_ref[r, s0 + k] = both[k].astype(out_ref.dtype)
                    return inner

                lax.fori_loop(0, KEPT // 2, step, 0, unroll=8)

        return carry

    lax.fori_loop(0, n_left, row, 0)


def products(table, panel_parts, lefts, base, add=None):
    n = len(lefts)
    adds = () if add is None else (add,)
    smem = pl.BlockSpec(memory_space=pltpu.SMEM)
    hbm = pl.BlockSpec(memory_space=pl.ANY)
    vmem = pl.BlockSpec(memory_space=pltpu.VMEM)
    return pl.pallas_call(
        functools.partial(products_kernel, len(panel_parts), n, base, len(adds)),
        out_shape=jax.ShapeDtypeStruct((n, KEPT, BLK, BLK), jnp.bfloat16),
        in_specs=[smem] * 3
        + [pl.BlockSpec(memory_space=pltpu.HBM)]
        + [hbm] * (len(panel_parts) - 1 + n)
        + [vmem] * len(adds),
        out_specs=vmem,
        scratch_shapes=[
            pltpu.VMEM((SET + 1, BLK, BLK), jnp.bfloat16),
            pltpu.VMEM((n, ROWS, BLK, BLK), jnp.bfloat16),
            pltpu.SemaphoreType.DMA((len(panel_parts),)),
            pltpu.SemaphoreType.DMA((n,)),
        ],
        compiler_params=pltpu.CompilerParams(vmem_limit_bytes=24 * 1024 * 1024),
        cost_estimate=pl.CostEstimate(
            flops=n * KEPT * ROWS * 2 * BLK**3,
            bytes_accessed=8 * 1024 * 1024,
            transcendentals=0,
        ),
        name="products",
    )(*table, *(pltpu.with_memory_space_constraint(a, pltpu.HBM) for a in panel_parts[:1]), *panel_parts[1:], *lefts, *adds)


def plus_kernel(rows, *refs):
    out_ref = refs[-1]

    def step(i, carry):
        total = refs[0][rows[0], i].astype(jnp.float32)
        for row, ref in zip(rows[1:], refs[1:-1]):
            total = total + ref[row, i].astype(jnp.float32)
        out_ref[0, i] = total.astype(out_ref.dtype)
        return carry

    lax.fori_loop(0, KEPT, step, 0, unroll=4)


def plus(*terms):
    vmem = pl.BlockSpec(memory_space=pltpu.VMEM)
    return pl.pallas_call(
        functools.partial(plus_kernel, tuple(row for _, row in terms)),
        out_shape=jax.ShapeDtypeStruct((1, KEPT, BLK, BLK), jnp.bfloat16),
        in_specs=[vmem] * len(terms),
        out_specs=vmem,
        compiler_params=pltpu.CompilerParams(vmem_limit_bytes=16 * 1024 * 1024),
        cost_estimate=pl.CostEstimate(
            flops=0, bytes_accessed=(len(terms) + 1) * KEPT * BLK * BLK * 2, transcendentals=0
        ),
        name="plus",
    )(*(array for array, _ in terms))


def stage(*arrays):
    return lax.optimization_barrier(arrays)


def reached(z):
    j = jnp.arange(SEL, dtype=jnp.int32)
    return (z + NZ // 2 * (j // ROWS)) % NZ * ROWS + j % ROWS


def local(left_blocks, left_cols, reach_blocks, reach_cols):
    z = lax.axis_index("row")
    col = lax.axis_index("col")
    c = col % NC
    x = col // NC % NX
    y = col // (NC * NX)
    sign = 1 - 2 * c
    blocks = reach_blocks[:, 0]

    near_panel = lax.all_gather(blocks, "col", axis=0, tiled=True)

    own_left = left_blocks[0, 0]
    cols_here = left_cols[:, 0]
    own_cols = lax.dynamic_index_in_dim(cols_here, z, 0, keepdims=False)
    names = jnp.concatenate([reached(z + offset * sign + NZ) for offset in OFFSETS])
    picked_at = jnp.argmax(names[:, None] == own_cols[None, :], axis=1)

    far_l, near_l, leaf_l, own_l = pick(own_left, picked_at.astype(jnp.int32))
    far_set, far_l, near_l, leaf_l, own_l, reach_cols = stage(
        send(blocks, lambda z, y, x, c: (z + NZ // 2, y, x, c)),
        far_l,
        near_l,
        leaf_l,
        own_l,
        reach_cols,
    )
    ring = [in_plane(far_set, distance, 0) for distance in (1, -1, 2)]
    far_cols = send(reach_cols, lambda z, y, x, c: (z + NZ // 2, y, x, c))
    far_set, ring = stage(far_set, ring)
    far_l = along_z(far_l, 2)

    steps = jnp.array(OFFSETS, dtype=jnp.int32)
    cols = cols_here[(z - steps * sign + NZ) % NZ]
    slot = jnp.arange(KEPT, dtype=jnp.int32)

    def place(offset):
        offset = offset % 4
        return jnp.where(offset == 0, 0, jnp.where(offset == 3, 1, jnp.where(offset == 1, 2, 3)))

    dx = place(slot // NC % NX - x + NX)
    dy = place(slot // (NC * NX) - y + NY)
    first, then = jnp.where(slot % NC == 0, dx, dy), jnp.where(slot % NC == 0, dy, dx)
    far_place = jnp.where(slot % NC == c, 0, SET // 2) + then * 32 + first * 8
    j = jnp.arange(ROWS, dtype=jnp.int32)
    here = reached(z)

    def table(kept, places, names):
        place_of = places[None, :] + j[:, None]
        present = jnp.any(names[None, :, None] == cols[:, None, :], axis=2)
        rank = jnp.sum(present[:, None, :] & (j[None, None, :] < j[None, :, None]), axis=2)
        hit = present[:, None, :] & (rank[:, None, :] == j[None, :, None])
        order = jnp.sum(jnp.where(hit, j[None, None, :], 0), axis=2)
        same = kept[None, :, None, :] == cols[:, None, :, None]
        at = jnp.sum(jnp.where(same, place_of[None, :, None, :] - SET, 0), axis=3)
        idx = SET + jnp.sum(jnp.where(hit[:, :, :, None], at[:, None, :, :], 0), axis=2)
        return idx, order, jnp.sum(present.astype(jnp.int32), axis=1)

    def rows(tables, first, last):
        return tuple(t[first:last].reshape(-1) for t in tables)

    near_table = table(reach_cols, slot * ROWS, here[:ROWS])
    far_table = table(far_cols, far_place, here[ROWS:])
    tables = [rows(t, *span) for t in (near_table, far_table) for span in ((0, 1), (1, 4))]

    first = pack((far_set, *ring), ROWS)
    first, up, down, far_l, near_l, leaf_l, first_got, tables = stage(
        first,
        in_plane(first, 1, 1),
        in_plane(first, -1, 1),
        far_l,
        along_z(near_l, 1),
        along_z(leaf_l, -1),
        swap(first),
        tables,
    )
    half = 2 * ROWS
    last = (
        in_plane(pack((up,), half), 1, 1),
        in_plane(pack((down,), half, jnp.full((1,), half, jnp.int32)), -1, 1),
    )
    lefts = (near_l, leaf_l, own_l)
    near_far = products(tables[0], (near_panel,), (far_l,), 0)
    up_got, down_got, last, near_far = stage(swap(up), swap(down), last, near_far)
    own_parts = (first, up, down, *last)
    got_parts = (first_got, up_got, down_got, swap(last[0]), swap(last[1]))
    far_panel = (*own_parts, *got_parts)

    far_term = products(tables[2], far_panel, (far_l,), ROWS, near_far)
    far_got = along_z(far_term, -1)
    near_panel, far_term = stage(near_panel, far_term)
    near_rest = products(tables[1], (near_panel,), lefts, 0)
    terms = products(tables[3], far_panel, lefts, ROWS, near_rest)
    leaf_got = along_z(terms[1:2], 1)
    near_got = along_z(plus((terms, 0), (far_got, 0)), -1)
    return plus((terms, 2), (leaf_got, 0), (near_got, 0))[None]


def solution(mesh):
    in_specs = (
        P("row", "col", None, None, None),
        P(None, "col", None),
        P("row", "col", None, None),
        P("row", None),
    )
    out_specs = P("row", "col", None, None, None)
    return jax.shard_map(local, mesh=mesh, in_specs=in_specs, out_specs=out_specs, check_vma=False)
```

time: 573 us -> 144 us (0.25); the launches traced: 562 us -> 142 us
  local copies, waits for them, and re-layouts: 255 us -> 4.2 us
  waiting for transfers between devices: 226 us -> 45.4 us
  starting transfers between devices: 4.55 us -> 45.3 us
  matrix products: 38.6 us -> 0 us
  Pallas kernels: 0 us -> 29.9 us
  other arithmetic: 23.6 us -> 3.83 us
    gather x65 -> x1, local copies, waits for them, and re-layouts: 250 us -> 0.56 us  [local(): cols = cols_here[(z - steps * sign + NZ) % NZ]]
    reduce_scatter x1 -> x0, waiting for transfers between devices: 98.9 us -> none  [local(): lax.psum_scatter(partial_value.astype(jnp.float32).astype(jnp.bfloat16),...]
    ppermute x7 -> x20, waiting for transfers between devices: 126 us -> 41.9 us  [send(): return lax.ppermute(block, AXES, pairs)]
    ppermute x7 -> x20, starting transfers between devices: 4.51 us -> 45.3 us  [send(): return lax.ppermute(block, AXES, pairs)]
    dot_general x8 -> x0, matrix products: 38.6 us -> none  [slab_terms(): jnp.einsum('cxy,csyz->sxz', selected, chosen, preferred_element_type=jnp....]
    pallas_call x0 -> x10, Pallas kernels: none -> 29.9 us  [the longest x4 24.4 us: products(): pl.pallas_call(functools.partial(products_kernel, len(panel_parts), n, ba...]
    select_n x18 -> x1, other arithmetic: 8.5 us -> 0.67 us  [local(): cols = cols_here[(z - steps * sign + NZ) % NZ]]
    top_k x16 -> x0, other arithmetic: 7.56 us -> none  [pick_panel(): picked = lax.top_k(-order_key, CAP)[1]]
  transfers between devices with their start and end apart: 9 -> 21, of which waited for: 7 -> 9; matrix products, arithmetic and copies ran while one was open for 8% -> 4% of each run, Pallas kernels for 0% -> 17%
where the time goes in v2:
time: 144 us; the launch traced here: 142 us
  waiting for transfers between devices  45.4 us (32%)
  starting transfers between devices  45.3 us (31%)
  Pallas kernels  29.9 us (21%)
  between operations  13.7 us (10%)
  local copies, waits for them, and re-layouts  4.2 us (3%)
  other arithmetic  3.83 us (3%)
    ppermute x20, starting transfers between devices, send(): return lax.ppermute(block, AXES, pairs)  45.3 us
    ppermute x20, waiting for transfers between devices, send(): return lax.ppermute(block, AXES, pairs)  41.9 us
    pallas_call x4, Pallas kernels, products(): pl.pallas_call(functools.partial(products_kernel, len(panel_parts), n, ba...  24.4 us
  transfers between devices with their start and end apart: 21, of which 9 were waited for; matrix products, arithmetic and copies ran while one was open for 4% of the time, Pallas kernels for 17%

profile of v2, /device:TPU:1, one launch (start us, length us, event | category | flops | bytes accessed | tf_op | source)
XLA Modules:
  0.0 142.3 jit_solution(1701759180925286284)
XLA Ops:
  6.5 0.7 all-gather.3.cloned.1.call-update
  7.3 7.8 %collective-permute-start = (bf16[8,128,128]{2,1,0:T(8,128)(2,1)}, bf16[8,128,128]{2,1,0:T(8,128)(2,1)S(1)}, u32[]{:S(2)}, u32[]{:S(2)}) collective-permute-start(bf16[8,128,128]{2,1,0:T(8,128)(2,1)} %bitcast.19), channel_id=1, source_target_pairs={{0,128},{1,129},{2,130},{3,131},{4,132},{5,133},{6,134},{7,135},{8... | collective-permute-start | bytes 786440 | tf_op jit(solution)/shard_map/ppermute | solution.py:31
  15.1 0.7 compare_select_fusion
  15.8 0.6 gather_fusion
  16.6 0.3 compare_reduce_fusion
  16.9 0.2 convert_reduce_fusion
  17.1 0.2 select_reduce_fusion.4
  17.3 0.6 iota_reduce_fusion
  18.0 1.2 copy-done.4
  19.2 1.5 %pick.1 = (bf16[16,128,128]{2,1,0:T(8,128)(2,1)}, bf16[16,128,128]{2,1,0:T(8,128)(2,1)S(1)}, bf16[16,128,128]{2,1,0:T(8,128)(2,1)S(1)}, bf16[16,128,128]{2,1,0:T(8,128)(2,1)S(1)}) custom-call(s32[64]{0:T(128)S(1)} %get-tuple-element.45.at_ref, bf16[32,128,128]{2,1,0:T(8,128)(2,1)S(1)} %bitcast.14), custom_call_target="tpu_custom_call" | custom-call | bytes 4194304 | tf_op jit(solution)/shard_map/pick/pallas_call | solution.py:85
  20.7 0.8 copy-done.2
  21.5 0.8 copy-done.6
  22.3 3.0 %collective-permute-start.3 = (bf16[8,128,128]{2,1,0:T(8,128)(2,1)S(1)}, bf16[8,128,128]{2,1,0:T(8,128)(2,1)S(1)}, u32[]{:S(2)}, u32[]{:S(2)}) collective-permute-start(bf16[8,128,128]{2,1,0:T(8,128)(2,1)S(1)} %collective-permute-done.refs_0_), channel_id=1, source_target_pairs={{0,4},{1,17},{2,6},{3,19},{4,0},{5,21},{6,2},{7,23},{8,12},{9,25},... | collective-permute-start | bytes 786440 | tf_op jit(solution)/shard_map/ppermute | solution.py:31
  25.3 0.8 collective-permute-start.2
  26.1 0.7 collective-permute-start.1
  26.8 8.9 %collective-permute-start.6 = (bf16[16,128,128]{2,1,0:T(8,128)(2,1)}, bf16[16,128,128]{2,1,0:T(8,128)(2,1)}, u32[]{:S(2)}, u32[]{:S(2)}) collective-permute-start(bf16[16,128,128]{2,1,0:T(8,128)(2,1)} %get-tuple-element.55), channel_id=1, source_target_pairs={{0,64},{1,193},{2,66},{3,195},{4,68},{5,197},{6,70},{7,199},{8,72}... | collective-permute-start | bytes 1572872 | tf_op jit(solution)/shard_map/ppermute | solution.py:31
  35.7 0.6 pack.3.refs_0_
  36.3 1.5 %collective-permute-start.9 = (bf16[32,128,128]{2,1,0:T(8,128)(2,1)S(1)}, bf16[32,128,128]{2,1,0:T(8,128)(2,1)}, u32[]{:S(2)}, u32[]{:S(2)}) collective-permute-start(bf16[32,128,128]{2,1,0:T(8,128)(2,1)S(1)} %pack.3.refs_0_), channel_id=1, source_target_pairs={{0,1},{1,0},{2,3},{3,2},{4,5},{5,4},{6,7},{7,6},{8,9},{9,8},{10,11... | collective-permute-start | bytes 3145736 | tf_op jit(solution)/shard_map/ppermute | solution.py:31
  37.8 2.4 %collective-permute-start.5 = (bf16[32,128,128]{2,1,0:T(8,128)(2,1)S(1)}, bf16[32,128,128]{2,1,0:T(8,128)(2,1)S(1)}, u32[]{:S(2)}, u32[]{:S(2)}) collective-permute-start(bf16[32,128,128]{2,1,0:T(8,128)(2,1)S(1)} %pack.3.refs_0_), channel_id=1, source_target_pairs={{0,24},{1,7},{2,26},{3,1},{4,28},{5,3},{6,30},{7,5},{8,0},{9,15},{... | collective-permute-start | bytes 3145736 | tf_op jit(solution)/shard_map/ppermute | solution.py:31
  40.2 9.5 %collective-permute-start.10 = (s32[8,32]{1,0:T(8,128)S(1)}, s32[8,32]{1,0:T(8,128)S(1)}, u32[]{:S(2)}, u32[]{:S(2)}) collective-permute-start(s32[8,32]{1,0:T(8,128)S(1)} %copy-done.7), channel_id=1, source_target_pairs={{0,128},{1,129},{2,130},{3,131},{4,132},{5,133},{6,134},{7,135},{8... | collective-permute-start | bytes 3080 | tf_op jit(solution)/shard_map/ppermute | solution.py:31
  49.7 0.1 convert_reduce_fusion.2
  50.2 0.5 collective-permute-done.10
  50.7 1.8 %collective-permute-start.7 = (bf16[16,128,128]{2,1,0:T(8,128)(2,1)}, bf16[16,128,128]{2,1,0:T(8,128)(2,1)}, u32[]{:S(2)}, u32[]{:S(2)}) collective-permute-start(bf16[16,128,128]{2,1,0:T(8,128)(2,1)} %copy-done.6), channel_id=1, source_target_pairs={{0,32},{1,225},{2,34},{3,227},{4,36},{5,229},{6,38},{7,231},{8,40}... | collective-permute-start | bytes 1572872 | tf_op jit(solution)/shard_map/ppermute | solution.py:31
  52.5 1.2 select_reduce_fusion
  53.7 0.1 select_reduce_fusion.2
  54.0 0.1 select_reduce_fusion.3
  54.4 5.6 %collective-permute-done.7.refs_1_.refs_10_ = bf16[16,128,128]{2,1,0:T(8,128)(2,1)} collective-permute-done((bf16[16,128,128]{2,1,0:T(8,128)(2,1)}, bf16[16,128,128]{2,1,0:T(8,128)(2,1)}, u32[]{:S(2)}, u32[]{:S(2)}) %collective-permute-start.7) | collective-permute-done | bytes 524320 | tf_op jit(solution)/shard_map/ppermute | solution.py:31
  60.0 8.0 %collective-permute-done.8.refs_2_.refs_11_ = bf16[16,128,128]{2,1,0:T(8,128)(2,1)} collective-permute-done((bf16[16,128,128]{2,1,0:T(8,128)(2,1)}, bf16[16,128,128]{2,1,0:T(8,128)(2,1)}, u32[]{:S(2)}, u32[]{:S(2)}) %collective-permute-start.8) | collective-permute-done | bytes 524320 | tf_op jit(solution)/shard_map/ppermute | solution.py:31
  68.1 0.5 collective-permute-start.12
  68.6 0.8 pack.4
  69.4 0.8 pack.5
  70.3 2.6 %collective-permute-start.14 = (bf16[16,128,128]{2,1,0:T(8,128)(2,1)}, bf16[16,128,128]{2,1,0:T(8,128)(2,1)}, u32[]{:S(2)}, u32[]{:S(2)}) collective-permute-start(bf16[16,128,128]{2,1,0:T(8,128)(2,1)} %pack.5), channel_id=1, source_target_pairs={{0,24},{1,7},{2,26},{3,1},{4,28},{5,3},{6,30},{7,5},{8,0},{9,15},{... | collective-permute-start | bytes 1572872 | tf_op jit(solution)/shard_map/ppermute | solution.py:31
  72.9 2.8 %all-gather.3.cloned.1.call-done = bf16[256,1,128,128]{3,2,1,0:T(8,128)(2,1)} async-done(((bf16[8,1,128,128]{3,2,1,0:T(8,128)(2,1)}), bf16[256,1,128,128]{3,2,1,0:T(8,128)(2,1)}) %all-gather.3.cloned.1.call-update) | async-done | bytes 8388624 | tf_op jit(solution)/shard_map/all_gather | solution.py:236
  75.7 5.0 %products.4.refs_11_ = bf16[1,32,128,128]{3,2,1,0:T(8,128)(2,1)S(1)} custom-call(s32[256]{0:T(256)S(1)} %reshape.198.idx_ref, s32[8]{0:T(128)S(1)} %slice_bitcast_fusion.1.order_ref, s32[1]{0:T(128)S(1)} %bitcast.16, bf16[256,128,128]{2,1,0:T(8,128)(2,1)} %bitcast.17, bf16[16,128,128]{2,1,0:T(8,128)(2,1)} %collective-permute-done.6.refs_1_.refs_10_), custom_call_target="tpu_custom_call" | custom-call | flops 1073741824 | bytes 8388608 | tf_op jit(solution)/shard_map/products/pallas_call | solution.py:166
  80.7 2.0 %collective-permute-done.13.refs_3_ = bf16[16,128,128]{2,1,0:T(8,128)(2,1)} collective-permute-done((bf16[16,128,128]{2,1,0:T(8,128)(2,1)}, bf16[16,128,128]{2,1,0:T(8,128)(2,1)}, u32[]{:S(2)}, u32[]{:S(2)}) %collective-permute-start.13) | collective-permute-done | bytes 524320 | tf_op jit(solution)/shard_map/ppermute | solution.py:31
  82.8 1.5 %collective-permute-start.15 = (bf16[16,128,128]{2,1,0:T(8,128)(2,1)}, bf16[16,128,128]{2,1,0:T(8,128)(2,1)S(1)}, u32[]{:S(2)}, u32[]{:S(2)}) collective-permute-start(bf16[16,128,128]{2,1,0:T(8,128)(2,1)} %collective-permute-done.13.refs_3_), channel_id=1, source_target_pairs={{0,1},{1,0},{2,3},{3,2},{4,5},{5,4},{6,7},{7,6},{8,9},{9,8},{10,11... | collective-permute-start | bytes 1572872 | tf_op jit(solution)/shard_map/ppermute | solution.py:31
  84.3 1.7 %collective-permute-done.15.refs_8_ = bf16[16,128,128]{2,1,0:T(8,128)(2,1)S(1)} collective-permute-done((bf16[16,128,128]{2,1,0:T(8,128)(2,1)}, bf16[16,128,128]{2,1,0:T(8,128)(2,1)S(1)}, u32[]{:S(2)}, u32[]{:S(2)}) %collective-permute-start.15) | collective-permute-done | bytes 524320 | tf_op jit(solution)/shard_map/ppermute | solution.py:31
  86.0 0.7 collective-permute-done.16.refs_9_
  86.7 4.7 %products.5 = bf16[1,32,128,128]{3,2,1,0:T(8,128)(2,1)S(1)} custom-call(s32[256]{0:T(256)S(1)} %reshape.202.idx_ref, s32[8]{0:T(128)S(1)} %slice_bitcast_fusion.order_ref, s32[1]{0:T(128)S(1)} %bitcast.15, bf16[32,128,128]{2,1,0:T(8,128)(2,1)} %copy-done.1, bf16[32,128,128]{2,1,0:T(8,128)(2,1)S(1)} %collective-permute-done.4.refs_0_.refs_1_, ...), custom_call_target="tpu_custom_call" | custom-call | flops 1073741824 | bytes 8388608 | tf_op jit(solution)/shard_map/products/pallas_call | solution.py:166
  91.5 1.8 %collective-permute-start.18 = (bf16[1,32,128,128]{3,2,1,0:T(8,128)(2,1)S(1)}, bf16[1,32,128,128]{3,2,1,0:T(8,128)(2,1)S(1)}, u32[]{:S(2)}, u32[]{:S(2)}) collective-permute-start(bf16[1,32,128,128]{3,2,1,0:T(8,128)(2,1)S(1)} %products.5), channel_id=1, source_target_pairs={{0,224},{1,33},{2,226},{3,35},{4,228},{5,37},{6,230},{7,39},{8,232... | collective-permute-start | bytes 3145736 | tf_op jit(solution)/shard_map/ppermute | solution.py:31
  93.3 7.6 %products.6.refs_13_ = bf16[3,32,128,128]{3,2,1,0:T(8,128)(2,1)S(1)} custom-call(s32[768]{0:T(1024)S(1)} %reshape.200.idx_ref, s32[24]{0:T(128)S(1)} %reshape.201.order_ref, s32[3]{0:T(128)S(1)} %slice.51.count_ref, bf16[256,128,128]{2,1,0:T(8,128)(2,1)} %bitcast.18, bf16[16,128,128]{2,1,0:T(8,128)(2,1)} %collective-permute-done.7.refs_1_.refs_10_, ...), custom_call_target="tpu_custom_call" | custom-call | flops 3221225472 | bytes 8388608 | tf_op jit(solution)/shard_map/products/pallas_call | solution.py:166
  100.9 7.0 %products.7.refs_0_ = bf16[3,32,128,128]{3,2,1,0:T(8,128)(2,1)S(1)} custom-call(s32[768]{0:T(1024)S(1)} %reshape.204.idx_ref, s32[24]{0:T(128)S(1)} %reshape.205.order_ref, s32[3]{0:T(128)S(1)} %slice.58.count_ref, bf16[32,128,128]{2,1,0:T(8,128)(2,1)} %copy-done.1, bf16[32,128,128]{2,1,0:T(8,128)(2,1)S(1)} %collective-permute-done.4.refs_0_.refs_1_, ...), custom_call_target="tpu_custom_call" | custom-call | flops 3221225472 | bytes 8388608 | tf_op jit(solution)/shard_map/products/pallas_call | solution.py:166
  108.0 0.1 slice.66
  108.2 0.3 plus.2
  108.5 2.3 %collective-permute-start.19 = (bf16[1,32,128,128]{3,2,1,0:T(8,128)(2,1)S(1)}, bf16[1,32,128,128]{3,2,1,0:T(8,128)(2,1)S(1)}, u32[]{:S(2)}, u32[]{:S(2)}) collective-permute-start(bf16[1,32,128,128]{3,2,1,0:T(8,128)(2,1)S(1)} %plus.2), channel_id=1, source_target_pairs={{0,224},{1,33},{2,226},{3,35},{4,228},{5,37},{6,230},{7,39},{8,232... | collective-permute-start | bytes 3145736 | tf_op jit(solution)/shard_map/ppermute | solution.py:31
  110.7 20.7 %collective-permute-done.17.refs_1_ = bf16[1,32,128,128]{3,2,1,0:T(8,128)(2,1)S(1)} collective-permute-done((bf16[1,32,128,128]{3,2,1,0:T(8,128)(2,1)S(1)}, bf16[1,32,128,128]{3,2,1,0:T(8,128)(2,1)S(1)}, u32[]{:S(2)}, u32[]{:S(2)}) %collective-permute-start.17) | collective-permute-done | bytes 1048608 | tf_op jit(solution)/shard_map/ppermute | solution.py:31
  131.4 2.7 %collective-permute-done.19.refs_2_ = bf16[1,32,128,128]{3,2,1,0:T(8,128)(2,1)S(1)} collective-permute-done((bf16[1,32,128,128]{3,2,1,0:T(8,128)(2,1)S(1)}, bf16[1,32,128,128]{3,2,1,0:T(8,128)(2,1)S(1)}, u32[]{:S(2)}, u32[]{:S(2)}) %collective-permute-start.19) | collective-permute-done | bytes 1048608 | tf_op jit(solution)/shard_map/ppermute | solution.py:31
  134.1 1.4 plus.3
  (63 shorter events, 1.3 us)
Async XLA Ops:
  6.5 9.2 %copy-start = (s32[8,1,32]{2,1,0:T(1,128)S(1)}, s32[8,1,32]{2,1,0:T(1,128)}, u32[]{:S(2)}) copy-start(s32[8,1,32]{2,1,0:T(1,128)} %param.6) | copy-start | bytes 3076
  6.5 33.7 %copy-start.7 = (s32[8,32]{1,0:T(8,128)S(1)}, s32[8,32]{1,0:T(8,128)}, u32[]{:S(2)}) copy-start(s32[8,32]{1,0:T(8,128)} %param.8) | copy-start | bytes 3076
  6.5 69.1 %all-gather.3.cloned.1.call-start = ((), (), s32[]{:S(2)}) async-start(), calls=%async_computation | async-start | bytes 8650752 | tf_op jit(solution)/shard_map/all_gather | solution.py:236
  7.3 15.0 %collective-permute-start = (bf16[8,128,128]{2,1,0:T(8,128)(2,1)}, bf16[8,128,128]{2,1,0:T(8,128)(2,1)S(1)}, u32[]{:S(2)}, u32[]{:S(2)}) collective-permute-start(bf16[8,128,128]{2,1,0:T(8,128)(2,1)} %bitcast.19), channel_id=1, source_target_pairs={{0,128},{1,129},{2,130},{3,131},{4,132},{5,133},{6,134},{7,135},{8... | collective-permute-start | bytes 786440 | tf_op jit(solution)/shard_map/ppermute | solution.py:31
  18.0 1.2 copy-start.4
  20.7 0.8 copy-start.2
  21.5 0.8 copy-start.6
  22.3 27.6 %copy-start.5 = (bf16[16,128,128]{2,1,0:T(8,128)(2,1)}, bf16[16,128,128]{2,1,0:T(8,128)(2,1)S(1)}, u32[]{:S(2)}) copy-start(bf16[16,128,128]{2,1,0:T(8,128)(2,1)S(1)} %get-tuple-element.57) | copy-start | bytes 1572868
  22.3 13.4 %collective-permute-start.3 = (bf16[8,128,128]{2,1,0:T(8,128)(2,1)S(1)}, bf16[8,128,128]{2,1,0:T(8,128)(2,1)S(1)}, u32[]{:S(2)}, u32[]{:S(2)}) collective-permute-start(bf16[8,128,128]{2,1,0:T(8,128)(2,1)S(1)} %collective-permute-done.refs_0_), channel_id=1, source_target_pairs={{0,4},{1,17},{2,6},{3,19},{4,0},{5,21},{6,2},{7,23},{8,12},{9,25},... | collective-permute-start | bytes 786440 | tf_op jit(solution)/shard_map/ppermute | solution.py:31
  25.3 10.4 %collective-permute-start.2 = (bf16[8,128,128]{2,1,0:T(8,128)(2,1)S(1)}, bf16[8,128,128]{2,1,0:T(8,128)(2,1)S(1)}, u32[]{:S(2)}, u32[]{:S(2)}) collective-permute-start(bf16[8,128,128]{2,1,0:T(8,128)(2,1)S(1)} %collective-permute-done.refs_0_), channel_id=1, source_target_pairs={{0,6},{1,25},{2,0},{3,27},{4,2},{5,29},{6,4},{7,31},{8,14},{9,1},{... | collective-permute-start | bytes 786440 | tf_op jit(solution)/shard_map/ppermute | solution.py:31
  26.1 9.6 %collective-permute-start.1 = (bf16[8,128,128]{2,1,0:T(8,128)(2,1)S(1)}, bf16[8,128,128]{2,1,0:T(8,128)(2,1)S(1)}, u32[]{:S(2)}, u32[]{:S(2)}) collective-permute-start(bf16[8,128,128]{2,1,0:T(8,128)(2,1)S(1)} %collective-permute-done.refs_0_), channel_id=1, source_target_pairs={{0,2},{1,9},{2,4},{3,11},{4,6},{5,13},{6,0},{7,15},{8,10},{9,17},{... | collective-permute-start | bytes 786440 | tf_op jit(solution)/shard_map/ppermute | solution.py:31
  26.8 27.0 %collective-permute-start.6 = (bf16[16,128,128]{2,1,0:T(8,128)(2,1)}, bf16[16,128,128]{2,1,0:T(8,128)(2,1)}, u32[]{:S(2)}, u32[]{:S(2)}) collective-permute-start(bf16[16,128,128]{2,1,0:T(8,128)(2,1)} %get-tuple-element.55), channel_id=1, source_target_pairs={{0,64},{1,193},{2,66},{3,195},{4,68},{5,197},{6,70},{7,199},{8,72}... | collective-permute-start | bytes 1572872 | tf_op jit(solution)/shard_map/ppermute | solution.py:31
  36.3 44.4 %copy-start.1 = (bf16[32,128,128]{2,1,0:T(8,128)(2,1)}, bf16[32,128,128]{2,1,0:T(8,128)(2,1)S(1)}, u32[]{:S(2)}) copy-start(bf16[32,128,128]{2,1,0:T(8,128)(2,1)S(1)} %pack.3.refs_0_) | copy-start | bytes 3145732
  36.3 31.7 %collective-permute-start.9 = (bf16[32,128,128]{2,1,0:T(8,128)(2,1)S(1)}, bf16[32,128,128]{2,1,0:T(8,128)(2,1)}, u32[]{:S(2)}, u32[]{:S(2)}) collective-permute-start(bf16[32,128,128]{2,1,0:T(8,128)(2,1)S(1)} %pack.3.refs_0_), channel_id=1, source_target_pairs={{0,1},{1,0},{2,3},{3,2},{4,5},{5,4},{6,7},{7,6},{8,9},{9,8},{10,11... | collective-permute-start | bytes 3145736 | tf_op jit(solution)/shard_map/ppermute | solution.py:31
  37.8 30.1 %collective-permute-start.5 = (bf16[32,128,128]{2,1,0:T(8,128)(2,1)S(1)}, bf16[32,128,128]{2,1,0:T(8,128)(2,1)S(1)}, u32[]{:S(2)}, u32[]{:S(2)}) collective-permute-start(bf16[32,128,128]{2,1,0:T(8,128)(2,1)S(1)} %pack.3.refs_0_), channel_id=1, source_target_pairs={{0,24},{1,7},{2,26},{3,1},{4,28},{5,3},{6,30},{7,5},{8,0},{9,15},{... | collective-permute-start | bytes 3145736 | tf_op jit(solution)/shard_map/ppermute | solution.py:31
  40.2 27.8 %collective-permute-start.4 = (bf16[32,128,128]{2,1,0:T(8,128)(2,1)S(1)}, bf16[32,128,128]{2,1,0:T(8,128)(2,1)S(1)}, u32[]{:S(2)}, u32[]{:S(2)}) collective-permute-start(bf16[32,128,128]{2,1,0:T(8,128)(2,1)S(1)} %pack.3.refs_0_), channel_id=1, source_target_pairs={{0,8},{1,3},{2,10},{3,5},{4,12},{5,7},{6,14},{7,1},{8,16},{9,11},{... | collective-permute-start | bytes 3145736 | tf_op jit(solution)/shard_map/ppermute | solution.py:31
  40.2 10.5 %collective-permute-start.10 = (s32[8,32]{1,0:T(8,128)S(1)}, s32[8,32]{1,0:T(8,128)S(1)}, u32[]{:S(2)}, u32[]{:S(2)}) collective-permute-start(s32[8,32]{1,0:T(8,128)S(1)} %copy-done.7), channel_id=1, source_target_pairs={{0,128},{1,129},{2,130},{3,131},{4,132},{5,133},{6,134},{7,135},{8... | collective-permute-start | bytes 3080 | tf_op jit(solution)/shard_map/ppermute | solution.py:31
  50.7 9.3 %collective-permute-start.7 = (bf16[16,128,128]{2,1,0:T(8,128)(2,1)}, bf16[16,128,128]{2,1,0:T(8,128)(2,1)}, u32[]{:S(2)}, u32[]{:S(2)}) collective-permute-start(bf16[16,128,128]{2,1,0:T(8,128)(2,1)} %copy-done.6), channel_id=1, source_target_pairs={{0,32},{1,225},{2,34},{3,227},{4,36},{5,229},{6,38},{7,231},{8,40}... | collective-permute-start | bytes 1572872 | tf_op jit(solution)/shard_map/ppermute | solution.py:31
  53.8 14.1 %collective-permute-start.8 = (bf16[16,128,128]{2,1,0:T(8,128)(2,1)}, bf16[16,128,128]{2,1,0:T(8,128)(2,1)}, u32[]{:S(2)}, u32[]{:S(2)}) collective-permute-start(bf16[16,128,128]{2,1,0:T(8,128)(2,1)} %copy-done.5), channel_id=1, source_target_pairs={{0,224},{1,33},{2,226},{3,35},{4,228},{5,37},{6,230},{7,39},{8,232... | collective-permute-start | bytes 1572872 | tf_op jit(solution)/shard_map/ppermute | solution.py:31
  68.0 14.8 %collective-permute-start.11 = (bf16[32,128,128]{2,1,0:T(8,128)(2,1)S(1)}, bf16[32,128,128]{2,1,0:T(8,128)(2,1)}, u32[]{:S(2)}, u32[]{:S(2)}) collective-permute-start(bf16[32,128,128]{2,1,0:T(8,128)(2,1)S(1)} %collective-permute-done.4.refs_0_.refs_1_), channel_id=1, source_target_pairs={{0,1},{1,0},{2,3},{3,2},{4,5},{5,4},{6,7},{7,6},{8,9},{9,8},{10,11... | collective-permute-start | bytes 3145736 | tf_op jit(solution)/shard_map/ppermute | solution.py:31
  68.1 14.7 %collective-permute-start.12 = (bf16[32,128,128]{2,1,0:T(8,128)(2,1)S(1)}, bf16[32,128,128]{2,1,0:T(8,128)(2,1)}, u32[]{:S(2)}, u32[]{:S(2)}) collective-permute-start(bf16[32,128,128]{2,1,0:T(8,128)(2,1)S(1)} %collective-permute-done.5.refs_0_.refs_2_), channel_id=1, source_target_pairs={{0,1},{1,0},{2,3},{3,2},{4,5},{5,4},{6,7},{7,6},{8,9},{9,8},{10,11... | collective-permute-start | bytes 3145736 | tf_op jit(solution)/shard_map/ppermute | solution.py:31
  70.3 10.5 %collective-permute-start.14 = (bf16[16,128,128]{2,1,0:T(8,128)(2,1)}, bf16[16,128,128]{2,1,0:T(8,128)(2,1)}, u32[]{:S(2)}, u32[]{:S(2)}) collective-permute-start(bf16[16,128,128]{2,1,0:T(8,128)(2,1)} %pack.5), channel_id=1, source_target_pairs={{0,24},{1,7},{2,26},{3,1},{4,28},{5,3},{6,30},{7,5},{8,0},{9,15},{... | collective-permute-start | bytes 1572872 | tf_op jit(solution)/shard_map/ppermute | solution.py:31
  72.9 9.9 %collective-permute-start.13 = (bf16[16,128,128]{2,1,0:T(8,128)(2,1)}, bf16[16,128,128]{2,1,0:T(8,128)(2,1)}, u32[]{:S(2)}, u32[]{:S(2)}) collective-permute-start(bf16[16,128,128]{2,1,0:T(8,128)(2,1)} %pack.4), channel_id=1, source_target_pairs={{0,8},{1,3},{2,10},{3,5},{4,12},{5,7},{6,14},{7,1},{8,16},{9,11},{... | collective-permute-start | bytes 1572872 | tf_op jit(solution)/shard_map/ppermute | solution.py:31
  80.7 12.6 %copy-start.3 = (bf16[16,128,128]{2,1,0:T(8,128)(2,1)S(1)}, bf16[16,128,128]{2,1,0:T(8,128)(2,1)}, u32[]{:S(2)}) copy-start(bf16[16,128,128]{2,1,0:T(8,128)(2,1)} %copy-done.2) | copy-start | bytes 1572868
  82.8 3.2 %collective-permute-start.15 = (bf16[16,128,128]{2,1,0:T(8,128)(2,1)}, bf16[16,128,128]{2,1,0:T(8,128)(2,1)S(1)}, u32[]{:S(2)}, u32[]{:S(2)}) collective-permute-start(bf16[16,128,128]{2,1,0:T(8,128)(2,1)} %collective-permute-done.13.refs_3_), channel_id=1, source_target_pairs={{0,1},{1,0},{2,3},{3,2},{4,5},{5,4},{6,7},{7,6},{8,9},{9,8},{10,11... | collective-permute-start | bytes 1572872 | tf_op jit(solution)/shard_map/ppermute | solution.py:31
  84.2 2.5 %collective-permute-start.16 = (bf16[16,128,128]{2,1,0:T(8,128)(2,1)}, bf16[16,128,128]{2,1,0:T(8,128)(2,1)S(1)}, u32[]{:S(2)}, u32[]{:S(2)}) collective-permute-start(bf16[16,128,128]{2,1,0:T(8,128)(2,1)} %collective-permute-done.14.refs_4_), channel_id=1, source_target_pairs={{0,1},{1,0},{2,3},{3,2},{4,5},{5,4},{6,7},{7,6},{8,9},{9,8},{10,11... | collective-permute-start | bytes 1572872 | tf_op jit(solution)/shard_map/ppermute | solution.py:31
  91.5 16.7 %collective-permute-start.18 = (bf16[1,32,128,128]{3,2,1,0:T(8,128)(2,1)S(1)}, bf16[1,32,128,128]{3,2,1,0:T(8,128)(2,1)S(1)}, u32[]{:S(2)}, u32[]{:S(2)}) collective-permute-start(bf16[1,32,128,128]{3,2,1,0:T(8,128)(2,1)S(1)} %products.5), channel_id=1, source_target_pairs={{0,224},{1,33},{2,226},{3,35},{4,228},{5,37},{6,230},{7,39},{8,232... | collective-permute-start | bytes 3145736 | tf_op jit(solution)/shard_map/ppermute | solution.py:31
  108.1 23.3 %collective-permute-start.17 = (bf16[1,32,128,128]{3,2,1,0:T(8,128)(2,1)S(1)}, bf16[1,32,128,128]{3,2,1,0:T(8,128)(2,1)S(1)}, u32[]{:S(2)}, u32[]{:S(2)}) collective-permute-start(bf16[1,32,128,128]{3,2,1,0:T(8,128)(2,1)S(1)} %slice.66), channel_id=1, source_target_pairs={{0,32},{1,225},{2,34},{3,227},{4,36},{5,229},{6,38},{7,231},{8,40}... | collective-permute-start | bytes 3145736 | tf_op jit(solution)/shard_map/ppermute | solution.py:31
  108.5 25.6 %collective-permute-start.19 = (bf16[1,32,128,128]{3,2,1,0:T(8,128)(2,1)S(1)}, bf16[1,32,128,128]{3,2,1,0:T(8,128)(2,1)S(1)}, u32[]{:S(2)}, u32[]{:S(2)}) collective-permute-start(bf16[1,32,128,128]{3,2,1,0:T(8,128)(2,1)S(1)} %plus.2), channel_id=1, source_target_pairs={{0,224},{1,33},{2,226},{3,35},{4,228},{5,37},{6,230},{7,39},{8,232... | collective-permute-start | bytes 3145736 | tf_op jit(solution)/shard_map/ppermute | solution.py:31
Sparse Core Ops, SparseCore 0:
  9.9 65.7 all-gather.2

commit v3 on v2

v3 whole, which is shorter than its diff:
```python
import functools

import jax
import jax.numpy as jnp
from jax import lax
from jax.experimental import pallas as pl
from jax.experimental.pallas import tpu as pltpu
from jax.sharding import PartitionSpec as P

BLK = 128
NZ, NY, NX, NC = 8, 4, 4, 2
KEPT = 32
ROWS = 8
SEL = 16
SET = 512
AXES = ("row", "col")
OFFSETS = (2, 1, -1, 0)


def send(block, target):
    pairs = []
    for z in range(NZ):
        for y in range(NY):
            for x in range(NX):
                for c in range(NC):
                    tz, ty, tx, tc = target(z, y, x, c)
                    tz, ty, tx = tz % NZ, ty % NY, tx % NX
                    src = ((z * NY + y) * NX + x) * NC + c
                    dst = ((tz * NY + ty) * NX + tx) * NC + tc
                    pairs.append((src, dst))
    return lax.ppermute(block, AXES, pairs)


def swap(block):
    return send(block, lambda z, y, x, c: (z, y, x, 1 - c))


def along_z(block, distance):
    return send(block, lambda z, y, x, c: (z + distance * (1 - 2 * c), y, x, c))


def in_plane(block, distance, flip):
    def target(z, y, x, c):
        if c ^ flip:
            return (z, y + distance, x, c)
        return (z, y, x + distance, c)

    return send(block, target)


def join_kernel(*refs):
    parts, out_ref, sems = refs[:-2], refs[-2], refs[-1]
    copies = []
    at = 0
    for n, ref in enumerate(parts):
        size = ref.shape[0]
        copies.append(pltpu.make_async_copy(ref, out_ref.at[pl.ds(at, size)], sems.at[n]))
        at += size
    for copy in copies:
        copy.start()
    for copy in copies:
        copy.wait()


def join(parts, others):
    total = sum(part.shape[0] for part in parts + others)
    return pl.pallas_call(
        join_kernel,
        out_shape=jax.ShapeDtypeStruct((total, BLK, BLK), jnp.bfloat16),
        in_specs=[pl.BlockSpec(memory_space=pltpu.HBM)] * len(parts)
        + [pl.BlockSpec(memory_space=pl.ANY)] * len(others),
        out_specs=pl.BlockSpec(memory_space=pltpu.VMEM),
        scratch_shapes=[pltpu.SemaphoreType.DMA((len(parts + others),))],
        compiler_params=pltpu.CompilerParams(vmem_limit_bytes=4 * 1024 * 1024),
        cost_estimate=pl.CostEstimate(
            flops=0, bytes_accessed=4 * total * BLK * BLK, transcendentals=0
        ),
        name="join",
    )(*(pltpu.with_memory_space_constraint(part, pltpu.HBM) for part in parts), *others)


def halves_kernel(up_ref, down_ref, first_ref, second_ref, sems):
    half = first_ref.shape[0]
    copies = [
        pltpu.make_async_copy(up_ref.at[pl.ds(0, half)], first_ref, sems.at[0]),
        pltpu.make_async_copy(down_ref.at[pl.ds(half, half)], second_ref, sems.at[1]),
    ]
    for copy in copies:
        copy.start()
    for copy in copies:
        copy.wait()


def halves(up, down):
    half = up.shape[0] // 2
    hbm = pl.BlockSpec(memory_space=pl.ANY)
    return pl.pallas_call(
        halves_kernel,
        out_shape=[jax.ShapeDtypeStruct((half, BLK, BLK), jnp.bfloat16)] * 2,
        in_specs=[hbm] * 2,
        out_specs=[hbm] * 2,
        scratch_shapes=[pltpu.SemaphoreType.DMA((2,))],
        compiler_params=pltpu.CompilerParams(vmem_limit_bytes=1024 * 1024),
        cost_estimate=pl.CostEstimate(
            flops=0, bytes_accessed=8 * half * BLK * BLK, transcendentals=0
        ),
        name="halves",
    )(up, down)


def pick_kernel(at_ref, blocks_ref, *outs):
    for n, out in enumerate(outs):
        for i in range(SEL):
            out[i] = blocks_ref[at_ref[n * SEL + i]]


def pick(blocks, at):
    n = len(OFFSETS)
    vmem = pl.BlockSpec(memory_space=pltpu.VMEM)
    return pl.pallas_call(
        pick_kernel,
        out_shape=[jax.ShapeDtypeStruct((SEL, BLK, BLK), jnp.bfloat16)] * n,
        in_specs=[pl.BlockSpec(memory_space=pltpu.SMEM), vmem],
        out_specs=[vmem] * n,
        compiler_params=pltpu.CompilerParams(vmem_limit_bytes=8 * 1024 * 1024),
        cost_estimate=pl.CostEstimate(
            flops=0, bytes_accessed=4 * n * SEL * BLK * BLK, transcendentals=0
        ),
        name="pick",
    )(at, blocks)


def products_kernel(n_panel, n_left, n_add, idx_ref, order_ref, count_ref, *refs):
    panel_refs, refs = refs[:n_panel], refs[n_panel:]
    left_refs, refs = refs[:n_left], refs[n_left:]
    add_refs, out_refs = refs[:n_add], refs[n_add:-4]
    panel, lefts, panel_sem, left_sem = refs[-4:]
    copies = []
    at = 0
    for n, ref in enumerate(panel_refs):
        size = ref.shape[0]
        copies.append(pltpu.make_async_copy(ref, panel.at[pl.ds(at, size)], panel_sem.at[n]))
        at += size
    for r, ref in enumerate(left_refs):
        copies.append(pltpu.make_async_copy(ref, lefts.at[r], left_sem.at[r]))
    for copy in copies:
        copy.start()
    panel[at] = jnp.zeros((BLK, BLK), panel.dtype)
    for copy in copies:
        copy.wait()
    for r in range(n_left):
        pairs_here = (count_ref[r] + 1) // 2
        for pairs in range(SEL // 2 + 1):

            @pl.when(pairs_here == pairs)
            def _(r=r, pairs=pairs):
                def step(sp, inner):
                    s0 = 2 * sp
                    if pairs:
                        strips = []
                        for t in range(2 * pairs):
                            spot = (r * SEL + t) * KEPT + s0
                            strips.append(
                                jnp.concatenate(
                                    [panel[idx_ref[spot]], panel[idx_ref[spot + 1]]], axis=1
                                )
                            )
                        lhs = jnp.concatenate(
                            [lefts[r, order_ref[r * SEL + t]] for t in range(2 * pairs)], axis=1
                        )
                        total = jnp.dot(
                            lhs,
                            jnp.concatenate(strips, axis=0),
                            preferred_element_type=jnp.float32,
                        )
                    else:
                        total = jnp.zeros((BLK, 2 * BLK), jnp.float32)
                    both = [total[:, :BLK], total[:, BLK:]]
                    for k in range(2):
                        if n_add:
                            both[k] = both[k] + add_refs[r][0, s0 + k].astype(jnp.float32)
                        out_refs[r][0, s0 + k] = both[k].astype(jnp.bfloat16)
                    return inner

                lax.fori_loop(0, KEPT // 2, step, 0, unroll=4)


def products(table, panel_parts, lefts, adds=()):
    n = len(lefts)
    total = sum(part.shape[0] for part in panel_parts)
    smem = pl.BlockSpec(memory_space=pltpu.SMEM)
    hbm = pl.BlockSpec(memory_space=pl.ANY)
    vmem = pl.BlockSpec(memory_space=pltpu.VMEM)
    return pl.pallas_call(
        functools.partial(products_kernel, len(panel_parts), n, len(adds)),
        out_shape=[jax.ShapeDtypeStruct((1, KEPT, BLK, BLK), jnp.bfloat16)] * n,
        in_specs=[smem] * 3 + [hbm] * (len(panel_parts) + n) + [vmem] * len(adds),
        out_specs=[vmem] * n,
        scratch_shapes=[
            pltpu.VMEM((total + 1, BLK, BLK), jnp.bfloat16),
            pltpu.VMEM((n, SEL, BLK, BLK), jnp.bfloat16),
            pltpu.SemaphoreType.DMA((len(panel_parts),)),
            pltpu.SemaphoreType.DMA((n,)),
        ],
        compiler_params=pltpu.CompilerParams(vmem_limit_bytes=24 * 1024 * 1024),
        cost_estimate=pl.CostEstimate(
            flops=n * KEPT * SEL * 2 * BLK**3,
            bytes_accessed=total * BLK * BLK * 2,
            transcendentals=0,
        ),
        name="products",
    )(*table, *panel_parts, *lefts, *adds)


def plus_kernel(rows, *refs):
    out_ref = refs[-1]

    def step(i, carry):
        total = refs[0][rows[0], i].astype(jnp.float32)
        for row, ref in zip(rows[1:], refs[1:-1]):
            total = total + ref[row, i].astype(jnp.float32)
        out_ref[0, i] = total.astype(out_ref.dtype)
        return carry

    lax.fori_loop(0, KEPT, step, 0, unroll=4)


def plus(*terms):
    vmem = pl.BlockSpec(memory_space=pltpu.VMEM)
    return pl.pallas_call(
        functools.partial(plus_kernel, tuple(row for _, row in terms)),
        out_shape=jax.ShapeDtypeStruct((1, KEPT, BLK, BLK), jnp.bfloat16),
        in_specs=[vmem] * len(terms),
        out_specs=vmem,
        compiler_params=pltpu.CompilerParams(vmem_limit_bytes=16 * 1024 * 1024),
        cost_estimate=pl.CostEstimate(
            flops=0, bytes_accessed=(len(terms) + 1) * KEPT * BLK * BLK * 2, transcendentals=0
        ),
        name="plus",
    )(*(array for array, _ in terms))


def stage(*arrays):
    return lax.optimization_barrier(arrays)


def reached(z):
    j = jnp.arange(SEL, dtype=jnp.int32)
    return (z + NZ // 2 * (j // ROWS)) % NZ * ROWS + j % ROWS


def local(left_blocks, left_cols, reach_blocks, reach_cols):
    z = lax.axis_index("row")
    col = lax.axis_index("col")
    c = col % NC
    x = col // NC % NX
    y = col // (NC * NX)
    sign = 1 - 2 * c
    blocks = reach_blocks[:, 0]

    own_left = left_blocks[0, 0]
    cols_here = left_cols[:, 0]
    own_cols = lax.dynamic_index_in_dim(cols_here, z, 0, keepdims=False)
    names = jnp.concatenate([reached(z + offset * sign + NZ) for offset in OFFSETS])
    picked_at = jnp.argmax(names[:, None] == own_cols[None, :], axis=1)

    def round_one(block):
        return [in_plane(block, distance, 0) for distance in (1, -1, 2)]

    near_ring, picked, reach_cols, far_set = stage(
        round_one(blocks),
        pick(own_left, picked_at.astype(jnp.int32)),
        reach_cols,
        send(blocks, lambda z, y, x, c: (z + NZ // 2, y, x, c)),
    )
    far_l, near_l, leaf_l, own_l = picked
    far_l = along_z(far_l, 2)
    far_cols, far_ring, leaf_l = stage(
        send(reach_cols, lambda z, y, x, c: (z + NZ // 2, y, x, c)), round_one(far_set), leaf_l
    )
    first = join((blocks, *near_ring), (far_set, *far_ring))

    steps = jnp.array(OFFSETS, dtype=jnp.int32)
    cols = cols_here[(z - steps * sign + NZ) % NZ]
    slot = jnp.arange(KEPT, dtype=jnp.int32)

    def place(offset):
        offset = offset % 4
        return jnp.where(offset == 0, 0, jnp.where(offset == 3, 1, jnp.where(offset == 1, 2, 3)))

    dx = place(slot // NC % NX - x + NX)
    dy = place(slot // (NC * NX) - y + NY)
    then, ahead = jnp.where(slot % NC == 0, dy, dx), jnp.where(slot % NC == 0, dx, dy)
    turn = jnp.where(slot % NC == c, jnp.where(then == 3, 4, then), jnp.where(then == 0, 3, then + 4))
    near_place = turn * 64 + ahead * 8
    j = jnp.arange(SEL, dtype=jnp.int32)

    kept = jnp.concatenate([reach_cols, far_cols], axis=0)
    place_of = near_place[None, :] + (j // ROWS * 32 + j % ROWS)[:, None]
    present = jnp.any(reached(z)[None, :, None] == cols[:, None, :], axis=2)
    rank = jnp.sum(present[:, None, :] & (j[None, None, :] < j[None, :, None]), axis=2)
    hit = present[:, None, :] & (rank[:, None, :] == j[None, :, None])
    order = jnp.sum(jnp.where(hit, j[None, None, :], 0), axis=2)
    same = kept[None, :, None, :] == cols[:, None, :, None]
    at = jnp.sum(jnp.where(same, place_of[None, :, None, :] - SET, 0), axis=3)
    idx = SET + jnp.sum(jnp.where(hit[:, :, :, None], at[:, None, :, :], 0), axis=2)
    count = jnp.sum(present.astype(jnp.int32), axis=1)
    half = SET // 2
    idx_early = jnp.where(idx < half, idx, half)
    idx_late = jnp.where((idx >= half) & (idx < SET), idx - half, half)

    def entry(blocks_at, first, last):
        return tuple(t[first:last].reshape(-1) for t in (blocks_at, order, count))

    tables = entry(idx_early, 0, 1), entry(idx_late, 0, 1), entry(idx, 1, 3), entry(idx, 3, 4)

    tables, far_l, leaf_l, first_got, first, up, down, near_l = stage(
        tables,
        far_l,
        along_z(leaf_l, -1),
        swap(first),
        first,
        in_plane(first, 1, 1),
        in_plane(first, -1, 1),
        near_l,
    )
    near_half, far_half = halves(up, down)
    up, down, near_l, near_half, far_half = stage(up, down, near_l, near_half, far_half)
    early = (first, up, down, first_got)
    up_got, down_got, near_l, near_on, far_on, early_term = stage(
        swap(up),
        swap(down),
        along_z(near_l, 1),
        in_plane(near_half, 1, 1),
        in_plane(far_half, -1, 1),
        products(tables[0], early, (far_l,)),
    )
    late = (near_on, far_on, up_got, down_got, swap(near_on), swap(far_on))

    (far_term,) = products(tables[1], late, (far_l,), early_term)
    far_got = along_z(far_term, -1)
    near_l, leaf_l, far_term = stage(near_l, leaf_l, far_term)
    near_term, leaf_term = products(tables[2], early + late, (near_l, leaf_l))
    leaf_got = along_z(leaf_term, 1)
    near_got = along_z(plus((near_term, 0), (far_got, 0)), -1)
    own_l, leaf_term = stage(own_l, leaf_term)
    (own_term,) = products(tables[3], early + late, (own_l,))
    return plus((own_term, 0), (leaf_got, 0), (near_got, 0))[None]


def solution(mesh):
    in_specs = (
        P("row", "col", None, None, None),
        P(None, "col", None),
        P("row", "col", None, None),
        P("row", None),
    )
    out_specs = P("row", "col", None, None, None)
    return jax.shard_map(local, mesh=mesh, in_specs=in_specs, out_specs=out_specs, check_vma=False)
```

time: 144 us -> 134 us (0.931)
  between operations: 13.7 us -> 0.26 us
  local copies, waits for them, and re-layouts: 4.2 us -> 7.64 us
    ppermute x20 -> x23, waiting for transfers between devices: 41.9 us -> 45.4 us  [send(): return lax.ppermute(block, AXES, pairs)]
    unnamed x16 -> x24, local copies, waits for them, and re-layouts: 2.83 us -> 5.99 us
    all_gather x1 -> x0, waiting for transfers between devices: 2.78 us -> none  [local(): near_panel = lax.all_gather(blocks, 'col', axis=0, tiled=True)]
    pallas_call x7 -> x6, Pallas kernels: 26.7 us -> 28.9 us  [the longest x4 26 us: products(): pl.pallas_call(functools.partial(products_kernel, len(panel_parts), n, le...]
    ppermute x20 -> x23, starting transfers between devices: 45.3 us -> 45.4 us  [send(): return lax.ppermute(block, AXES, pairs)]
  transfers between devices with their start and end apart: 21 -> 23, of which waited for: 9 -> 11; matrix products, arithmetic and copies ran while one was open for 4% -> 4% of each run, Pallas kernels for 17% -> 17%
where the time goes in v3:
time: 134 us
  starting transfers between devices  45.4 us (34%)
  waiting for transfers between devices  45.4 us (34%)
  Pallas kernels  31.2 us (23%)
  local copies, waits for them, and re-layouts  7.64 us (6%)
  other arithmetic  3.63 us (3%)
    ppermute x23, starting transfers between devices, send(): return lax.ppermute(block, AXES, pairs)  45.4 us
    ppermute x23, waiting for transfers between devices, send(): return lax.ppermute(block, AXES, pairs)  45.4 us
    pallas_call x4, Pallas kernels, products(): pl.pallas_call(functools.partial(products_kernel, len(panel_parts), n, le...  26 us
    unnamed x24, local copies, waits for them, and re-layouts  5.99 us
  transfers between devices with their start and end apart: 23, of which 11 were waited for; matrix products, arithmetic and copies ran while one was open for 4% of the time, Pallas kernels for 17%

profile of v3, /device:TPU:1, one launch (start us, length us, event | category | flops | bytes accessed | tf_op | source)
XLA Modules:
  0.0 133.6 jit_solution(7001400602530254192)
XLA Ops:
  0.0 7.7 %collective-permute-start.3 = (bf16[8,128,128]{2,1,0:T(8,128)(2,1)}, bf16[8,128,128]{2,1,0:T(8,128)(2,1)S(1)}, u32[]{:S(2)}, u32[]{:S(2)}) collective-permute-start(bf16[8,128,128]{2,1,0:T(8,128)(2,1)} %bitcast.12), channel_id=1, source_target_pairs={{0,128},{1,129},{2,130},{3,131},{4,132},{5,133},{6,134},{7,135},{8... | collective-permute-start | bytes 786440 | tf_op jit(solution)/shard_map/ppermute | solution.py:31
  7.7 2.9 %collective-permute-start.2 = (bf16[8,128,128]{2,1,0:T(8,128)(2,1)}, bf16[8,128,128]{2,1,0:T(8,128)(2,1)S(1)}, u32[]{:S(2)}, u32[]{:S(2)}) collective-permute-start(bf16[8,128,128]{2,1,0:T(8,128)(2,1)} %bitcast.13), channel_id=1, source_target_pairs={{0,4},{1,17},{2,6},{3,19},{4,0},{5,21},{6,2},{7,23},{8,12},{9,25},... | collective-permute-start | bytes 786440 | tf_op jit(solution)/shard_map/ppermute | solution.py:31
  10.7 0.8 collective-permute-start.1
  11.4 0.7 collective-permute-start
  12.3 0.6 iota_reduce_fusion
  12.9 1.2 copy-done.1
  14.1 0.7 pick.1
  14.8 0.8 copy-done.4
  15.6 0.8 copy-done.6
  16.4 0.8 copy-done.7
  17.2 0.7 compare_select_fusion.2
  18.4 0.5 copy-done.9
  19.1 2.3 %collective-permute-start.7 = (bf16[8,128,128]{2,1,0:T(8,128)(2,1)S(1)}, bf16[8,128,128]{2,1,0:T(8,128)(2,1)S(1)}, u32[]{:S(2)}, u32[]{:S(2)}) collective-permute-start(bf16[8,128,128]{2,1,0:T(8,128)(2,1)S(1)} %collective-permute-done.3.refs_4_), channel_id=1, source_target_pairs={{0,4},{1,17},{2,6},{3,19},{4,0},{5,21},{6,2},{7,23},{8,12},{9,25},... | collective-permute-start | bytes 786440 | tf_op jit(solution)/shard_map/ppermute | solution.py:31
  21.4 0.9 collective-permute-start.6
  22.3 0.5 collective-permute-start.5
  22.9 0.6 gather_fusion
  23.7 2.5 %collective-permute-start.4 = (s32[8,32]{1,0:T(8,128)}, s32[8,32]{1,0:T(8,128)S(1)}, u32[]{:S(2)}, u32[]{:S(2)}) collective-permute-start(s32[8,32]{1,0:T(8,128)} %param.8), channel_id=1, source_target_pairs={{0,128},{1,129},{2,130},{3,131},{4,132},{5,133},{6,134},{7,135},{8... | collective-permute-start | bytes 3080 | tf_op jit(solution)/shard_map/ppermute | solution.py:31
  26.3 4.1 %collective-permute-done.4 = s32[8,32]{1,0:T(8,128)S(1)} collective-permute-done((s32[8,32]{1,0:T(8,128)}, s32[8,32]{1,0:T(8,128)S(1)}, u32[]{:S(2)}, u32[]{:S(2)}) %collective-permute-start.4) | collective-permute-done | bytes 1056 | tf_op jit(solution)/shard_map/ppermute | solution.py:31
  30.4 0.7 copy-done.2
  31.1 0.9 copy-done.3
  32.0 1.3 join.1.refs_0_
  33.3 2.6 %collective-permute-start.12 = (bf16[64,128,128]{2,1,0:T(8,128)(2,1)S(1)}, bf16[64,128,128]{2,1,0:T(8,128)(2,1)}, u32[]{:S(2)}, u32[]{:S(2)}) collective-permute-start(bf16[64,128,128]{2,1,0:T(8,128)(2,1)S(1)} %join.1.refs_0_), channel_id=1, source_target_pairs={{0,24},{1,7},{2,26},{3,1},{4,28},{5,3},{6,30},{7,5},{8,0},{9,15},{... | collective-permute-start | bytes 6291464 | tf_op jit(solution)/shard_map/ppermute | solution.py:31
  35.9 4.6 %collective-permute-start.10 = (bf16[64,128,128]{2,1,0:T(8,128)(2,1)S(1)}, bf16[64,128,128]{2,1,0:T(8,128)(2,1)}, u32[]{:S(2)}, u32[]{:S(2)}) collective-permute-start(bf16[64,128,128]{2,1,0:T(8,128)(2,1)S(1)} %join.1.refs_0_), channel_id=1, source_target_pairs={{0,1},{1,0},{2,3},{3,2},{4,5},{5,4},{6,7},{7,6},{8,9},{9,8},{10,11... | collective-permute-start | bytes 6291464 | tf_op jit(solution)/shard_map/ppermute | solution.py:31
  41.0 0.6 fusion.29
  41.7 5.4 %collective-permute-start.8 = (bf16[16,128,128]{2,1,0:T(8,128)(2,1)}, bf16[16,128,128]{2,1,0:T(8,128)(2,1)S(1)}, u32[]{:S(2)}, u32[]{:S(2)}) collective-permute-start(bf16[16,128,128]{2,1,0:T(8,128)(2,1)} %copy-done.7), channel_id=1, source_target_pairs={{0,64},{1,193},{2,66},{3,195},{4,68},{5,197},{6,70},{7,199},{8,72}... | collective-permute-start | bytes 1572872 | tf_op jit(solution)/shard_map/ppermute | solution.py:31
  47.1 1.2 select_reduce_fusion
  48.9 14.4 %collective-permute-done.8.refs_4_.refs_6_ = bf16[16,128,128]{2,1,0:T(8,128)(2,1)S(1)} collective-permute-done((bf16[16,128,128]{2,1,0:T(8,128)(2,1)}, bf16[16,128,128]{2,1,0:T(8,128)(2,1)S(1)}, u32[]{:S(2)}, u32[]{:S(2)}) %collective-permute-start.8) | collective-permute-done | bytes 524320 | tf_op jit(solution)/shard_map/ppermute | solution.py:31
  63.3 1.4 %collective-permute-done.9.refs_11_ = bf16[16,128,128]{2,1,0:T(8,128)(2,1)} collective-permute-done((bf16[16,128,128]{2,1,0:T(8,128)(2,1)}, bf16[16,128,128]{2,1,0:T(8,128)(2,1)}, u32[]{:S(2)}, u32[]{:S(2)}) %collective-permute-start.9) | collective-permute-done | bytes 524320 | tf_op jit(solution)/shard_map/ppermute | solution.py:31
  64.6 1.6 %halves.1 = (bf16[32,128,128]{2,1,0:T(8,128)(2,1)S(1)}, bf16[32,128,128]{2,1,0:T(8,128)(2,1)S(1)}) custom-call(bf16[64,128,128]{2,1,0:T(8,128)(2,1)} %collective-permute-done.11.up_ref.refs_1_, bf16[64,128,128]{2,1,0:T(8,128)(2,1)} %collective-permute-done.12.down_ref.refs_2_), custom_call_target="tpu_custom_call" | custom-call | bytes 4194304 | tf_op jit(solution)/shard_map/halves/pallas_call | solution.py:97
  66.3 3.3 %collective-permute-start.13 = (bf16[64,128,128]{2,1,0:T(8,128)(2,1)}, bf16[64,128,128]{2,1,0:T(8,128)(2,1)S(1)}, u32[]{:S(2)}, u32[]{:S(2)}) collective-permute-start(bf16[64,128,128]{2,1,0:T(8,128)(2,1)} %collective-permute-done.11.up_ref.refs_1_), channel_id=1, source_target_pairs={{0,1},{1,0},{2,3},{3,2},{4,5},{5,4},{6,7},{7,6},{8,9},{9,8},{10,11... | collective-permute-start | bytes 6291464 | tf_op jit(solution)/shard_map/ppermute | solution.py:31
  69.6 0.3 collective-permute-start.16
  69.9 2.4 %collective-permute-start.17 = (bf16[32,128,128]{2,1,0:T(8,128)(2,1)S(1)}, bf16[32,128,128]{2,1,0:T(8,128)(2,1)S(1)}, u32[]{:S(2)}, u32[]{:S(2)}) collective-permute-start(bf16[32,128,128]{2,1,0:T(8,128)(2,1)S(1)} %get-tuple-element.93), channel_id=1, source_target_pairs={{0,24},{1,7},{2,26},{3,1},{4,28},{5,3},{6,30},{7,5},{8,0},{9,15},{... | collective-permute-start | bytes 3145736 | tf_op jit(solution)/shard_map/ppermute | solution.py:31
  72.3 2.4 %collective-permute-start.15 = (bf16[16,128,128]{2,1,0:T(8,128)(2,1)S(1)}, bf16[16,128,128]{2,1,0:T(8,128)(2,1)S(1)}, u32[]{:S(2)}, u32[]{:S(2)}) collective-permute-start(bf16[16,128,128]{2,1,0:T(8,128)(2,1)S(1)} %copy-done.5), channel_id=1, source_target_pairs={{0,32},{1,225},{2,34},{3,227},{4,36},{5,229},{6,38},{7,231},{8,40}... | collective-permute-start | bytes 1572872 | tf_op jit(solution)/shard_map/ppermute | solution.py:31
  74.7 6.9 %products.4.refs_7_ = bf16[1,32,128,128]{3,2,1,0:T(8,128)(2,1)S(1)} custom-call(s32[512]{0:T(512)S(1)} %reshape.226.idx_ref, s32[16]{0:T(128)S(1)} %get-tuple-element.109.order_ref, s32[1]{0:T(128)} %get-tuple-element.110.count_ref, bf16[64,128,128]{2,1,0:T(8,128)(2,1)S(1)} %join.1.refs_0_, bf16[64,128,128]{2,1,0:T(8,128)(2,1)} %collective-permute-done.11.up_ref.refs_1_, ...), custom_call_target="tpu_custom_call" | custom-call | flops 2147483648 | bytes 8388608 | tf_op jit(solution)/shard_map/products/pallas_call | solution.py:194
  81.6 3.2 %collective-permute-done.16.refs_0_.refs_4_ = bf16[32,128,128]{2,1,0:T(8,128)(2,1)S(1)} collective-permute-done((bf16[32,128,128]{2,1,0:T(8,128)(2,1)S(1)}, bf16[32,128,128]{2,1,0:T(8,128)(2,1)S(1)}, u32[]{:S(2)}, u32[]{:S(2)}) %collective-permute-start.16) | collective-permute-done | bytes 1048608 | tf_op jit(solution)/shard_map/ppermute | solution.py:31
  84.8 1.4 %collective-permute-start.18 = (bf16[32,128,128]{2,1,0:T(8,128)(2,1)S(1)}, bf16[32,128,128]{2,1,0:T(8,128)(2,1)S(1)}, u32[]{:S(2)}, u32[]{:S(2)}) collective-permute-start(bf16[32,128,128]{2,1,0:T(8,128)(2,1)S(1)} %collective-permute-done.16.refs_0_.refs_4_), channel_id=1, source_target_pairs={{0,1},{1,0},{2,3},{3,2},{4,5},{5,4},{6,7},{7,6},{8,9},{9,8},{10,11... | collective-permute-start | bytes 3145736 | tf_op jit(solution)/shard_map/ppermute | solution.py:31
  86.2 2.2 %collective-permute-done.18.refs_4_.refs_8_ = bf16[32,128,128]{2,1,0:T(8,128)(2,1)S(1)} collective-permute-done((bf16[32,128,128]{2,1,0:T(8,128)(2,1)S(1)}, bf16[32,128,128]{2,1,0:T(8,128)(2,1)S(1)}, u32[]{:S(2)}, u32[]{:S(2)}) %collective-permute-start.18) | collective-permute-done | bytes 1048608 | tf_op jit(solution)/shard_map/ppermute | solution.py:31
  88.4 1.5 %collective-permute-done.19.refs_5_.refs_9_ = bf16[32,128,128]{2,1,0:T(8,128)(2,1)S(1)} collective-permute-done((bf16[32,128,128]{2,1,0:T(8,128)(2,1)S(1)}, bf16[32,128,128]{2,1,0:T(8,128)(2,1)S(1)}, u32[]{:S(2)}, u32[]{:S(2)}) %collective-permute-start.19) | collective-permute-done | bytes 1048608 | tf_op jit(solution)/shard_map/ppermute | solution.py:31
  89.9 4.6 %products.5 = bf16[1,32,128,128]{3,2,1,0:T(8,128)(2,1)S(1)} custom-call(s32[512]{0:T(512)S(1)} %reshape.228.idx_ref, s32[16]{0:T(128)S(1)} %get-tuple-element.109.order_ref, s32[1]{0:T(128)} %get-tuple-element.110.count_ref, bf16[32,128,128]{2,1,0:T(8,128)(2,1)S(1)} %collective-permute-done.16.refs_0_.refs_4_, ...), custom_call_target="tpu_custom_call" | custom-call | flops 2147483648 | bytes 8388608 | tf_op jit(solution)/shard_map/products/pallas_call | solution.py:194
  94.5 1.3 collective-permute-start.21
  95.8 8.2 %products.6 = (bf16[1,32,128,128]{3,2,1,0:T(8,128)(2,1)S(1)}, bf16[1,32,128,128]{3,2,1,0:T(8,128)(2,1)S(1)}) custom-call(s32[1024]{0:T(1024)S(1)} %reshape.229.idx_ref, s32[32]{0:T(128)S(1)} %reshape.230.order_ref, s32[2]{0:T(128)S(1)} %slice.38.count_ref, bf16[64,128,128]{2,1,0:T(8,128)(2,1)S(1)} %join.1.refs_0_, ...), custom_call_target="tpu_custom_call" | custom-call | flops 4294967296 | bytes 16777216 | tf_op jit(solution)/shard_map/products/pallas_call | solution.py:194
  104.0 1.6 %collective-permute-start.20 = (bf16[1,32,128,128]{3,2,1,0:T(8,128)(2,1)S(1)}, bf16[1,32,128,128]{3,2,1,0:T(8,128)(2,1)S(1)}, u32[]{:S(2)}, u32[]{:S(2)}) collective-permute-start(bf16[1,32,128,128]{3,2,1,0:T(8,128)(2,1)S(1)} %get-tuple-element.114), channel_id=1, source_target_pairs={{0,32},{1,225},{2,34},{3,227},{4,36},{5,229},{6,38},{7,231},{8,40}... | collective-permute-start | bytes 3145736 | tf_op jit(solution)/shard_map/ppermute | solution.py:31
  105.6 3.8 %collective-permute-done.21.refs_1_ = bf16[1,32,128,128]{3,2,1,0:T(8,128)(2,1)S(1)} collective-permute-done((bf16[1,32,128,128]{3,2,1,0:T(8,128)(2,1)S(1)}, bf16[1,32,128,128]{3,2,1,0:T(8,128)(2,1)S(1)}, u32[]{:S(2)}, u32[]{:S(2)}) %collective-permute-start.21) | collective-permute-done | bytes 1048608 | tf_op jit(solution)/shard_map/ppermute | solution.py:31
  109.7 1.7 %collective-permute-start.22 = (bf16[1,32,128,128]{3,2,1,0:T(8,128)(2,1)S(1)}, bf16[1,32,128,128]{3,2,1,0:T(8,128)(2,1)S(1)}, u32[]{:S(2)}, u32[]{:S(2)}) collective-permute-start(bf16[1,32,128,128]{3,2,1,0:T(8,128)(2,1)S(1)} %plus.2), channel_id=1, source_target_pairs={{0,224},{1,33},{2,226},{3,35},{4,228},{5,37},{6,230},{7,39},{8,232... | collective-permute-start | bytes 3145736 | tf_op jit(solution)/shard_map/ppermute | solution.py:31
  111.4 6.4 %products.7.refs_0_ = bf16[1,32,128,128]{3,2,1,0:T(8,128)(2,1)S(1)} custom-call(s32[512]{0:T(512)S(1)} %reshape.231.idx_ref, s32[16]{0:T(128)S(1)} %get-tuple-element.80.order_ref, s32[1]{0:T(128)} %get-tuple-element.81.count_ref, bf16[64,128,128]{2,1,0:T(8,128)(2,1)S(1)} %join.1.refs_0_, bf16[64,128,128]{2,1,0:T(8,128)(2,1)} %collective-permute-done.11.up_ref.refs_1_, ...), custom_call_target="tpu_custom_call" | custom-call | flops 2147483648 | bytes 16777216 | tf_op jit(solution)/shard_map/products/pallas_call | solution.py:194
  117.8 6.9 %collective-permute-done.20.refs_1_ = bf16[1,32,128,128]{3,2,1,0:T(8,128)(2,1)S(1)} collective-permute-done((bf16[1,32,128,128]{3,2,1,0:T(8,128)(2,1)S(1)}, bf16[1,32,128,128]{3,2,1,0:T(8,128)(2,1)S(1)}, u32[]{:S(2)}, u32[]{:S(2)}) %collective-permute-start.20) | collective-permute-done | bytes 1048608 | tf_op jit(solution)/shard_map/ppermute | solution.py:31
  124.7 7.5 %collective-permute-done.22.refs_2_ = bf16[1,32,128,128]{3,2,1,0:T(8,128)(2,1)S(1)} collective-permute-done((bf16[1,32,128,128]{3,2,1,0:T(8,128)(2,1)S(1)}, bf16[1,32,128,128]{3,2,1,0:T(8,128)(2,1)S(1)}, u32[]{:S(2)}, u32[]{:S(2)}) %collective-permute-start.22) | collective-permute-done | bytes 1048608 | tf_op jit(solution)/shard_map/ppermute | solution.py:31
  132.2 1.4 %plus.3 = bf16[1,32,128,128]{3,2,1,0:T(8,128)(2,1)} custom-call(bf16[1,32,128,128]{3,2,1,0:T(8,128)(2,1)S(1)} %products.7.refs_0_, bf16[1,32,128,128]{3,2,1,0:T(8,128)(2,1)S(1)} %collective-permute-done.20.refs_1_, bf16[1,32,128,128]{3,2,1,0:T(8,128)(2,1)S(1)} %collective-permute-done.22.refs_2_), custom_call_target="tpu_custom_call" | custom-call | bytes 4194304 | tf_op jit(solution)/shard_map/plus/pallas_call | solution.py:230
  (64 shorter events, 2.8 us)
Async XLA Ops:
  0.0 12.1 %copy-start = (s32[8,1,32]{2,1,0:T(1,128)S(1)}, s32[8,1,32]{2,1,0:T(1,128)}, u32[]{:S(2)}) copy-start(s32[8,1,32]{2,1,0:T(1,128)} %param.6) | copy-start | bytes 3076
  0.0 17.9 %collective-permute-start.3 = (bf16[8,128,128]{2,1,0:T(8,128)(2,1)}, bf16[8,128,128]{2,1,0:T(8,128)(2,1)S(1)}, u32[]{:S(2)}, u32[]{:S(2)}) collective-permute-start(bf16[8,128,128]{2,1,0:T(8,128)(2,1)} %bitcast.12), channel_id=1, source_target_pairs={{0,128},{1,129},{2,130},{3,131},{4,132},{5,133},{6,134},{7,135},{8... | collective-permute-start | bytes 786440 | tf_op jit(solution)/shard_map/ppermute | solution.py:31
  7.7 10.1 %collective-permute-start.2 = (bf16[8,128,128]{2,1,0:T(8,128)(2,1)}, bf16[8,128,128]{2,1,0:T(8,128)(2,1)S(1)}, u32[]{:S(2)}, u32[]{:S(2)}) collective-permute-start(bf16[8,128,128]{2,1,0:T(8,128)(2,1)} %bitcast.13), channel_id=1, source_target_pairs={{0,4},{1,17},{2,6},{3,19},{4,0},{5,21},{6,2},{7,23},{8,12},{9,25},... | collective-permute-start | bytes 786440 | tf_op jit(solution)/shard_map/ppermute | solution.py:31
  10.7 7.5 %collective-permute-start.1 = (bf16[8,128,128]{2,1,0:T(8,128)(2,1)}, bf16[8,128,128]{2,1,0:T(8,128)(2,1)S(1)}, u32[]{:S(2)}, u32[]{:S(2)}) collective-permute-start(bf16[8,128,128]{2,1,0:T(8,128)(2,1)} %bitcast.14), channel_id=1, source_target_pairs={{0,6},{1,25},{2,0},{3,27},{4,2},{5,29},{6,4},{7,31},{8,14},{9,1},{... | collective-permute-start | bytes 786440 | tf_op jit(solution)/shard_map/ppermute | solution.py:31
  11.4 6.9 %collective-permute-start = (bf16[8,128,128]{2,1,0:T(8,128)(2,1)}, bf16[8,128,128]{2,1,0:T(8,128)(2,1)S(1)}, u32[]{:S(2)}, u32[]{:S(2)}) collective-permute-start(bf16[8,128,128]{2,1,0:T(8,128)(2,1)} %bitcast.15), channel_id=1, source_target_pairs={{0,2},{1,9},{2,4},{3,11},{4,6},{5,13},{6,0},{7,15},{8,10},{9,17},{... | collective-permute-start | bytes 786440 | tf_op jit(solution)/shard_map/ppermute | solution.py:31
  12.9 1.2 copy-start.1
  14.8 0.8 copy-start.4
  15.6 0.8 copy-start.6
  16.4 0.8 copy-start.7
  17.9 12.5 %copy-start.8 = (bf16[8,128,128]{2,1,0:T(8,128)(2,1)}, bf16[8,128,128]{2,1,0:T(8,128)(2,1)S(1)}, u32[]{:S(2)}) copy-start(bf16[8,128,128]{2,1,0:T(8,128)(2,1)S(1)} %collective-permute-done.2.refs_3_) | copy-start | bytes 786436
  18.2 0.7 copy-start.9
  18.4 0.7 copy-start.10
  19.1 11.3 %collective-permute-start.7 = (bf16[8,128,128]{2,1,0:T(8,128)(2,1)S(1)}, bf16[8,128,128]{2,1,0:T(8,128)(2,1)S(1)}, u32[]{:S(2)}, u32[]{:S(2)}) collective-permute-start(bf16[8,128,128]{2,1,0:T(8,128)(2,1)S(1)} %collective-permute-done.3.refs_4_), channel_id=1, source_target_pairs={{0,4},{1,17},{2,6},{3,19},{4,0},{5,21},{6,2},{7,23},{8,12},{9,25},... | collective-permute-start | bytes 786440 | tf_op jit(solution)/shard_map/ppermute | solution.py:31
  21.4 8.9 %collective-permute-start.6 = (bf16[8,128,128]{2,1,0:T(8,128)(2,1)S(1)}, bf16[8,128,128]{2,1,0:T(8,128)(2,1)S(1)}, u32[]{:S(2)}, u32[]{:S(2)}) collective-permute-start(bf16[8,128,128]{2,1,0:T(8,128)(2,1)S(1)} %collective-permute-done.3.refs_4_), channel_id=1, source_target_pairs={{0,6},{1,25},{2,0},{3,27},{4,2},{5,29},{6,4},{7,31},{8,14},{9,1},{... | collective-permute-start | bytes 786440 | tf_op jit(solution)/shard_map/ppermute | solution.py:31
  22.3 8.0 %collective-permute-start.5 = (bf16[8,128,128]{2,1,0:T(8,128)(2,1)S(1)}, bf16[8,128,128]{2,1,0:T(8,128)(2,1)S(1)}, u32[]{:S(2)}, u32[]{:S(2)}) collective-permute-start(bf16[8,128,128]{2,1,0:T(8,128)(2,1)S(1)} %collective-permute-done.3.refs_4_), channel_id=1, source_target_pairs={{0,2},{1,9},{2,4},{3,11},{4,6},{5,13},{6,0},{7,15},{8,10},{9,17},{... | collective-permute-start | bytes 786440 | tf_op jit(solution)/shard_map/ppermute | solution.py:31
  23.4 23.6 %copy-start.11 = (s32[8,32]{1,0:T(8,128)S(1)}, s32[8,32]{1,0:T(8,128)}, u32[]{:S(2)}) copy-start(s32[8,32]{1,0:T(8,128)} %param.8) | copy-start | bytes 3076
  23.7 6.7 %collective-permute-start.4 = (s32[8,32]{1,0:T(8,128)}, s32[8,32]{1,0:T(8,128)S(1)}, u32[]{:S(2)}, u32[]{:S(2)}) collective-permute-start(s32[8,32]{1,0:T(8,128)} %param.8), channel_id=1, source_target_pairs={{0,128},{1,129},{2,130},{3,131},{4,132},{5,133},{6,134},{7,135},{8... | collective-permute-start | bytes 3080 | tf_op jit(solution)/shard_map/ppermute | solution.py:31
  30.4 0.7 copy-start.2
  31.1 0.9 copy-start.3
  33.3 31.3 %collective-permute-start.12 = (bf16[64,128,128]{2,1,0:T(8,128)(2,1)S(1)}, bf16[64,128,128]{2,1,0:T(8,128)(2,1)}, u32[]{:S(2)}, u32[]{:S(2)}) collective-permute-start(bf16[64,128,128]{2,1,0:T(8,128)(2,1)S(1)} %join.1.refs_0_), channel_id=1, source_target_pairs={{0,24},{1,7},{2,26},{3,1},{4,28},{5,3},{6,30},{7,5},{8,0},{9,15},{... | collective-permute-start | bytes 6291464 | tf_op jit(solution)/shard_map/ppermute | solution.py:31
  35.8 28.8 %collective-permute-start.11 = (bf16[64,128,128]{2,1,0:T(8,128)(2,1)S(1)}, bf16[64,128,128]{2,1,0:T(8,128)(2,1)}, u32[]{:S(2)}, u32[]{:S(2)}) collective-permute-start(bf16[64,128,128]{2,1,0:T(8,128)(2,1)S(1)} %join.1.refs_0_), channel_id=1, source_target_pairs={{0,8},{1,3},{2,10},{3,5},{4,12},{5,7},{6,14},{7,1},{8,16},{9,11},{... | collective-permute-start | bytes 6291464 | tf_op jit(solution)/shard_map/ppermute | solution.py:31
  35.9 28.8 %collective-permute-start.10 = (bf16[64,128,128]{2,1,0:T(8,128)(2,1)S(1)}, bf16[64,128,128]{2,1,0:T(8,128)(2,1)}, u32[]{:S(2)}, u32[]{:S(2)}) collective-permute-start(bf16[64,128,128]{2,1,0:T(8,128)(2,1)S(1)} %join.1.refs_0_), channel_id=1, source_target_pairs={{0,1},{1,0},{2,3},{3,2},{4,5},{5,4},{6,7},{7,6},{8,9},{9,8},{10,11... | collective-permute-start | bytes 6291464 | tf_op jit(solution)/shard_map/ppermute | solution.py:31
  41.7 21.6 %collective-permute-start.8 = (bf16[16,128,128]{2,1,0:T(8,128)(2,1)}, bf16[16,128,128]{2,1,0:T(8,128)(2,1)S(1)}, u32[]{:S(2)}, u32[]{:S(2)}) collective-permute-start(bf16[16,128,128]{2,1,0:T(8,128)(2,1)} %copy-done.7), channel_id=1, source_target_pairs={{0,64},{1,193},{2,66},{3,195},{4,68},{5,197},{6,70},{7,199},{8,72}... | collective-permute-start | bytes 1572872 | tf_op jit(solution)/shard_map/ppermute | solution.py:31
  47.1 17.5 %collective-permute-start.9 = (bf16[16,128,128]{2,1,0:T(8,128)(2,1)}, bf16[16,128,128]{2,1,0:T(8,128)(2,1)}, u32[]{:S(2)}, u32[]{:S(2)}) collective-permute-start(bf16[16,128,128]{2,1,0:T(8,128)(2,1)} %copy-done.6), channel_id=1, source_target_pairs={{0,224},{1,33},{2,226},{3,35},{4,228},{5,37},{6,230},{7,39},{8,232... | collective-permute-start | bytes 1572872 | tf_op jit(solution)/shard_map/ppermute | solution.py:31
  64.6 7.7 %copy-start.5 = (bf16[16,128,128]{2,1,0:T(8,128)(2,1)S(1)}, bf16[16,128,128]{2,1,0:T(8,128)(2,1)}, u32[]{:S(2)}) copy-start(bf16[16,128,128]{2,1,0:T(8,128)(2,1)} %copy-done.4) | copy-start | bytes 1572868
  66.3 18.5 %collective-permute-start.13 = (bf16[64,128,128]{2,1,0:T(8,128)(2,1)}, bf16[64,128,128]{2,1,0:T(8,128)(2,1)S(1)}, u32[]{:S(2)}, u32[]{:S(2)}) collective-permute-start(bf16[64,128,128]{2,1,0:T(8,128)(2,1)} %collective-permute-done.11.up_ref.refs_1_), channel_id=1, source_target_pairs={{0,1},{1,0},{2,3},{3,2},{4,5},{5,4},{6,7},{7,6},{8,9},{9,8},{10,11... | collective-permute-start | bytes 6291464 | tf_op jit(solution)/shard_map/ppermute | solution.py:31
  69.5 15.3 %collective-permute-start.14 = (bf16[64,128,128]{2,1,0:T(8,128)(2,1)}, bf16[64,128,128]{2,1,0:T(8,128)(2,1)S(1)}, u32[]{:S(2)}, u32[]{:S(2)}) collective-permute-start(bf16[64,128,128]{2,1,0:T(8,128)(2,1)} %collective-permute-done.12.down_ref.refs_2_), channel_id=1, source_target_pairs={{0,1},{1,0},{2,3},{3,2},{4,5},{5,4},{6,7},{7,6},{8,9},{9,8},{10,11... | collective-permute-start | bytes 6291464 | tf_op jit(solution)/shard_map/ppermute | solution.py:31
  69.6 15.2 %collective-permute-start.16 = (bf16[32,128,128]{2,1,0:T(8,128)(2,1)S(1)}, bf16[32,128,128]{2,1,0:T(8,128)(2,1)S(1)}, u32[]{:S(2)}, u32[]{:S(2)}) collective-permute-start(bf16[32,128,128]{2,1,0:T(8,128)(2,1)S(1)} %get-tuple-element.92), channel_id=1, source_target_pairs={{0,8},{1,3},{2,10},{3,5},{4,12},{5,7},{6,14},{7,1},{8,16},{9,11},{... | collective-permute-start | bytes 3145736 | tf_op jit(solution)/shard_map/ppermute | solution.py:31
  69.9 14.8 %collective-permute-start.17 = (bf16[32,128,128]{2,1,0:T(8,128)(2,1)S(1)}, bf16[32,128,128]{2,1,0:T(8,128)(2,1)S(1)}, u32[]{:S(2)}, u32[]{:S(2)}) collective-permute-start(bf16[32,128,128]{2,1,0:T(8,128)(2,1)S(1)} %get-tuple-element.93), channel_id=1, source_target_pairs={{0,24},{1,7},{2,26},{3,1},{4,28},{5,3},{6,30},{7,5},{8,0},{9,15},{... | collective-permute-start | bytes 3145736 | tf_op jit(solution)/shard_map/ppermute | solution.py:31
  72.3 9.3 %collective-permute-start.15 = (bf16[16,128,128]{2,1,0:T(8,128)(2,1)S(1)}, bf16[16,128,128]{2,1,0:T(8,128)(2,1)S(1)}, u32[]{:S(2)}, u32[]{:S(2)}) collective-permute-start(bf16[16,128,128]{2,1,0:T(8,128)(2,1)S(1)} %copy-done.5), channel_id=1, source_target_pairs={{0,32},{1,225},{2,34},{3,227},{4,36},{5,229},{6,38},{7,231},{8,40}... | collective-permute-start | bytes 1572872 | tf_op jit(solution)/shard_map/ppermute | solution.py:31
  84.8 3.6 %collective-permute-start.18 = (bf16[32,128,128]{2,1,0:T(8,128)(2,1)S(1)}, bf16[32,128,128]{2,1,0:T(8,128)(2,1)S(1)}, u32[]{:S(2)}, u32[]{:S(2)}) collective-permute-start(bf16[32,128,128]{2,1,0:T(8,128)(2,1)S(1)} %collective-permute-done.16.refs_0_.refs_4_), channel_id=1, source_target_pairs={{0,1},{1,0},{2,3},{3,2},{4,5},{5,4},{6,7},{7,6},{8,9},{9,8},{10,11... | collective-permute-start | bytes 3145736 | tf_op jit(solution)/shard_map/ppermute | solution.py:31
  86.1 3.8 %collective-permute-start.19 = (bf16[32,128,128]{2,1,0:T(8,128)(2,1)S(1)}, bf16[32,128,128]{2,1,0:T(8,128)(2,1)S(1)}, u32[]{:S(2)}, u32[]{:S(2)}) collective-permute-start(bf16[32,128,128]{2,1,0:T(8,128)(2,1)S(1)} %collective-permute-done.17.refs_1_.refs_5_), channel_id=1, source_target_pairs={{0,1},{1,0},{2,3},{3,2},{4,5},{5,4},{6,7},{7,6},{8,9},{9,8},{10,11... | collective-permute-start | bytes 3145736 | tf_op jit(solution)/shard_map/ppermute | solution.py:31
  94.5 14.9 %collective-permute-start.21 = (bf16[1,32,128,128]{3,2,1,0:T(8,128)(2,1)S(1)}, bf16[1,32,128,128]{3,2,1,0:T(8,128)(2,1)S(1)}, u32[]{:S(2)}, u32[]{:S(2)}) collective-permute-start(bf16[1,32,128,128]{3,2,1,0:T(8,128)(2,1)S(1)} %products.5), channel_id=1, source_target_pairs={{0,224},{1,33},{2,226},{3,35},{4,228},{5,37},{6,230},{7,39},{8,232... | collective-permute-start | bytes 3145736 | tf_op jit(solution)/shard_map/ppermute | solution.py:31
  104.0 20.7 %collective-permute-start.20 = (bf16[1,32,128,128]{3,2,1,0:T(8,128)(2,1)S(1)}, bf16[1,32,128,128]{3,2,1,0:T(8,128)(2,1)S(1)}, u32[]{:S(2)}, u32[]{:S(2)}) collective-permute-start(bf16[1,32,128,128]{3,2,1,0:T(8,128)(2,1)S(1)} %get-tuple-element.114), channel_id=1, source_target_pairs={{0,32},{1,225},{2,34},{3,227},{4,36},{5,229},{6,38},{7,231},{8,40}... | collective-permute-start | bytes 3145736 | tf_op jit(solution)/shard_map/ppermute | solution.py:31
  109.7 22.5 %collective-permute-start.22 = (bf16[1,32,128,128]{3,2,1,0:T(8,128)(2,1)S(1)}, bf16[1,32,128,128]{3,2,1,0:T(8,128)(2,1)S(1)}, u32[]{:S(2)}, u32[]{:S(2)}) collective-permute-start(bf16[1,32,128,128]{3,2,1,0:T(8,128)(2,1)S(1)} %plus.2), channel_id=1, source_target_pairs={{0,224},{1,33},{2,226},{3,35},{4,228},{5,37},{6,230},{7,39},{8,232... | collective-permute-start | bytes 3145736 | tf_op jit(solution)/shard_map/ppermute | solution.py:31

commit v4 on v3

--- a/solution.py
+++ b/solution.py
@@ -13,6 +13,7 @@
 ROWS = 8
 SEL = 16
 SET = 512
+EARLY = 384
 AXES = ("row", "col")
 OFFSETS = (2, 1, -1, 0)
 
@@ -267,17 +268,16 @@
     def round_one(block):
         return [in_plane(block, distance, 0) for distance in (1, -1, 2)]
 
-    near_ring, picked, reach_cols, far_set = stage(
+    picked_at, reach_cols = stage(picked_at.astype(jnp.int32), reach_cols)
+    far_cols, near_ring, picked, far_set = stage(
+        send(reach_cols, lambda z, y, x, c: (z + NZ // 2, y, x, c)),
         round_one(blocks),
-        pick(own_left, picked_at.astype(jnp.int32)),
-        reach_cols,
+        pick(own_left, picked_at),
         send(blocks, lambda z, y, x, c: (z + NZ // 2, y, x, c)),
     )
     far_l, near_l, leaf_l, own_l = picked
     far_l = along_z(far_l, 2)
-    far_cols, far_ring, leaf_l = stage(
-        send(reach_cols, lambda z, y, x, c: (z + NZ // 2, y, x, c)), round_one(far_set), leaf_l
-    )
+    far_ring, leaf_l = stage(round_one(far_set), leaf_l)
     first = join((blocks, *near_ring), (far_set, *far_ring))
 
     steps = jnp.array(OFFSETS, dtype=jnp.int32)
@@ -291,7 +291,7 @@
     dx = place(slot // NC % NX - x + NX)
     dy = place(slot // (NC * NX) - y + NY)
     then, ahead = jnp.where(slot % NC == 0, dy, dx), jnp.where(slot % NC == 0, dx, dy)
-    turn = jnp.where(slot % NC == c, jnp.where(then == 3, 4, then), jnp.where(then == 0, 3, then + 4))
+    turn = jnp.where(slot % NC == c, jnp.where(then == 3, 6, then), jnp.where(then == 3, 7, then + 3))
     near_place = turn * 64 + ahead * 8
     j = jnp.arange(SEL, dtype=jnp.int32)
 
@@ -305,20 +305,20 @@
     at = jnp.sum(jnp.where(same, place_of[None, :, None, :] - SET, 0), axis=3)
     idx = SET + jnp.sum(jnp.where(hit[:, :, :, None], at[:, None, :, :], 0), axis=2)
     count = jnp.sum(present.astype(jnp.int32), axis=1)
-    half = SET // 2
-    idx_early = jnp.where(idx < half, idx, half)
-    idx_late = jnp.where((idx >= half) & (idx < SET), idx - half, half)
+    idx_early = jnp.where(idx < EARLY, idx, EARLY)
+    idx_late = jnp.where((idx >= EARLY) & (idx < SET), idx - EARLY, SET - EARLY)
 
     def entry(blocks_at, first, last):
         return tuple(t[first:last].reshape(-1) for t in (blocks_at, order, count))
 
     tables = entry(idx_early, 0, 1), entry(idx_late, 0, 1), entry(idx, 1, 3), entry(idx, 3, 4)
 
+    tables, ready = stage(tables, first)
     tables, far_l, leaf_l, first_got, first, up, down, near_l = stage(
         tables,
         far_l,
         along_z(leaf_l, -1),
-        swap(first),
+        swap(ready),
         first,
         in_plane(first, 1, 1),
         in_plane(first, -1, 1),
@@ -326,16 +326,18 @@
     )
     near_half, far_half = halves(up, down)
     up, down, near_l, near_half, far_half = stage(up, down, near_l, near_half, far_half)
-    early = (first, up, down, first_got)
+    up_got, down_got = swap(up), swap(down)
+    early = (first, up, down, first_got, up_got, down_got)
     up_got, down_got, near_l, near_on, far_on, early_term = stage(
-        swap(up),
-        swap(down),
+        up_got,
+        down_got,
         along_z(near_l, 1),
         in_plane(near_half, 1, 1),
         in_plane(far_half, -1, 1),
         products(tables[0], early, (far_l,)),
     )
-    late = (near_on, far_on, up_got, down_got, swap(near_on), swap(far_on))
+    early = early[:4] + (up_got, down_got)
+    late = (near_on, far_on, swap(near_on), swap(far_on))
 
     (far_term,) = products(tables[1], late, (far_l,), early_term)
     far_got = along_z(far_term, -1)

time: 134 us -> 129 us (0.963)
  waiting for transfers between devices: 45.4 us -> 62.5 us
  Pallas kernels: 31.2 us -> 21 us
  starting transfers between devices: 45.4 us -> 37.2 us
  local copies, waits for them, and re-layouts: 7.64 us -> 3.68 us
    ppermute x23, waiting for transfers between devices: 45.4 us -> 62.5 us  [send(): return lax.ppermute(block, AXES, pairs)]
    pallas_call x4, Pallas kernels: 26 us -> 17.3 us  [products(): pl.pallas_call(functools.partial(products_kernel, len(panel_parts), n, le...]
    ppermute x23, starting transfers between devices: 45.4 us -> 37.2 us  [send(): return lax.ppermute(block, AXES, pairs)]
    unnamed x24 -> x10, local copies, waits for them, and re-layouts: 5.99 us -> 2.05 us
    pallas_call x1, Pallas kernels: 1.62 us -> 0.16 us  [halves(): pl.pallas_call(halves_kernel, out_shape=[jax.ShapeDtypeStruct((half, BLK,...]
  transfers between devices with their start and end apart: 23 -> 23, of which waited for: 11 -> 16; matrix products, arithmetic and copies ran while one was open for 4% -> 5% of each run, Pallas kernels for 17% -> 12%
where the time goes in v4:
time: 129 us
  waiting for transfers between devices  62.5 us (48%)
  starting transfers between devices  37.2 us (29%)
  Pallas kernels  21 us (16%)
  other arithmetic  4.34 us (3%)
  local copies, waits for them, and re-layouts  3.68 us (3%)
    ppermute x23, waiting for transfers between devices, send(): return lax.ppermute(block, AXES, pairs)  62.5 us
    ppermute x23, starting transfers between devices, send(): return lax.ppermute(block, AXES, pairs)  37.2 us
    pallas_call x4, Pallas kernels, products(): pl.pallas_call(functools.partial(products_kernel, len(panel_parts), n, le...  17.3 us
  transfers between devices with their start and end apart: 23, of which 16 were waited for; matrix products, arithmetic and copies ran while one was open for 5% of the time, Pallas kernels for 12%

profile of v4, /device:TPU:1, one launch (start us, length us, event | category | flops | bytes accessed | tf_op | source)
XLA Modules:
  0.0 128.9 jit_solution(8738767879195753052)
XLA Ops:
  0.0 7.7 %collective-permute-start.4 = (bf16[8,128,128]{2,1,0:T(8,128)(2,1)}, bf16[8,128,128]{2,1,0:T(8,128)(2,1)S(1)}, u32[]{:S(2)}, u32[]{:S(2)}) collective-permute-start(bf16[8,128,128]{2,1,0:T(8,128)(2,1)} %bitcast.12), channel_id=1, source_target_pairs={{0,128},{1,129},{2,130},{3,131},{4,132},{5,133},{6,134},{7,135},{8... | collective-permute-start | bytes 786440 | tf_op jit(solution)/shard_map/ppermute | solution.py:32
  7.7 2.9 %collective-permute-start.3 = (bf16[8,128,128]{2,1,0:T(8,128)(2,1)}, bf16[8,128,128]{2,1,0:T(8,128)(2,1)S(1)}, u32[]{:S(2)}, u32[]{:S(2)}) collective-permute-start(bf16[8,128,128]{2,1,0:T(8,128)(2,1)} %bitcast.13), channel_id=1, source_target_pairs={{0,4},{1,17},{2,6},{3,19},{4,0},{5,21},{6,2},{7,23},{8,12},{9,25},... | collective-permute-start | bytes 786440 | tf_op jit(solution)/shard_map/ppermute | solution.py:32
  10.7 0.8 collective-permute-start.2
  11.4 0.7 collective-permute-start.1
  12.3 0.6 iota_reduce_fusion
  13.0 0.7 compare_select_fusion.1
  13.7 0.6 gather_fusion
  14.2 0.2 compare_reduce_fusion
  15.0 0.6 fusion.29
  15.8 1.2 copy-done.1
  17.0 0.7 pick.1
  17.7 1.9 %collective-permute-done = s32[8,32]{1,0:T(8,128)S(1)} collective-permute-done((s32[8,32]{1,0:T(8,128)}, s32[8,32]{1,0:T(8,128)S(1)}, u32[]{:S(2)}, u32[]{:S(2)}) %collective-permute-start) | collective-permute-done | bytes 1056 | tf_op jit(solution)/shard_map/ppermute | solution.py:32
  19.7 0.7 copy-done.3
  20.5 0.9 collective-permute-start.7
  21.4 2.2 %collective-permute-start.6 = (bf16[8,128,128]{2,1,0:T(8,128)(2,1)S(1)}, bf16[8,128,128]{2,1,0:T(8,128)(2,1)S(1)}, u32[]{:S(2)}, u32[]{:S(2)}) collective-permute-start(bf16[8,128,128]{2,1,0:T(8,128)(2,1)S(1)} %collective-permute-done.4.refs_4_), channel_id=1, source_target_pairs={{0,6},{1,25},{2,0},{3,27},{4,2},{5,29},{6,4},{7,31},{8,14},{9,1},{... | collective-permute-start | bytes 786440 | tf_op jit(solution)/shard_map/ppermute | solution.py:32
  23.6 0.7 pad_add_fusion
  24.3 1.2 select_reduce_fusion
  25.5 0.2 select_reduce_fusion.1
  26.1 1.1 collective-permute-done.7.refs_7_
  27.2 3.1 %collective-permute-done.6.refs_6_ = bf16[8,128,128]{2,1,0:T(8,128)(2,1)S(1)} collective-permute-done((bf16[8,128,128]{2,1,0:T(8,128)(2,1)S(1)}, bf16[8,128,128]{2,1,0:T(8,128)(2,1)S(1)}, u32[]{:S(2)}, u32[]{:S(2)}) %collective-permute-start.6) | collective-permute-done | bytes 262176 | tf_op jit(solution)/shard_map/ppermute | solution.py:32
  30.3 1.3 join.1.refs_0_
  31.6 3.9 %collective-permute-start.10 = (bf16[64,128,128]{2,1,0:T(8,128)(2,1)S(1)}, bf16[64,128,128]{2,1,0:T(8,128)(2,1)S(1)}, u32[]{:S(2)}, u32[]{:S(2)}) collective-permute-start(bf16[64,128,128]{2,1,0:T(8,128)(2,1)S(1)} %join.1.refs_0_), channel_id=1, source_target_pairs={{0,1},{1,0},{2,3},{3,2},{4,5},{5,4},{6,7},{7,6},{8,9},{9,8},{10,11... | collective-permute-start | bytes 6291464 | tf_op jit(solution)/shard_map/ppermute | solution.py:32
  35.5 2.1 %collective-permute-start.12 = (bf16[64,128,128]{2,1,0:T(8,128)(2,1)S(1)}, bf16[64,128,128]{2,1,0:T(8,128)(2,1)S(1)}, u32[]{:S(2)}, u32[]{:S(2)}) collective-permute-start(bf16[64,128,128]{2,1,0:T(8,128)(2,1)S(1)} %join.1.refs_0_), channel_id=1, source_target_pairs={{0,24},{1,7},{2,26},{3,1},{4,28},{5,3},{6,30},{7,5},{8,0},{9,15},{... | collective-permute-start | bytes 6291464 | tf_op jit(solution)/shard_map/ppermute | solution.py:32
  37.6 3.1 %collective-permute-start.8 = (bf16[16,128,128]{2,1,0:T(8,128)(2,1)S(1)}, bf16[16,128,128]{2,1,0:T(8,128)(2,1)S(1)}, u32[]{:S(2)}, u32[]{:S(2)}) collective-permute-start(bf16[16,128,128]{2,1,0:T(8,128)(2,1)S(1)} %get-tuple-element.103), channel_id=1, source_target_pairs={{0,64},{1,193},{2,66},{3,195},{4,68},{5,197},{6,70},{7,199},{8,72}... | collective-permute-start | bytes 1572872 | tf_op jit(solution)/shard_map/ppermute | solution.py:32
  40.8 16.4 %collective-permute-done.8.refs_6_.refs_4_ = bf16[16,128,128]{2,1,0:T(8,128)(2,1)S(1)} collective-permute-done((bf16[16,128,128]{2,1,0:T(8,128)(2,1)S(1)}, bf16[16,128,128]{2,1,0:T(8,128)(2,1)S(1)}, u32[]{:S(2)}, u32[]{:S(2)}) %collective-permute-start.8) | collective-permute-done | bytes 524320 | tf_op jit(solution)/shard_map/ppermute | solution.py:32
  57.1 3.0 %collective-permute-done.9.refs_11_ = bf16[16,128,128]{2,1,0:T(8,128)(2,1)S(1)} collective-permute-done((bf16[16,128,128]{2,1,0:T(8,128)(2,1)S(1)}, bf16[16,128,128]{2,1,0:T(8,128)(2,1)S(1)}, u32[]{:S(2)}, u32[]{:S(2)}) %collective-permute-start.9) | collective-permute-done | bytes 524320 | tf_op jit(solution)/shard_map/ppermute | solution.py:32
  60.1 0.6 collective-permute-done.12.down_ref.refs_2_
  60.7 3.3 %collective-permute-done.11.up_ref.refs_1_ = bf16[64,128,128]{2,1,0:T(8,128)(2,1)S(1)} collective-permute-done((bf16[64,128,128]{2,1,0:T(8,128)(2,1)S(1)}, bf16[64,128,128]{2,1,0:T(8,128)(2,1)S(1)}, u32[]{:S(2)}, u32[]{:S(2)}) %collective-permute-start.11) | collective-permute-done | bytes 2097184 | tf_op jit(solution)/shard_map/ppermute | solution.py:32
  64.2 2.0 %collective-permute-start.13 = (bf16[64,128,128]{2,1,0:T(8,128)(2,1)S(1)}, bf16[64,128,128]{2,1,0:T(8,128)(2,1)S(1)}, u32[]{:S(2)}, u32[]{:S(2)}) collective-permute-start(bf16[64,128,128]{2,1,0:T(8,128)(2,1)S(1)} %collective-permute-done.11.up_ref.refs_1_), channel_id=1, source_target_pairs={{0,1},{1,0},{2,3},{3,2},{4,5},{5,4},{6,7},{7,6},{8,9},{9,8},{10,11... | collective-permute-start | bytes 6291464 | tf_op jit(solution)/shard_map/ppermute | solution.py:32
  66.2 2.7 %collective-permute-start.17 = (bf16[32,128,128]{2,1,0:T(8,128)(2,1)S(1)}, bf16[32,128,128]{2,1,0:T(8,128)(2,1)S(1)}, u32[]{:S(2)}, u32[]{:S(2)}) collective-permute-start(bf16[32,128,128]{2,1,0:T(8,128)(2,1)S(1)} %get-tuple-element.121), channel_id=1, source_target_pairs={{0,24},{1,7},{2,26},{3,1},{4,28},{5,3},{6,30},{7,5},{8,0},{9,15},{... | collective-permute-start | bytes 3145736 | tf_op jit(solution)/shard_map/ppermute | solution.py:32
  68.9 2.4 %collective-permute-start.15 = (bf16[16,128,128]{2,1,0:T(8,128)(2,1)S(1)}, bf16[16,128,128]{2,1,0:T(8,128)(2,1)S(1)}, u32[]{:S(2)}, u32[]{:S(2)}) collective-permute-start(bf16[16,128,128]{2,1,0:T(8,128)(2,1)S(1)} %get-tuple-element.119), channel_id=1, source_target_pairs={{0,32},{1,225},{2,34},{3,227},{4,36},{5,229},{6,38},{7,231},{8,40}... | collective-permute-start | bytes 1572872 | tf_op jit(solution)/shard_map/ppermute | solution.py:32
  71.4 1.6 %collective-permute-done.14.refs_5_ = bf16[64,128,128]{2,1,0:T(8,128)(2,1)S(1)} collective-permute-done((bf16[64,128,128]{2,1,0:T(8,128)(2,1)S(1)}, bf16[64,128,128]{2,1,0:T(8,128)(2,1)S(1)}, u32[]{:S(2)}, u32[]{:S(2)}) %collective-permute-start.14) | collective-permute-done | bytes 2097184 | tf_op jit(solution)/shard_map/ppermute | solution.py:32
  72.9 3.5 %products.4.refs_5_ = bf16[1,32,128,128]{3,2,1,0:T(8,128)(2,1)S(1)} custom-call(s32[512]{0:T(512)S(1)} %reshape.225.idx_ref, s32[16]{0:T(128)S(1)} %get-tuple-element.137.order_ref, s32[1]{0:T(128)} %get-tuple-element.138.count_ref, bf16[64,128,128]{2,1,0:T(8,128)(2,1)S(1)} %join.1.refs_0_, bf16[64,128,128]{2,1,0:T(8,128)(2,1)S(1)} %collective-permute-done.11.up_ref.refs_1_, ...), custom_call_target="tpu_custom_call" | custom-call | flops 2147483648 | bytes 12582912 | tf_op jit(solution)/shard_map/products/pallas_call | solution.py:195
  76.4 1.1 collective-permute-done.15.refs_10_
  77.5 3.9 %collective-permute-done.16.refs_0_.refs_6_ = bf16[32,128,128]{2,1,0:T(8,128)(2,1)S(1)} collective-permute-done((bf16[32,128,128]{2,1,0:T(8,128)(2,1)S(1)}, bf16[32,128,128]{2,1,0:T(8,128)(2,1)S(1)}, u32[]{:S(2)}, u32[]{:S(2)}) %collective-permute-start.16) | collective-permute-done | bytes 1048608 | tf_op jit(solution)/shard_map/ppermute | solution.py:32
  81.4 1.3 collective-permute-start.18
  82.7 2.3 %collective-permute-done.18.refs_2_.refs_8_ = bf16[32,128,128]{2,1,0:T(8,128)(2,1)S(1)} collective-permute-done((bf16[32,128,128]{2,1,0:T(8,128)(2,1)S(1)}, bf16[32,128,128]{2,1,0:T(8,128)(2,1)S(1)}, u32[]{:S(2)}, u32[]{:S(2)}) %collective-permute-start.18) | collective-permute-done | bytes 1048608 | tf_op jit(solution)/shard_map/ppermute | solution.py:32
  85.0 1.5 %collective-permute-done.19.refs_3_.refs_9_ = bf16[32,128,128]{2,1,0:T(8,128)(2,1)S(1)} collective-permute-done((bf16[32,128,128]{2,1,0:T(8,128)(2,1)S(1)}, bf16[32,128,128]{2,1,0:T(8,128)(2,1)S(1)}, u32[]{:S(2)}, u32[]{:S(2)}) %collective-permute-start.19) | collective-permute-done | bytes 1048608 | tf_op jit(solution)/shard_map/ppermute | solution.py:32
  86.5 2.9 %products.5 = bf16[1,32,128,128]{3,2,1,0:T(8,128)(2,1)S(1)} custom-call(s32[512]{0:T(512)S(1)} %reshape.227.idx_ref, s32[16]{0:T(128)S(1)} %get-tuple-element.137.order_ref, s32[1]{0:T(128)} %get-tuple-element.138.count_ref, bf16[32,128,128]{2,1,0:T(8,128)(2,1)S(1)} %collective-permute-done.16.refs_0_.refs_6_, ...), custom_call_target="tpu_custom_call" | custom-call | flops 2147483648 | bytes 4194304 | tf_op jit(solution)/shard_map/products/pallas_call | solution.py:195
  89.4 1.3 collective-permute-start.21
  90.7 6.3 %products.6 = (bf16[1,32,128,128]{3,2,1,0:T(8,128)(2,1)S(1)}, bf16[1,32,128,128]{3,2,1,0:T(8,128)(2,1)S(1)}) custom-call(s32[1024]{0:T(1024)S(1)} %reshape.228.idx_ref, s32[32]{0:T(128)S(1)} %reshape.229.order_ref, s32[2]{0:T(128)S(1)} %slice.38.count_ref, bf16[64,128,128]{2,1,0:T(8,128)(2,1)S(1)} %join.1.refs_0_, ...), custom_call_target="tpu_custom_call" | custom-call | flops 4294967296 | bytes 16777216 | tf_op jit(solution)/shard_map/products/pallas_call | solution.py:195
  97.0 2.9 %collective-permute-start.20 = (bf16[1,32,128,128]{3,2,1,0:T(8,128)(2,1)S(1)}, bf16[1,32,128,128]{3,2,1,0:T(8,128)(2,1)S(1)}, u32[]{:S(2)}, u32[]{:S(2)}) collective-permute-start(bf16[1,32,128,128]{3,2,1,0:T(8,128)(2,1)S(1)} %get-tuple-element.142), channel_id=1, source_target_pairs={{0,32},{1,225},{2,34},{3,227},{4,36},{5,229},{6,38},{7,231},{8,40}... | collective-permute-start | bytes 3145736 | tf_op jit(solution)/shard_map/ppermute | solution.py:32
  99.9 6.5 %collective-permute-done.21.refs_1_ = bf16[1,32,128,128]{3,2,1,0:T(8,128)(2,1)S(1)} collective-permute-done((bf16[1,32,128,128]{3,2,1,0:T(8,128)(2,1)S(1)}, bf16[1,32,128,128]{3,2,1,0:T(8,128)(2,1)S(1)}, u32[]{:S(2)}, u32[]{:S(2)}) %collective-permute-start.21) | collective-permute-done | bytes 1048608 | tf_op jit(solution)/shard_map/ppermute | solution.py:32
  106.4 0.3 plus.2
  106.8 4.5 %products.7.refs_0_ = bf16[1,32,128,128]{3,2,1,0:T(8,128)(2,1)S(1)} custom-call(s32[512]{0:T(512)S(1)} %reshape.230.idx_ref, s32[16]{0:T(128)S(1)} %get-tuple-element.108.order_ref, s32[1]{0:T(128)} %get-tuple-element.109.count_ref, bf16[64,128,128]{2,1,0:T(8,128)(2,1)S(1)} %join.1.refs_0_, bf16[64,128,128]{2,1,0:T(8,128)(2,1)S(1)} %collective-permute-done.11.up_ref.refs_1_, ...), custom_call_target="tpu_custom_call" | custom-call | flops 2147483648 | bytes 16777216 | tf_op jit(solution)/shard_map/products/pallas_call | solution.py:195
  111.3 6.5 %collective-permute-done.20.refs_1_ = bf16[1,32,128,128]{3,2,1,0:T(8,128)(2,1)S(1)} collective-permute-done((bf16[1,32,128,128]{3,2,1,0:T(8,128)(2,1)S(1)}, bf16[1,32,128,128]{3,2,1,0:T(8,128)(2,1)S(1)}, u32[]{:S(2)}, u32[]{:S(2)}) %collective-permute-start.20) | collective-permute-done | bytes 1048608 | tf_op jit(solution)/shard_map/ppermute | solution.py:32
  117.8 9.7 %collective-permute-done.22.refs_2_ = bf16[1,32,128,128]{3,2,1,0:T(8,128)(2,1)S(1)} collective-permute-done((bf16[1,32,128,128]{3,2,1,0:T(8,128)(2,1)S(1)}, bf16[1,32,128,128]{3,2,1,0:T(8,128)(2,1)S(1)}, u32[]{:S(2)}, u32[]{:S(2)}) %collective-permute-start.22) | collective-permute-done | bytes 1048608 | tf_op jit(solution)/shard_map/ppermute | solution.py:32
  127.6 1.4 %plus.3 = bf16[1,32,128,128]{3,2,1,0:T(8,128)(2,1)} custom-call(bf16[1,32,128,128]{3,2,1,0:T(8,128)(2,1)S(1)} %products.7.refs_0_, bf16[1,32,128,128]{3,2,1,0:T(8,128)(2,1)S(1)} %collective-permute-done.20.refs_1_, bf16[1,32,128,128]{3,2,1,0:T(8,128)(2,1)S(1)} %collective-permute-done.22.refs_2_), custom_call_target="tpu_custom_call" | custom-call | bytes 4194304 | tf_op jit(solution)/shard_map/plus/pallas_call | solution.py:231
  (50 shorter events, 1.8 us)
Async XLA Ops:
  0.0 12.1 %copy-start = (s32[8,1,32]{2,1,0:T(1,128)S(1)}, s32[8,1,32]{2,1,0:T(1,128)}, u32[]{:S(2)}) copy-start(s32[8,1,32]{2,1,0:T(1,128)} %param.6) | copy-start | bytes 3076
  0.0 19.6 %collective-permute-start.4 = (bf16[8,128,128]{2,1,0:T(8,128)(2,1)}, bf16[8,128,128]{2,1,0:T(8,128)(2,1)S(1)}, u32[]{:S(2)}, u32[]{:S(2)}) collective-permute-start(bf16[8,128,128]{2,1,0:T(8,128)(2,1)} %bitcast.12), channel_id=1, source_target_pairs={{0,128},{1,129},{2,130},{3,131},{4,132},{5,133},{6,134},{7,135},{8... | collective-permute-start | bytes 786440 | tf_op jit(solution)/shard_map/ppermute | solution.py:32
  7.7 11.9 %collective-permute-start.3 = (bf16[8,128,128]{2,1,0:T(8,128)(2,1)}, bf16[8,128,128]{2,1,0:T(8,128)(2,1)S(1)}, u32[]{:S(2)}, u32[]{:S(2)}) collective-permute-start(bf16[8,128,128]{2,1,0:T(8,128)(2,1)} %bitcast.13), channel_id=1, source_target_pairs={{0,4},{1,17},{2,6},{3,19},{4,0},{5,21},{6,2},{7,23},{8,12},{9,25},... | collective-permute-start | bytes 786440 | tf_op jit(solution)/shard_map/ppermute | solution.py:32
  10.7 9.0 %collective-permute-start.2 = (bf16[8,128,128]{2,1,0:T(8,128)(2,1)}, bf16[8,128,128]{2,1,0:T(8,128)(2,1)S(1)}, u32[]{:S(2)}, u32[]{:S(2)}) collective-permute-start(bf16[8,128,128]{2,1,0:T(8,128)(2,1)} %bitcast.14), channel_id=1, source_target_pairs={{0,6},{1,25},{2,0},{3,27},{4,2},{5,29},{6,4},{7,31},{8,14},{9,1},{... | collective-permute-start | bytes 786440 | tf_op jit(solution)/shard_map/ppermute | solution.py:32
  11.4 8.2 %collective-permute-start.1 = (bf16[8,128,128]{2,1,0:T(8,128)(2,1)}, bf16[8,128,128]{2,1,0:T(8,128)(2,1)S(1)}, u32[]{:S(2)}, u32[]{:S(2)}) collective-permute-start(bf16[8,128,128]{2,1,0:T(8,128)(2,1)} %bitcast.15), channel_id=1, source_target_pairs={{0,2},{1,9},{2,4},{3,11},{4,6},{5,13},{6,0},{7,15},{8,10},{9,17},{... | collective-permute-start | bytes 786440 | tf_op jit(solution)/shard_map/ppermute | solution.py:32
  12.9 6.7 %collective-permute-start = (s32[8,32]{1,0:T(8,128)}, s32[8,32]{1,0:T(8,128)S(1)}, u32[]{:S(2)}, u32[]{:S(2)}) collective-permute-start(s32[8,32]{1,0:T(8,128)} %param.8), channel_id=1, source_target_pairs={{0,128},{1,129},{2,130},{3,131},{4,132},{5,133},{6,134},{7,135},{8... | collective-permute-start | bytes 3080 | tf_op jit(solution)/shard_map/ppermute | solution.py:32
  15.8 1.2 copy-start.1
  19.6 10.7 %copy-start.2 = (bf16[8,128,128]{2,1,0:T(8,128)(2,1)}, bf16[8,128,128]{2,1,0:T(8,128)(2,1)S(1)}, u32[]{:S(2)}) copy-start(bf16[8,128,128]{2,1,0:T(8,128)(2,1)S(1)} %collective-permute-done.3.refs_3_) | copy-start | bytes 786436
  19.6 0.7 copy-start.3
  19.7 0.8 copy-start.4
  20.5 6.7 %collective-permute-start.7 = (bf16[8,128,128]{2,1,0:T(8,128)(2,1)S(1)}, bf16[8,128,128]{2,1,0:T(8,128)(2,1)S(1)}, u32[]{:S(2)}, u32[]{:S(2)}) collective-permute-start(bf16[8,128,128]{2,1,0:T(8,128)(2,1)S(1)} %collective-permute-done.4.refs_4_), channel_id=1, source_target_pairs={{0,4},{1,17},{2,6},{3,19},{4,0},{5,21},{6,2},{7,23},{8,12},{9,25},... | collective-permute-start | bytes 786440 | tf_op jit(solution)/shard_map/ppermute | solution.py:32
  21.4 8.9 %collective-permute-start.6 = (bf16[8,128,128]{2,1,0:T(8,128)(2,1)S(1)}, bf16[8,128,128]{2,1,0:T(8,128)(2,1)S(1)}, u32[]{:S(2)}, u32[]{:S(2)}) collective-permute-start(bf16[8,128,128]{2,1,0:T(8,128)(2,1)S(1)} %collective-permute-done.4.refs_4_), channel_id=1, source_target_pairs={{0,6},{1,25},{2,0},{3,27},{4,2},{5,29},{6,4},{7,31},{8,14},{9,1},{... | collective-permute-start | bytes 786440 | tf_op jit(solution)/shard_map/ppermute | solution.py:32
  23.6 6.7 %collective-permute-start.5 = (bf16[8,128,128]{2,1,0:T(8,128)(2,1)S(1)}, bf16[8,128,128]{2,1,0:T(8,128)(2,1)S(1)}, u32[]{:S(2)}, u32[]{:S(2)}) collective-permute-start(bf16[8,128,128]{2,1,0:T(8,128)(2,1)S(1)} %collective-permute-done.4.refs_4_), channel_id=1, source_target_pairs={{0,2},{1,9},{2,4},{3,11},{4,6},{5,13},{6,0},{7,15},{8,10},{9,17},{... | collective-permute-start | bytes 786440 | tf_op jit(solution)/shard_map/ppermute | solution.py:32
  31.6 28.5 %collective-permute-start.10 = (bf16[64,128,128]{2,1,0:T(8,128)(2,1)S(1)}, bf16[64,128,128]{2,1,0:T(8,128)(2,1)S(1)}, u32[]{:S(2)}, u32[]{:S(2)}) collective-permute-start(bf16[64,128,128]{2,1,0:T(8,128)(2,1)S(1)} %join.1.refs_0_), channel_id=1, source_target_pairs={{0,1},{1,0},{2,3},{3,2},{4,5},{5,4},{6,7},{7,6},{8,9},{9,8},{10,11... | collective-permute-start | bytes 6291464 | tf_op jit(solution)/shard_map/ppermute | solution.py:32
  35.5 25.2 %collective-permute-start.12 = (bf16[64,128,128]{2,1,0:T(8,128)(2,1)S(1)}, bf16[64,128,128]{2,1,0:T(8,128)(2,1)S(1)}, u32[]{:S(2)}, u32[]{:S(2)}) collective-permute-start(bf16[64,128,128]{2,1,0:T(8,128)(2,1)S(1)} %join.1.refs_0_), channel_id=1, source_target_pairs={{0,24},{1,7},{2,26},{3,1},{4,28},{5,3},{6,30},{7,5},{8,0},{9,15},{... | collective-permute-start | bytes 6291464 | tf_op jit(solution)/shard_map/ppermute | solution.py:32
  37.6 26.4 %collective-permute-start.11 = (bf16[64,128,128]{2,1,0:T(8,128)(2,1)S(1)}, bf16[64,128,128]{2,1,0:T(8,128)(2,1)S(1)}, u32[]{:S(2)}, u32[]{:S(2)}) collective-permute-start(bf16[64,128,128]{2,1,0:T(8,128)(2,1)S(1)} %join.1.refs_0_), channel_id=1, source_target_pairs={{0,8},{1,3},{2,10},{3,5},{4,12},{5,7},{6,14},{7,1},{8,16},{9,11},{... | collective-permute-start | bytes 6291464 | tf_op jit(solution)/shard_map/ppermute | solution.py:32
  37.6 19.5 %collective-permute-start.8 = (bf16[16,128,128]{2,1,0:T(8,128)(2,1)S(1)}, bf16[16,128,128]{2,1,0:T(8,128)(2,1)S(1)}, u32[]{:S(2)}, u32[]{:S(2)}) collective-permute-start(bf16[16,128,128]{2,1,0:T(8,128)(2,1)S(1)} %get-tuple-element.103), channel_id=1, source_target_pairs={{0,64},{1,193},{2,66},{3,195},{4,68},{5,197},{6,70},{7,199},{8,72}... | collective-permute-start | bytes 1572872 | tf_op jit(solution)/shard_map/ppermute | solution.py:32
  40.8 19.3 %collective-permute-start.9 = (bf16[16,128,128]{2,1,0:T(8,128)(2,1)S(1)}, bf16[16,128,128]{2,1,0:T(8,128)(2,1)S(1)}, u32[]{:S(2)}, u32[]{:S(2)}) collective-permute-start(bf16[16,128,128]{2,1,0:T(8,128)(2,1)S(1)} %get-tuple-element.104), channel_id=1, source_target_pairs={{0,224},{1,33},{2,226},{3,35},{4,228},{5,37},{6,230},{7,39},{8,232... | collective-permute-start | bytes 1572872 | tf_op jit(solution)/shard_map/ppermute | solution.py:32
  64.2 7.2 %collective-permute-start.13 = (bf16[64,128,128]{2,1,0:T(8,128)(2,1)S(1)}, bf16[64,128,128]{2,1,0:T(8,128)(2,1)S(1)}, u32[]{:S(2)}, u32[]{:S(2)}) collective-permute-start(bf16[64,128,128]{2,1,0:T(8,128)(2,1)S(1)} %collective-permute-done.11.up_ref.refs_1_), channel_id=1, source_target_pairs={{0,1},{1,0},{2,3},{3,2},{4,5},{5,4},{6,7},{7,6},{8,9},{9,8},{10,11... | collective-permute-start | bytes 6291464 | tf_op jit(solution)/shard_map/ppermute | solution.py:32
  66.1 6.8 %collective-permute-start.14 = (bf16[64,128,128]{2,1,0:T(8,128)(2,1)S(1)}, bf16[64,128,128]{2,1,0:T(8,128)(2,1)S(1)}, u32[]{:S(2)}, u32[]{:S(2)}) collective-permute-start(bf16[64,128,128]{2,1,0:T(8,128)(2,1)S(1)} %collective-permute-done.12.down_ref.refs_2_), channel_id=1, source_target_pairs={{0,1},{1,0},{2,3},{3,2},{4,5},{5,4},{6,7},{7,6},{8,9},{9,8},{10,11... | collective-permute-start | bytes 6291464 | tf_op jit(solution)/shard_map/ppermute | solution.py:32
  66.2 15.2 %collective-permute-start.16 = (bf16[32,128,128]{2,1,0:T(8,128)(2,1)S(1)}, bf16[32,128,128]{2,1,0:T(8,128)(2,1)S(1)}, u32[]{:S(2)}, u32[]{:S(2)}) collective-permute-start(bf16[32,128,128]{2,1,0:T(8,128)(2,1)S(1)} %get-tuple-element.120), channel_id=1, source_target_pairs={{0,8},{1,3},{2,10},{3,5},{4,12},{5,7},{6,14},{7,1},{8,16},{9,11},{... | collective-permute-start | bytes 3145736 | tf_op jit(solution)/shard_map/ppermute | solution.py:32
  66.2 15.2 %collective-permute-start.17 = (bf16[32,128,128]{2,1,0:T(8,128)(2,1)S(1)}, bf16[32,128,128]{2,1,0:T(8,128)(2,1)S(1)}, u32[]{:S(2)}, u32[]{:S(2)}) collective-permute-start(bf16[32,128,128]{2,1,0:T(8,128)(2,1)S(1)} %get-tuple-element.121), channel_id=1, source_target_pairs={{0,24},{1,7},{2,26},{3,1},{4,28},{5,3},{6,30},{7,5},{8,0},{9,15},{... | collective-permute-start | bytes 3145736 | tf_op jit(solution)/shard_map/ppermute | solution.py:32
  68.9 8.6 %collective-permute-start.15 = (bf16[16,128,128]{2,1,0:T(8,128)(2,1)S(1)}, bf16[16,128,128]{2,1,0:T(8,128)(2,1)S(1)}, u32[]{:S(2)}, u32[]{:S(2)}) collective-permute-start(bf16[16,128,128]{2,1,0:T(8,128)(2,1)S(1)} %get-tuple-element.119), channel_id=1, source_target_pairs={{0,32},{1,225},{2,34},{3,227},{4,36},{5,229},{6,38},{7,231},{8,40}... | collective-permute-start | bytes 1572872 | tf_op jit(solution)/shard_map/ppermute | solution.py:32
  81.4 3.6 %collective-permute-start.18 = (bf16[32,128,128]{2,1,0:T(8,128)(2,1)S(1)}, bf16[32,128,128]{2,1,0:T(8,128)(2,1)S(1)}, u32[]{:S(2)}, u32[]{:S(2)}) collective-permute-start(bf16[32,128,128]{2,1,0:T(8,128)(2,1)S(1)} %collective-permute-done.16.refs_0_.refs_6_), channel_id=1, source_target_pairs={{0,1},{1,0},{2,3},{3,2},{4,5},{5,4},{6,7},{7,6},{8,9},{9,8},{10,11... | collective-permute-start | bytes 3145736 | tf_op jit(solution)/shard_map/ppermute | solution.py:32
  82.7 3.8 %collective-permute-start.19 = (bf16[32,128,128]{2,1,0:T(8,128)(2,1)S(1)}, bf16[32,128,128]{2,1,0:T(8,128)(2,1)S(1)}, u32[]{:S(2)}, u32[]{:S(2)}) collective-permute-start(bf16[32,128,128]{2,1,0:T(8,128)(2,1)S(1)} %collective-permute-done.17.refs_1_.refs_7_), channel_id=1, source_target_pairs={{0,1},{1,0},{2,3},{3,2},{4,5},{5,4},{6,7},{7,6},{8,9},{9,8},{10,11... | collective-permute-start | bytes 3145736 | tf_op jit(solution)/shard_map/ppermute | solution.py:32
  89.4 17.0 %collective-permute-start.21 = (bf16[1,32,128,128]{3,2,1,0:T(8,128)(2,1)S(1)}, bf16[1,32,128,128]{3,2,1,0:T(8,128)(2,1)S(1)}, u32[]{:S(2)}, u32[]{:S(2)}) collective-permute-start(bf16[1,32,128,128]{3,2,1,0:T(8,128)(2,1)S(1)} %products.5), channel_id=1, source_target_pairs={{0,224},{1,33},{2,226},{3,35},{4,228},{5,37},{6,230},{7,39},{8,232... | collective-permute-start | bytes 3145736 | tf_op jit(solution)/shard_map/ppermute | solution.py:32
  97.0 20.8 %collective-permute-start.20 = (bf16[1,32,128,128]{3,2,1,0:T(8,128)(2,1)S(1)}, bf16[1,32,128,128]{3,2,1,0:T(8,128)(2,1)S(1)}, u32[]{:S(2)}, u32[]{:S(2)}) collective-permute-start(bf16[1,32,128,128]{3,2,1,0:T(8,128)(2,1)S(1)} %get-tuple-element.142), channel_id=1, source_target_pairs={{0,32},{1,225},{2,34},{3,227},{4,36},{5,229},{6,38},{7,231},{8,40}... | collective-permute-start | bytes 3145736 | tf_op jit(solution)/shard_map/ppermute | solution.py:32
  106.7 20.9 %collective-permute-start.22 = (bf16[1,32,128,128]{3,2,1,0:T(8,128)(2,1)S(1)}, bf16[1,32,128,128]{3,2,1,0:T(8,128)(2,1)S(1)}, u32[]{:S(2)}, u32[]{:S(2)}) collective-permute-start(bf16[1,32,128,128]{3,2,1,0:T(8,128)(2,1)S(1)} %plus.2), channel_id=1, source_target_pairs={{0,224},{1,33},{2,226},{3,35},{4,228},{5,37},{6,230},{7,39},{8,232... | collective-permute-start | bytes 3145736 | tf_op jit(solution)/shard_map/ppermute | solution.py:32

commit v5 on v4

--- a/solution.py
+++ b/solution.py
@@ -277,9 +277,6 @@
     )
     far_l, near_l, leaf_l, own_l = picked
     far_l = along_z(far_l, 2)
-    far_ring, leaf_l = stage(round_one(far_set), leaf_l)
-    first = join((blocks, *near_ring), (far_set, *far_ring))
-
     steps = jnp.array(OFFSETS, dtype=jnp.int32)
     cols = cols_here[(z - steps * sign + NZ) % NZ]
     slot = jnp.arange(KEPT, dtype=jnp.int32)
@@ -313,12 +310,13 @@
 
     tables = entry(idx_early, 0, 1), entry(idx_late, 0, 1), entry(idx, 1, 3), entry(idx, 3, 4)
 
-    tables, ready = stage(tables, first)
+    far_ring, leaf_l, tables = stage(round_one(far_set), leaf_l, tables)
+    first = join((blocks, *near_ring), (far_set, *far_ring))
     tables, far_l, leaf_l, first_got, first, up, down, near_l = stage(
         tables,
         far_l,
         along_z(leaf_l, -1),
-        swap(ready),
+        swap(first),
         first,
         in_plane(first, 1, 1),
         in_plane(first, -1, 1),

time: 129 us -> 129 us (level)
  waiting for transfers between devices: 62.5 us -> 57 us
  starting transfers between devices: 37.2 us -> 41.4 us
  Pallas kernels: 21 us -> 22.5 us
    ppermute x23, waiting for transfers between devices: 62.5 us -> 57 us  [send(): return lax.ppermute(block, AXES, pairs)]
    ppermute x23, starting transfers between devices: 37.2 us -> 41.4 us  [send(): return lax.ppermute(block, AXES, pairs)]
    pallas_call x4, Pallas kernels: 17.3 us -> 18.7 us  [products(): pl.pallas_call(functools.partial(products_kernel, len(panel_parts), n, le...]
  transfers between devices with their start and end apart: 23 -> 23, of which waited for: 16 -> 15; matrix products, arithmetic and copies ran while one was open for 5% -> 5% of each run, Pallas kernels for 12% -> 12%
where the time goes in v5:
time: 129 us
  waiting for transfers between devices  57 us (44%)
  starting transfers between devices  41.4 us (32%)
  Pallas kernels  22.5 us (17%)
  other arithmetic  4.34 us (3%)
  local copies, waits for them, and re-layouts  3.68 us (3%)
    ppermute x23, waiting for transfers between devices, send(): return lax.ppermute(block, AXES, pairs)  57 us
    ppermute x23, starting transfers between devices, send(): return lax.ppermute(block, AXES, pairs)  41.4 us
    pallas_call x4, Pallas kernels, products(): pl.pallas_call(functools.partial(products_kernel, len(panel_parts), n, le...  18.7 us
  transfers between devices with their start and end apart: 23, of which 15 were waited for; matrix products, arithmetic and copies ran while one was open for 5% of the time, Pallas kernels for 12%

profile of v5, /device:TPU:1, one launch (start us, length us, event | category | flops | bytes accessed | tf_op | source)
XLA Modules:
  0.0 129.1 jit_solution(16307418543612173393)
XLA Ops:
  0.0 7.7 %collective-permute-start.4 = (bf16[8,128,128]{2,1,0:T(8,128)(2,1)}, bf16[8,128,128]{2,1,0:T(8,128)(2,1)S(1)}, u32[]{:S(2)}, u32[]{:S(2)}) collective-permute-start(bf16[8,128,128]{2,1,0:T(8,128)(2,1)} %bitcast.12), channel_id=1, source_target_pairs={{0,128},{1,129},{2,130},{3,131},{4,132},{5,133},{6,134},{7,135},{8... | collective-permute-start | bytes 786440 | tf_op jit(solution)/shard_map/ppermute | solution.py:32
  7.7 2.9 %collective-permute-start.3 = (bf16[8,128,128]{2,1,0:T(8,128)(2,1)}, bf16[8,128,128]{2,1,0:T(8,128)(2,1)S(1)}, u32[]{:S(2)}, u32[]{:S(2)}) collective-permute-start(bf16[8,128,128]{2,1,0:T(8,128)(2,1)} %bitcast.13), channel_id=1, source_target_pairs={{0,4},{1,17},{2,6},{3,19},{4,0},{5,21},{6,2},{7,23},{8,12},{9,25},... | collective-permute-start | bytes 786440 | tf_op jit(solution)/shard_map/ppermute | solution.py:32
  10.7 0.8 collective-permute-start.2
  11.4 0.7 collective-permute-start.1
  12.3 0.6 iota_reduce_fusion
  13.0 0.7 compare_select_fusion.1
  13.7 0.6 gather_fusion
  14.2 0.2 compare_reduce_fusion
  15.0 0.6 fusion.29
  15.8 1.2 copy-done.1
  17.0 0.7 pick.1
  17.7 1.9 %collective-permute-done = s32[8,32]{1,0:T(8,128)S(1)} collective-permute-done((s32[8,32]{1,0:T(8,128)}, s32[8,32]{1,0:T(8,128)S(1)}, u32[]{:S(2)}, u32[]{:S(2)}) %collective-permute-start) | collective-permute-done | bytes 1056 | tf_op jit(solution)/shard_map/ppermute | solution.py:32
  19.7 0.7 copy-done.3
  20.5 0.9 collective-permute-start.7
  21.4 2.2 %collective-permute-start.6 = (bf16[8,128,128]{2,1,0:T(8,128)(2,1)S(1)}, bf16[8,128,128]{2,1,0:T(8,128)(2,1)S(1)}, u32[]{:S(2)}, u32[]{:S(2)}) collective-permute-start(bf16[8,128,128]{2,1,0:T(8,128)(2,1)S(1)} %collective-permute-done.4.refs_4_), channel_id=1, source_target_pairs={{0,6},{1,25},{2,0},{3,27},{4,2},{5,29},{6,4},{7,31},{8,14},{9,1},{... | collective-permute-start | bytes 786440 | tf_op jit(solution)/shard_map/ppermute | solution.py:32
  23.6 0.7 pad_add_fusion
  24.3 1.2 select_reduce_fusion
  25.5 0.2 select_reduce_fusion.1
  26.1 1.1 collective-permute-done.7.refs_7_
  27.2 3.1 %collective-permute-done.6.refs_6_ = bf16[8,128,128]{2,1,0:T(8,128)(2,1)S(1)} collective-permute-done((bf16[8,128,128]{2,1,0:T(8,128)(2,1)S(1)}, bf16[8,128,128]{2,1,0:T(8,128)(2,1)S(1)}, u32[]{:S(2)}, u32[]{:S(2)}) %collective-permute-start.6) | collective-permute-done | bytes 262176 | tf_op jit(solution)/shard_map/ppermute | solution.py:32
  30.3 1.3 join.1.refs_0_
  31.6 2.6 %collective-permute-start.12 = (bf16[64,128,128]{2,1,0:T(8,128)(2,1)S(1)}, bf16[64,128,128]{2,1,0:T(8,128)(2,1)S(1)}, u32[]{:S(2)}, u32[]{:S(2)}) collective-permute-start(bf16[64,128,128]{2,1,0:T(8,128)(2,1)S(1)} %join.1.refs_0_), channel_id=1, source_target_pairs={{0,24},{1,7},{2,26},{3,1},{4,28},{5,3},{6,30},{7,5},{8,0},{9,15},{... | collective-permute-start | bytes 6291464 | tf_op jit(solution)/shard_map/ppermute | solution.py:32
  34.2 4.4 %collective-permute-start.10 = (bf16[64,128,128]{2,1,0:T(8,128)(2,1)S(1)}, bf16[64,128,128]{2,1,0:T(8,128)(2,1)S(1)}, u32[]{:S(2)}, u32[]{:S(2)}) collective-permute-start(bf16[64,128,128]{2,1,0:T(8,128)(2,1)S(1)} %join.1.refs_0_), channel_id=1, source_target_pairs={{0,1},{1,0},{2,3},{3,2},{4,5},{5,4},{6,7},{7,6},{8,9},{9,8},{10,11... | collective-permute-start | bytes 6291464 | tf_op jit(solution)/shard_map/ppermute | solution.py:32
  38.5 3.8 %collective-permute-start.8 = (bf16[16,128,128]{2,1,0:T(8,128)(2,1)S(1)}, bf16[16,128,128]{2,1,0:T(8,128)(2,1)S(1)}, u32[]{:S(2)}, u32[]{:S(2)}) collective-permute-start(bf16[16,128,128]{2,1,0:T(8,128)(2,1)S(1)} %get-tuple-element.96), channel_id=1, source_target_pairs={{0,64},{1,193},{2,66},{3,195},{4,68},{5,197},{6,70},{7,199},{8,72}... | collective-permute-start | bytes 1572872 | tf_op jit(solution)/shard_map/ppermute | solution.py:32
  42.3 17.1 %collective-permute-done.8.refs_6_.refs_4_ = bf16[16,128,128]{2,1,0:T(8,128)(2,1)S(1)} collective-permute-done((bf16[16,128,128]{2,1,0:T(8,128)(2,1)S(1)}, bf16[16,128,128]{2,1,0:T(8,128)(2,1)S(1)}, u32[]{:S(2)}, u32[]{:S(2)}) %collective-permute-start.8) | collective-permute-done | bytes 524320 | tf_op jit(solution)/shard_map/ppermute | solution.py:32
  59.4 0.6 collective-permute-done.9.refs_11_
  60.0 0.5 collective-permute-done.11.up_ref.refs_1_
  60.5 0.2 halves.1
  60.7 5.3 %collective-permute-start.13 = (bf16[64,128,128]{2,1,0:T(8,128)(2,1)S(1)}, bf16[64,128,128]{2,1,0:T(8,128)(2,1)S(1)}, u32[]{:S(2)}, u32[]{:S(2)}) collective-permute-start(bf16[64,128,128]{2,1,0:T(8,128)(2,1)S(1)} %collective-permute-done.11.up_ref.refs_1_), channel_id=1, source_target_pairs={{0,1},{1,0},{2,3},{3,2},{4,5},{5,4},{6,7},{7,6},{8,9},{9,8},{10,11... | collective-permute-start | bytes 6291464 | tf_op jit(solution)/shard_map/ppermute | solution.py:32
  66.2 2.7 %collective-permute-start.17 = (bf16[32,128,128]{2,1,0:T(8,128)(2,1)S(1)}, bf16[32,128,128]{2,1,0:T(8,128)(2,1)S(1)}, u32[]{:S(2)}, u32[]{:S(2)}) collective-permute-start(bf16[32,128,128]{2,1,0:T(8,128)(2,1)S(1)} %get-tuple-element.119), channel_id=1, source_target_pairs={{0,24},{1,7},{2,26},{3,1},{4,28},{5,3},{6,30},{7,5},{8,0},{9,15},{... | collective-permute-start | bytes 3145736 | tf_op jit(solution)/shard_map/ppermute | solution.py:32
  68.8 2.4 %collective-permute-start.15 = (bf16[16,128,128]{2,1,0:T(8,128)(2,1)S(1)}, bf16[16,128,128]{2,1,0:T(8,128)(2,1)S(1)}, u32[]{:S(2)}, u32[]{:S(2)}) collective-permute-start(bf16[16,128,128]{2,1,0:T(8,128)(2,1)S(1)} %get-tuple-element.117), channel_id=1, source_target_pairs={{0,32},{1,225},{2,34},{3,227},{4,36},{5,229},{6,38},{7,231},{8,40}... | collective-permute-start | bytes 1572872 | tf_op jit(solution)/shard_map/ppermute | solution.py:32
  71.3 1.6 %collective-permute-done.14.refs_5_ = bf16[64,128,128]{2,1,0:T(8,128)(2,1)S(1)} collective-permute-done((bf16[64,128,128]{2,1,0:T(8,128)(2,1)S(1)}, bf16[64,128,128]{2,1,0:T(8,128)(2,1)S(1)}, u32[]{:S(2)}, u32[]{:S(2)}) %collective-permute-start.14) | collective-permute-done | bytes 2097184 | tf_op jit(solution)/shard_map/ppermute | solution.py:32
  72.8 4.2 %products.4.refs_5_ = bf16[1,32,128,128]{3,2,1,0:T(8,128)(2,1)S(1)} custom-call(s32[512]{0:T(512)S(1)} %reshape.225.idx_ref, s32[16]{0:T(128)S(1)} %get-tuple-element.135.order_ref, s32[1]{0:T(128)} %get-tuple-element.136.count_ref, bf16[64,128,128]{2,1,0:T(8,128)(2,1)S(1)} %join.1.refs_0_, bf16[64,128,128]{2,1,0:T(8,128)(2,1)S(1)} %collective-permute-done.11.up_ref.refs_1_, ...), custom_call_target="tpu_custom_call" | custom-call | flops 2147483648 | bytes 12582912 | tf_op jit(solution)/shard_map/products/pallas_call | solution.py:195
  77.1 0.3 collective-permute-done.15.refs_10_
  77.4 3.9 %collective-permute-done.16.refs_0_.refs_6_ = bf16[32,128,128]{2,1,0:T(8,128)(2,1)S(1)} collective-permute-done((bf16[32,128,128]{2,1,0:T(8,128)(2,1)S(1)}, bf16[32,128,128]{2,1,0:T(8,128)(2,1)S(1)}, u32[]{:S(2)}, u32[]{:S(2)}) %collective-permute-start.16) | collective-permute-done | bytes 1048608 | tf_op jit(solution)/shard_map/ppermute | solution.py:32
  81.3 1.3 collective-permute-start.18
  82.6 2.3 %collective-permute-done.18.refs_2_.refs_8_ = bf16[32,128,128]{2,1,0:T(8,128)(2,1)S(1)} collective-permute-done((bf16[32,128,128]{2,1,0:T(8,128)(2,1)S(1)}, bf16[32,128,128]{2,1,0:T(8,128)(2,1)S(1)}, u32[]{:S(2)}, u32[]{:S(2)}) %collective-permute-start.18) | collective-permute-done | bytes 1048608 | tf_op jit(solution)/shard_map/ppermute | solution.py:32
  84.9 1.5 %collective-permute-done.19.refs_3_.refs_9_ = bf16[32,128,128]{2,1,0:T(8,128)(2,1)S(1)} collective-permute-done((bf16[32,128,128]{2,1,0:T(8,128)(2,1)S(1)}, bf16[32,128,128]{2,1,0:T(8,128)(2,1)S(1)}, u32[]{:S(2)}, u32[]{:S(2)}) %collective-permute-start.19) | collective-permute-done | bytes 1048608 | tf_op jit(solution)/shard_map/ppermute | solution.py:32
  86.4 3.7 %products.5 = bf16[1,32,128,128]{3,2,1,0:T(8,128)(2,1)S(1)} custom-call(s32[512]{0:T(512)S(1)} %reshape.227.idx_ref, s32[16]{0:T(128)S(1)} %get-tuple-element.135.order_ref, s32[1]{0:T(128)} %get-tuple-element.136.count_ref, bf16[32,128,128]{2,1,0:T(8,128)(2,1)S(1)} %collective-permute-done.16.refs_0_.refs_6_, ...), custom_call_target="tpu_custom_call" | custom-call | flops 2147483648 | bytes 4194304 | tf_op jit(solution)/shard_map/products/pallas_call | solution.py:195
  90.0 0.8 collective-permute-start.21
  90.9 6.3 %products.6 = (bf16[1,32,128,128]{3,2,1,0:T(8,128)(2,1)S(1)}, bf16[1,32,128,128]{3,2,1,0:T(8,128)(2,1)S(1)}) custom-call(s32[1024]{0:T(1024)S(1)} %reshape.228.idx_ref, s32[32]{0:T(128)S(1)} %reshape.229.order_ref, s32[2]{0:T(128)S(1)} %slice.38.count_ref, bf16[64,128,128]{2,1,0:T(8,128)(2,1)S(1)} %join.1.refs_0_, ...), custom_call_target="tpu_custom_call" | custom-call | flops 4294967296 | bytes 16777216 | tf_op jit(solution)/shard_map/products/pallas_call | solution.py:195
  97.2 2.6 %collective-permute-start.20 = (bf16[1,32,128,128]{3,2,1,0:T(8,128)(2,1)S(1)}, bf16[1,32,128,128]{3,2,1,0:T(8,128)(2,1)S(1)}, u32[]{:S(2)}, u32[]{:S(2)}) collective-permute-start(bf16[1,32,128,128]{3,2,1,0:T(8,128)(2,1)S(1)} %get-tuple-element.140), channel_id=1, source_target_pairs={{0,32},{1,225},{2,34},{3,227},{4,36},{5,229},{6,38},{7,231},{8,40}... | collective-permute-start | bytes 3145736 | tf_op jit(solution)/shard_map/ppermute | solution.py:32
  99.8 7.6 %collective-permute-done.21.refs_1_ = bf16[1,32,128,128]{3,2,1,0:T(8,128)(2,1)S(1)} collective-permute-done((bf16[1,32,128,128]{3,2,1,0:T(8,128)(2,1)S(1)}, bf16[1,32,128,128]{3,2,1,0:T(8,128)(2,1)S(1)}, u32[]{:S(2)}, u32[]{:S(2)}) %collective-permute-start.21) | collective-permute-done | bytes 1048608 | tf_op jit(solution)/shard_map/ppermute | solution.py:32
  107.4 0.3 plus.2
  107.8 4.5 %products.7.refs_0_ = bf16[1,32,128,128]{3,2,1,0:T(8,128)(2,1)S(1)} custom-call(s32[512]{0:T(512)S(1)} %reshape.230.idx_ref, s32[16]{0:T(128)S(1)} %get-tuple-element.106.order_ref, s32[1]{0:T(128)} %get-tuple-element.107.count_ref, bf16[64,128,128]{2,1,0:T(8,128)(2,1)S(1)} %join.1.refs_0_, bf16[64,128,128]{2,1,0:T(8,128)(2,1)S(1)} %collective-permute-done.11.up_ref.refs_1_, ...), custom_call_target="tpu_custom_call" | custom-call | flops 2147483648 | bytes 16777216 | tf_op jit(solution)/shard_map/products/pallas_call | solution.py:195
  112.4 5.9 %collective-permute-done.20.refs_1_ = bf16[1,32,128,128]{3,2,1,0:T(8,128)(2,1)S(1)} collective-permute-done((bf16[1,32,128,128]{3,2,1,0:T(8,128)(2,1)S(1)}, bf16[1,32,128,128]{3,2,1,0:T(8,128)(2,1)S(1)}, u32[]{:S(2)}, u32[]{:S(2)}) %collective-permute-start.20) | collective-permute-done | bytes 1048608 | tf_op jit(solution)/shard_map/ppermute | solution.py:32
  118.3 9.5 %collective-permute-done.22.refs_2_ = bf16[1,32,128,128]{3,2,1,0:T(8,128)(2,1)S(1)} collective-permute-done((bf16[1,32,128,128]{3,2,1,0:T(8,128)(2,1)S(1)}, bf16[1,32,128,128]{3,2,1,0:T(8,128)(2,1)S(1)}, u32[]{:S(2)}, u32[]{:S(2)}) %collective-permute-start.22) | collective-permute-done | bytes 1048608 | tf_op jit(solution)/shard_map/ppermute | solution.py:32
  127.7 1.4 %plus.3 = bf16[1,32,128,128]{3,2,1,0:T(8,128)(2,1)} custom-call(bf16[1,32,128,128]{3,2,1,0:T(8,128)(2,1)S(1)} %products.7.refs_0_, bf16[1,32,128,128]{3,2,1,0:T(8,128)(2,1)S(1)} %collective-permute-done.20.refs_1_, bf16[1,32,128,128]{3,2,1,0:T(8,128)(2,1)S(1)} %collective-permute-done.22.refs_2_), custom_call_target="tpu_custom_call" | custom-call | bytes 4194304 | tf_op jit(solution)/shard_map/plus/pallas_call | solution.py:231
  (50 shorter events, 1.7 us)
Async XLA Ops:
  0.0 12.1 %copy-start = (s32[8,1,32]{2,1,0:T(1,128)S(1)}, s32[8,1,32]{2,1,0:T(1,128)}, u32[]{:S(2)}) copy-start(s32[8,1,32]{2,1,0:T(1,128)} %param.6) | copy-start | bytes 3076
  0.0 19.6 %collective-permute-start.4 = (bf16[8,128,128]{2,1,0:T(8,128)(2,1)}, bf16[8,128,128]{2,1,0:T(8,128)(2,1)S(1)}, u32[]{:S(2)}, u32[]{:S(2)}) collective-permute-start(bf16[8,128,128]{2,1,0:T(8,128)(2,1)} %bitcast.12), channel_id=1, source_target_pairs={{0,128},{1,129},{2,130},{3,131},{4,132},{5,133},{6,134},{7,135},{8... | collective-permute-start | bytes 786440 | tf_op jit(solution)/shard_map/ppermute | solution.py:32
  7.7 11.9 %collective-permute-start.3 = (bf16[8,128,128]{2,1,0:T(8,128)(2,1)}, bf16[8,128,128]{2,1,0:T(8,128)(2,1)S(1)}, u32[]{:S(2)}, u32[]{:S(2)}) collective-permute-start(bf16[8,128,128]{2,1,0:T(8,128)(2,1)} %bitcast.13), channel_id=1, source_target_pairs={{0,4},{1,17},{2,6},{3,19},{4,0},{5,21},{6,2},{7,23},{8,12},{9,25},... | collective-permute-start | bytes 786440 | tf_op jit(solution)/shard_map/ppermute | solution.py:32
  10.7 9.0 %collective-permute-start.2 = (bf16[8,128,128]{2,1,0:T(8,128)(2,1)}, bf16[8,128,128]{2,1,0:T(8,128)(2,1)S(1)}, u32[]{:S(2)}, u32[]{:S(2)}) collective-permute-start(bf16[8,128,128]{2,1,0:T(8,128)(2,1)} %bitcast.14), channel_id=1, source_target_pairs={{0,6},{1,25},{2,0},{3,27},{4,2},{5,29},{6,4},{7,31},{8,14},{9,1},{... | collective-permute-start | bytes 786440 | tf_op jit(solution)/shard_map/ppermute | solution.py:32
  11.4 8.2 %collective-permute-start.1 = (bf16[8,128,128]{2,1,0:T(8,128)(2,1)}, bf16[8,128,128]{2,1,0:T(8,128)(2,1)S(1)}, u32[]{:S(2)}, u32[]{:S(2)}) collective-permute-start(bf16[8,128,128]{2,1,0:T(8,128)(2,1)} %bitcast.15), channel_id=1, source_target_pairs={{0,2},{1,9},{2,4},{3,11},{4,6},{5,13},{6,0},{7,15},{8,10},{9,17},{... | collective-permute-start | bytes 786440 | tf_op jit(solution)/shard_map/ppermute | solution.py:32
  12.9 6.7 %collective-permute-start = (s32[8,32]{1,0:T(8,128)}, s32[8,32]{1,0:T(8,128)S(1)}, u32[]{:S(2)}, u32[]{:S(2)}) collective-permute-start(s32[8,32]{1,0:T(8,128)} %param.8), channel_id=1, source_target_pairs={{0,128},{1,129},{2,130},{3,131},{4,132},{5,133},{6,134},{7,135},{8... | collective-permute-start | bytes 3080 | tf_op jit(solution)/shard_map/ppermute | solution.py:32
  15.8 1.2 copy-start.1
  19.6 10.7 %copy-start.2 = (bf16[8,128,128]{2,1,0:T(8,128)(2,1)}, bf16[8,128,128]{2,1,0:T(8,128)(2,1)S(1)}, u32[]{:S(2)}) copy-start(bf16[8,128,128]{2,1,0:T(8,128)(2,1)S(1)} %collective-permute-done.3.refs_3_) | copy-start | bytes 786436
  19.6 0.7 copy-start.3
  19.7 0.8 copy-start.4
  20.5 6.7 %collective-permute-start.7 = (bf16[8,128,128]{2,1,0:T(8,128)(2,1)S(1)}, bf16[8,128,128]{2,1,0:T(8,128)(2,1)S(1)}, u32[]{:S(2)}, u32[]{:S(2)}) collective-permute-start(bf16[8,128,128]{2,1,0:T(8,128)(2,1)S(1)} %collective-permute-done.4.refs_4_), channel_id=1, source_target_pairs={{0,4},{1,17},{2,6},{3,19},{4,0},{5,21},{6,2},{7,23},{8,12},{9,25},... | collective-permute-start | bytes 786440 | tf_op jit(solution)/shard_map/ppermute | solution.py:32
  21.4 8.9 %collective-permute-start.6 = (bf16[8,128,128]{2,1,0:T(8,128)(2,1)S(1)}, bf16[8,128,128]{2,1,0:T(8,128)(2,1)S(1)}, u32[]{:S(2)}, u32[]{:S(2)}) collective-permute-start(bf16[8,128,128]{2,1,0:T(8,128)(2,1)S(1)} %collective-permute-done.4.refs_4_), channel_id=1, source_target_pairs={{0,6},{1,25},{2,0},{3,27},{4,2},{5,29},{6,4},{7,31},{8,14},{9,1},{... | collective-permute-start | bytes 786440 | tf_op jit(solution)/shard_map/ppermute | solution.py:32
  23.6 6.7 %collective-permute-start.5 = (bf16[8,128,128]{2,1,0:T(8,128)(2,1)S(1)}, bf16[8,128,128]{2,1,0:T(8,128)(2,1)S(1)}, u32[]{:S(2)}, u32[]{:S(2)}) collective-permute-start(bf16[8,128,128]{2,1,0:T(8,128)(2,1)S(1)} %collective-permute-done.4.refs_4_), channel_id=1, source_target_pairs={{0,2},{1,9},{2,4},{3,11},{4,6},{5,13},{6,0},{7,15},{8,10},{9,17},{... | collective-permute-start | bytes 786440 | tf_op jit(solution)/shard_map/ppermute | solution.py:32
  31.6 28.4 %collective-permute-start.12 = (bf16[64,128,128]{2,1,0:T(8,128)(2,1)S(1)}, bf16[64,128,128]{2,1,0:T(8,128)(2,1)S(1)}, u32[]{:S(2)}, u32[]{:S(2)}) collective-permute-start(bf16[64,128,128]{2,1,0:T(8,128)(2,1)S(1)} %join.1.refs_0_), channel_id=1, source_target_pairs={{0,24},{1,7},{2,26},{3,1},{4,28},{5,3},{6,30},{7,5},{8,0},{9,15},{... | collective-permute-start | bytes 6291464 | tf_op jit(solution)/shard_map/ppermute | solution.py:32
  34.1 26.4 %collective-permute-start.11 = (bf16[64,128,128]{2,1,0:T(8,128)(2,1)S(1)}, bf16[64,128,128]{2,1,0:T(8,128)(2,1)S(1)}, u32[]{:S(2)}, u32[]{:S(2)}) collective-permute-start(bf16[64,128,128]{2,1,0:T(8,128)(2,1)S(1)} %join.1.refs_0_), channel_id=1, source_target_pairs={{0,8},{1,3},{2,10},{3,5},{4,12},{5,7},{6,14},{7,1},{8,16},{9,11},{... | collective-permute-start | bytes 6291464 | tf_op jit(solution)/shard_map/ppermute | solution.py:32
  34.2 26.4 %collective-permute-start.10 = (bf16[64,128,128]{2,1,0:T(8,128)(2,1)S(1)}, bf16[64,128,128]{2,1,0:T(8,128)(2,1)S(1)}, u32[]{:S(2)}, u32[]{:S(2)}) collective-permute-start(bf16[64,128,128]{2,1,0:T(8,128)(2,1)S(1)} %join.1.refs_0_), channel_id=1, source_target_pairs={{0,1},{1,0},{2,3},{3,2},{4,5},{5,4},{6,7},{7,6},{8,9},{9,8},{10,11... | collective-permute-start | bytes 6291464 | tf_op jit(solution)/shard_map/ppermute | solution.py:32
  38.5 20.8 %collective-permute-start.8 = (bf16[16,128,128]{2,1,0:T(8,128)(2,1)S(1)}, bf16[16,128,128]{2,1,0:T(8,128)(2,1)S(1)}, u32[]{:S(2)}, u32[]{:S(2)}) collective-permute-start(bf16[16,128,128]{2,1,0:T(8,128)(2,1)S(1)} %get-tuple-element.96), channel_id=1, source_target_pairs={{0,64},{1,193},{2,66},{3,195},{4,68},{5,197},{6,70},{7,199},{8,72}... | collective-permute-start | bytes 1572872 | tf_op jit(solution)/shard_map/ppermute | solution.py:32
  42.3 17.7 %collective-permute-start.9 = (bf16[16,128,128]{2,1,0:T(8,128)(2,1)S(1)}, bf16[16,128,128]{2,1,0:T(8,128)(2,1)S(1)}, u32[]{:S(2)}, u32[]{:S(2)}) collective-permute-start(bf16[16,128,128]{2,1,0:T(8,128)(2,1)S(1)} %get-tuple-element.97), channel_id=1, source_target_pairs={{0,224},{1,33},{2,226},{3,35},{4,228},{5,37},{6,230},{7,39},{8,232... | collective-permute-start | bytes 1572872 | tf_op jit(solution)/shard_map/ppermute | solution.py:32
  60.7 10.5 %collective-permute-start.13 = (bf16[64,128,128]{2,1,0:T(8,128)(2,1)S(1)}, bf16[64,128,128]{2,1,0:T(8,128)(2,1)S(1)}, u32[]{:S(2)}, u32[]{:S(2)}) collective-permute-start(bf16[64,128,128]{2,1,0:T(8,128)(2,1)S(1)} %collective-permute-done.11.up_ref.refs_1_), channel_id=1, source_target_pairs={{0,1},{1,0},{2,3},{3,2},{4,5},{5,4},{6,7},{7,6},{8,9},{9,8},{10,11... | collective-permute-start | bytes 6291464 | tf_op jit(solution)/shard_map/ppermute | solution.py:32
  66.0 6.8 %collective-permute-start.14 = (bf16[64,128,128]{2,1,0:T(8,128)(2,1)S(1)}, bf16[64,128,128]{2,1,0:T(8,128)(2,1)S(1)}, u32[]{:S(2)}, u32[]{:S(2)}) collective-permute-start(bf16[64,128,128]{2,1,0:T(8,128)(2,1)S(1)} %collective-permute-done.12.down_ref.refs_2_), channel_id=1, source_target_pairs={{0,1},{1,0},{2,3},{3,2},{4,5},{5,4},{6,7},{7,6},{8,9},{9,8},{10,11... | collective-permute-start | bytes 6291464 | tf_op jit(solution)/shard_map/ppermute | solution.py:32
  66.1 15.2 %collective-permute-start.16 = (bf16[32,128,128]{2,1,0:T(8,128)(2,1)S(1)}, bf16[32,128,128]{2,1,0:T(8,128)(2,1)S(1)}, u32[]{:S(2)}, u32[]{:S(2)}) collective-permute-start(bf16[32,128,128]{2,1,0:T(8,128)(2,1)S(1)} %get-tuple-element.118), channel_id=1, source_target_pairs={{0,8},{1,3},{2,10},{3,5},{4,12},{5,7},{6,14},{7,1},{8,16},{9,11},{... | collective-permute-start | bytes 3145736 | tf_op jit(solution)/shard_map/ppermute | solution.py:32
  66.2 15.2 %collective-permute-start.17 = (bf16[32,128,128]{2,1,0:T(8,128)(2,1)S(1)}, bf16[32,128,128]{2,1,0:T(8,128)(2,1)S(1)}, u32[]{:S(2)}, u32[]{:S(2)}) collective-permute-start(bf16[32,128,128]{2,1,0:T(8,128)(2,1)S(1)} %get-tuple-element.119), channel_id=1, source_target_pairs={{0,24},{1,7},{2,26},{3,1},{4,28},{5,3},{6,30},{7,5},{8,0},{9,15},{... | collective-permute-start | bytes 3145736 | tf_op jit(solution)/shard_map/ppermute | solution.py:32
  68.8 8.6 %collective-permute-start.15 = (bf16[16,128,128]{2,1,0:T(8,128)(2,1)S(1)}, bf16[16,128,128]{2,1,0:T(8,128)(2,1)S(1)}, u32[]{:S(2)}, u32[]{:S(2)}) collective-permute-start(bf16[16,128,128]{2,1,0:T(8,128)(2,1)S(1)} %get-tuple-element.117), channel_id=1, source_target_pairs={{0,32},{1,225},{2,34},{3,227},{4,36},{5,229},{6,38},{7,231},{8,40}... | collective-permute-start | bytes 1572872 | tf_op jit(solution)/shard_map/ppermute | solution.py:32
  81.3 3.6 %collective-permute-start.18 = (bf16[32,128,128]{2,1,0:T(8,128)(2,1)S(1)}, bf16[32,128,128]{2,1,0:T(8,128)(2,1)S(1)}, u32[]{:S(2)}, u32[]{:S(2)}) collective-permute-start(bf16[32,128,128]{2,1,0:T(8,128)(2,1)S(1)} %collective-permute-done.16.refs_0_.refs_6_), channel_id=1, source_target_pairs={{0,1},{1,0},{2,3},{3,2},{4,5},{5,4},{6,7},{7,6},{8,9},{9,8},{10,11... | collective-permute-start | bytes 3145736 | tf_op jit(solution)/shard_map/ppermute | solution.py:32
  82.6 3.8 %collective-permute-start.19 = (bf16[32,128,128]{2,1,0:T(8,128)(2,1)S(1)}, bf16[32,128,128]{2,1,0:T(8,128)(2,1)S(1)}, u32[]{:S(2)}, u32[]{:S(2)}) collective-permute-start(bf16[32,128,128]{2,1,0:T(8,128)(2,1)S(1)} %collective-permute-done.17.refs_1_.refs_7_), channel_id=1, source_target_pairs={{0,1},{1,0},{2,3},{3,2},{4,5},{5,4},{6,7},{7,6},{8,9},{9,8},{10,11... | collective-permute-start | bytes 3145736 | tf_op jit(solution)/shard_map/ppermute | solution.py:32
  90.0 17.4 %collective-permute-start.21 = (bf16[1,32,128,128]{3,2,1,0:T(8,128)(2,1)S(1)}, bf16[1,32,128,128]{3,2,1,0:T(8,128)(2,1)S(1)}, u32[]{:S(2)}, u32[]{:S(2)}) collective-permute-start(bf16[1,32,128,128]{3,2,1,0:T(8,128)(2,1)S(1)} %products.5), channel_id=1, source_target_pairs={{0,224},{1,33},{2,226},{3,35},{4,228},{5,37},{6,230},{7,39},{8,232... | collective-permute-start | bytes 3145736 | tf_op jit(solution)/shard_map/ppermute | solution.py:32
  97.2 21.1 %collective-permute-start.20 = (bf16[1,32,128,128]{3,2,1,0:T(8,128)(2,1)S(1)}, bf16[1,32,128,128]{3,2,1,0:T(8,128)(2,1)S(1)}, u32[]{:S(2)}, u32[]{:S(2)}) collective-permute-start(bf16[1,32,128,128]{3,2,1,0:T(8,128)(2,1)S(1)} %get-tuple-element.140), channel_id=1, source_target_pairs={{0,32},{1,225},{2,34},{3,227},{4,36},{5,229},{6,38},{7,231},{8,40}... | collective-permute-start | bytes 3145736 | tf_op jit(solution)/shard_map/ppermute | solution.py:32
  107.7 20.0 %collective-permute-start.22 = (bf16[1,32,128,128]{3,2,1,0:T(8,128)(2,1)S(1)}, bf16[1,32,128,128]{3,2,1,0:T(8,128)(2,1)S(1)}, u32[]{:S(2)}, u32[]{:S(2)}) collective-permute-start(bf16[1,32,128,128]{3,2,1,0:T(8,128)(2,1)S(1)} %plus.2), channel_id=1, source_target_pairs={{0,224},{1,33},{2,226},{3,35},{4,228},{5,37},{6,230},{7,39},{8,232... | collective-permute-start | bytes 3145736 | tf_op jit(solution)/shard_map/ppermute | solution.py:32
